TPU v7x, 768 devices: a whole 4x8x12 slice. The times are simulated.
768 devices in a mesh: row: 16 (over y, z_hi), col: 8 (over x, core), layer: 6 (over z_lo).
Axes of the slice: x: 4, y: 8, z: 12 (z_hi: 2, z_lo: 6; z = z_hi * 6 + z_lo), core: 2. Of those that a mesh axis runs over, the one named last changes fastest.
Arguments:
- left_tiles: bfloat16 [6, 16, 16, 6, 256, 256], P('layer', 'row', 'col'), may hold values from -6 to 6
- left_place: int32 [6, 16, 16, 6], P('layer', 'row', 'col'), may hold values from -1 to 23, as said below
- right_tiles: bfloat16 [6, 16, 16, 2, 256, 256], P('layer', 'row', 'col'), may hold values from -0.1875 to 0.1875
- right_place: int32 [6, 16, 16, 2], P('layer', 'row', 'col'), may hold values from -1 to 7, as said below
Outputs:
- product: bfloat16 [12288, 4096], P(('row', 'layer'), 'col')
Inputs may be any that keep to these rules, and one draw needn't show every extreme that they name: `left_place`: in each block the occupied slots come first, name distinct tile positions, and at least one slot is occupied; -1 marks an empty slot. `right_place`: in each block the occupied slots come first, name distinct tile positions, and at least one slot is occupied; -1 marks an empty slot.
All inputs are finite; a program needn't handle non-finite values.
Results may differ from a plain program's by a relative error of at most 0.015.
Values may be sent and summed in bfloat16 or wider, within the bound.
No kernel may reach another device: no remote copies, remote signals or barrier semaphores. Data moves between devices by JAX's collectives and lax.ppermute only.
A program may use at most 32 MiB of HBM per device.

v0:
```python
import jax
import jax.numpy as jnp
from jax import lax
from jax.sharding import PartitionSpec as P

TS = 256
KT = 8
RT = 3
CT = 1
STEPS = 4


def shifted(block, axis, distance):
    devices = range(lax.axis_size(axis))
    route = [((i - distance) % len(devices), i) for i in devices]
    return lax.ppermute(block, axis, route)


def block_product(left_block, left_slots, right_block, right_slots):
    inner_left = left_slots % KT
    row_left = jnp.where(left_slots >= 0, left_slots // KT, -1)
    inner_right = jnp.where(right_slots >= 0, right_slots // CT, -1)
    column_right = right_slots % CT
    columns = jnp.arange(CT, dtype=jnp.int32)
    select = (
        (inner_right[None, :, None] == inner_left[:, None, None])
        & (column_right[None, :, None] == columns[None, None, :])
    ).astype(jnp.bfloat16)
    right_strip = jnp.einsum(
        "abc,bxy->axcy", select, right_block, preferred_element_type=jnp.bfloat16
    )
    right_strip = right_strip.reshape(left_block.shape[0], TS, CT * TS)
    partial_rows = jnp.einsum(
        "axy,ayz->axz", left_block, right_strip, preferred_element_type=jnp.float32
    )
    rowhot = (row_left[:, None] == jnp.arange(RT, dtype=jnp.int32)[None, :]).astype(jnp.float32)
    return jnp.einsum("ar,axz->rxz", rowhot, partial_rows).reshape(RT * TS, CT * TS)


def local_terms(left_now, left_slots, right_now, right_slots):
    return jax.vmap(block_product, out_axes=1)(left_now, left_slots, right_now, right_slots)


def body(left_tiles, left_place, right_tiles, right_place):
    left_now = left_tiles[0, 0]
    left_slots = left_place[0, 0]
    right_first = right_tiles[0, 0]
    right_first_slots = right_place[0, 0]
    right_now = right_first
    right_slots = right_first_slots
    running = local_terms(left_now, left_slots, right_now, right_slots)
    for advance in range(1, STEPS):
        arriving, arriving_slots = shifted((left_now[0], left_slots[0]), "col", -1)
        left_now = jnp.concatenate([left_now[1:], arriving[None]], axis=0)
        left_slots = jnp.concatenate([left_slots[1:], arriving_slots[None]], axis=0)
        right_now, right_slots = shifted((right_now, right_slots), "row", -1)
        running = running + local_terms(left_now, left_slots, right_now, right_slots)
    row_count = running.shape[0]
    summand = running.reshape(row_count, -1)
    return lax.psum_scatter(summand.astype(jnp.bfloat16), "layer", scatter_dimension=0, tiled=True)


def solution(mesh):
    return jax.shard_map(
        body,
        mesh=mesh,
        in_specs=(
            P("layer", "row", "col", None, None, None),
            P("layer", "row", "col", None),
            P("layer", "row", "col", None, None, None),
            P("layer", "row", "col", None),
        ),
        out_specs=P(("row", "layer"), "col"),
        check_vma=False,
    )
```

profile of v0, /device:TPU:56, one launch (start us, length us, event | category | flops | bytes accessed | tf_op | source)
XLA Modules:
  0.0 242.2 jit_solution(14958956790320303725)
XLA Ops:
  6.5 0.0 reduce-scatter.4.cloned.1.call-start
  6.5 0.8 slice_bitcast_fusion.5
  7.3 2.2 collective-permute-start
  9.5 0.7 collective-permute-start.4
  10.2 2.4 copy.58
  12.6 0.0 copy-start.3
  12.6 0.0 copy-start.4
  12.6 0.0 copy-start.1
  12.6 16.0 %collective-permute-start.3 = (bf16[2,2,256,256]{3,1,2,0:T(2,128)(2,1)}, bf16[2,2,256,256]{3,1,2,0:T(2,128)(2,1)S(1)}, u32[]{:S(2)}, u32[]{:S(2)}) collective-permute-start(bf16[2,2,256,256]{3,1,2,0:T(2,128)(2,1)} %bitcast.98), channel_id=1, source_target_pairs={{48,0},{96,48},{144,96},{192,144},{240,192},{288,240},{336,288},{3... | collective-permute-start | bytes 1572872 | tf_op jit(solution)/shard_map/ppermute | solution.py:16
  28.6 1.9 collective-permute-start.2
  30.5 2.7 %slice_bitcast_fusion.2 = (bf16[1,6,256,256]{3,2,1,0:T(8,128)(2,1)}, bf16[6,256,256]{2,1,0:T(8,128)(2,1)S(1)}, bf16[6,256,256]{2,1,0:T(8,128)(2,1)}) fusion(bf16[1,1,2,6,256,256]{5,4,3,2,1,0:T(8,128)(2,1)} %param.4), kind=kLoop, calls=%fused_computation.27 | loop fusion | bytes 3932160 | tf_op jit(solution)/shard_map/slice | solution.py:54
  33.3 0.0 copy-start
  33.3 0.0 collective-permute-start.1
  33.3 0.0 copy-done.3
  33.3 0.0 copy-done.4
  33.3 0.0 copy-done.1
  33.4 1.2 fusion.40
  34.6 0.1 copy-done
  34.7 1.9 convolution_bitcast_fusion
  36.6 3.2 %copy.20 = bf16[2,6,256,256]{3,1,2,0:T(8,128)(2,1)S(1)} copy(bf16[2,6,256,256]{2,3,1,0:T(8,128)(2,1)} %convolution_bitcast_fusion) | data formatting | bytes 3145728 | tf_op jit(solution)/shard_map/vmap(axy,ayz->axz)/dot_general | solution.py:33
  39.8 0.7 fusion.26
  40.5 0.0 copy-start.2
  40.5 21.3 %collective-permute-done.2 = s32[2,2]{1,0:T(2,128)S(1)} collective-permute-done((s32[2,2]{1,0:T(2,128)}, s32[2,2]{1,0:T(2,128)S(1)}, u32[]{:S(2)}, u32[]{:S(2)}) %collective-permute-start.2) | collective-permute-done | bytes 48 | tf_op jit(solution)/shard_map/ppermute | solution.py:16
  61.8 11.7 %collective-permute-start.6 = (s32[2,2]{1,0:T(2,128)S(1)}, s32[2,2]{1,0:T(2,128)S(1)}, u32[]{:S(2)}, u32[]{:S(2)}) collective-permute-start(s32[2,2]{1,0:T(2,128)S(1)} %collective-permute-done.2), channel_id=1, source_target_pairs={{48,0},{96,48},{144,96},{192,144},{240,192},{288,240},{336,288},{3... | collective-permute-start | bytes 56 | tf_op jit(solution)/shard_map/ppermute | solution.py:16
  73.6 1.3 collective-permute-done.6
  74.9 0.0 collective-permute-start.5
  74.9 0.0 collective-permute-done
  74.9 11.4 %collective-permute-start.10 = (s32[2,2]{1,0:T(2,128)S(1)}, s32[2,2]{1,0:T(2,128)S(1)}, u32[]{:S(2)}, u32[]{:S(2)}) collective-permute-start(s32[2,2]{1,0:T(2,128)S(1)} %collective-permute-done.6), channel_id=1, source_target_pairs={{48,0},{96,48},{144,96},{192,144},{240,192},{288,240},{336,288},{3... | collective-permute-start | bytes 56 | tf_op jit(solution)/shard_map/ppermute | solution.py:16
  86.3 1.6 collective-permute-done.10
  87.8 1.7 collective-permute-start.8
  89.5 0.0 collective-permute-done.4
  89.5 1.3 collective-permute-done.8
  90.8 0.0 collective-permute-done.3
  90.8 9.4 %collective-permute-start.7 = (bf16[2,2,256,256]{3,1,2,0:T(2,128)(2,1)S(1)}, bf16[2,2,256,256]{3,1,2,0:T(2,128)(2,1)S(1)}, u32[]{:S(2)}, u32[]{:S(2)}) collective-permute-start(bf16[2,2,256,256]{3,1,2,0:T(2,128)(2,1)S(1)} %collective-permute-done.3), channel_id=1, source_target_pairs={{48,0},{96,48},{144,96},{192,144},{240,192},{288,240},{336,288},{3... | collective-permute-start | bytes 1572872 | tf_op jit(solution)/shard_map/ppermute | solution.py:16
  100.3 1.2 fusion.38
  101.5 0.0 collective-permute-done.1
  101.5 2.6 %collective-permute-start.9 = (bf16[6,256,256]{2,1,0:T(8,128)(2,1)}, bf16[6,256,256]{2,1,0:T(8,128)(2,1)S(1)}, u32[]{:S(2)}, u32[]{:S(2)}) collective-permute-start(bf16[6,256,256]{2,1,0:T(8,128)(2,1)} %collective-permute-done.1), channel_id=1, source_target_pairs={{6,0},{12,6},{18,12},{24,18},{30,24},{36,30},{42,36},{0,42},{7,1},... | collective-permute-start | bytes 2359304 | tf_op jit(solution)/shard_map/ppermute | solution.py:16
  104.1 0.0 copy-done.2
  104.1 1.8 fusion.8
  105.9 29.9 %collective-permute-done.7 = bf16[2,2,256,256]{3,1,2,0:T(2,128)(2,1)S(1)} collective-permute-done((bf16[2,2,256,256]{3,1,2,0:T(2,128)(2,1)S(1)}, bf16[2,2,256,256]{3,1,2,0:T(2,128)(2,1)S(1)}, u32[]{:S(2)}, u32[]{:S(2)}) %collective-permute-start.7) | collective-permute-done | bytes 524320 | tf_op jit(solution)/shard_map/ppermute | solution.py:16
  135.8 8.1 %collective-permute-start.11 = (bf16[2,2,256,256]{3,1,2,0:T(2,128)(2,1)S(1)}, bf16[2,2,256,256]{3,1,2,0:T(2,128)(2,1)S(1)}, u32[]{:S(2)}, u32[]{:S(2)}) collective-permute-start(bf16[2,2,256,256]{3,1,2,0:T(2,128)(2,1)S(1)} %collective-permute-done.7), channel_id=1, source_target_pairs={{48,0},{96,48},{144,96},{192,144},{240,192},{288,240},{336,288},{3... | collective-permute-start | bytes 1572872 | tf_op jit(solution)/shard_map/ppermute | solution.py:16
  143.9 1.2 fusion.36
  145.1 0.0 collective-permute-done.5
  145.1 1.7 fusion.12
  146.9 1.2 fusion.2
  148.0 23.2 %collective-permute-done.11 = bf16[2,2,256,256]{3,1,2,0:T(2,128)(2,1)S(1)} collective-permute-done((bf16[2,2,256,256]{3,1,2,0:T(2,128)(2,1)S(1)}, bf16[2,2,256,256]{3,1,2,0:T(2,128)(2,1)S(1)}, u32[]{:S(2)}, u32[]{:S(2)}) %collective-permute-start.11) | collective-permute-done | bytes 524320 | tf_op jit(solution)/shard_map/ppermute | solution.py:16
  171.3 1.2 fusion.34
  172.5 0.0 collective-permute-done.9
  172.5 0.6 fusion.16
  173.1 1.2 fusion
  174.2 1.6 add_convert_fusion
  175.9 0.1 copy.27
  176.0 0.3 copy.28
  176.3 1.2 copy.38
  177.5 0.0 reduce-scatter.4.cloned.1.call-update
  177.5 57.9 %reduce-scatter.4.cloned.1.call-done = bf16[128,512]{1,0:T(8,128)(2,1)} async-done(((bf16[768,512]{1,0:T(8,128)(2,1)}), bf16[128,512]{1,0:T(8,128)(2,1)}) %reduce-scatter.4.cloned.1.call-update) | async-done | bytes 131088 | tf_op jit(solution)/shard_map/reduce_scatter | solution.py:60
  (6 shorter events, 0.0 us)
Async XLA Ops:
  6.5 228.8 %reduce-scatter.4.cloned.1.call-start = ((), (), s32[]{:S(2)}) async-start(), calls=%async_computation.1 | async-start | bytes 917504 | tf_op jit(solution)/shard_map/reduce_scatter | solution.py:60
  7.3 67.6 %collective-permute-start = (s32[6]{0:T(128)S(1)}, s32[6]{0:T(128)S(1)}, u32[]{:S(2)}, u32[]{:S(2)}) collective-permute-start(s32[6]{0:T(128)S(1)} %get-tuple-element.12), channel_id=1, source_target_pairs={{6,0},{12,6},{18,12},{24,18},{30,24},{36,30},{42,36},{0,42},{7,1},... | collective-permute-start | bytes 80 | tf_op jit(solution)/shard_map/ppermute | solution.py:16
  9.5 80.0 %collective-permute-start.4 = (s32[6]{0:T(128)S(1)}, s32[6]{0:T(128)S(1)}, u32[]{:S(2)}, u32[]{:S(2)}) collective-permute-start(s32[6]{0:T(128)S(1)} %get-tuple-element.11), channel_id=1, source_target_pairs={{6,0},{12,6},{18,12},{24,18},{30,24},{36,30},{42,36},{0,42},{7,1},... | collective-permute-start | bytes 80 | tf_op jit(solution)/shard_map/ppermute | solution.py:16
  12.6 20.7 %copy-start.3 = (s32[1,1,2,6]{3,2,1,0:T(2,128)S(1)}, s32[1,1,2,6]{3,2,1,0:T(2,128)}, u32[]{:S(2)}) copy-start(s32[1,1,2,6]{3,2,1,0:T(2,128)} %param.5) | copy-start | bytes 148
  12.6 20.8 %copy-start.4 = (s32[1,1,2,2]{3,2,1,0:T(2,128)S(1)}, s32[1,1,2,2]{3,2,1,0:T(2,128)}, u32[]{:S(2)}) copy-start(s32[1,1,2,2]{3,2,1,0:T(2,128)} %param.7) | copy-start | bytes 52
  12.6 20.8 %copy-start.1 = (bf16[1,1,2,2,256,256]{5,4,3,2,1,0:T(8,128)(2,1)S(1)}, bf16[1,1,2,2,256,256]{5,4,3,2,1,0:T(8,128)(2,1)}, u32[]{:S(2)}) copy-start(bf16[1,1,2,2,256,256]{5,4,3,2,1,0:T(8,128)(2,1)} %param.6) | copy-start | bytes 1572868
  12.6 78.3 %collective-permute-start.3 = (bf16[2,2,256,256]{3,1,2,0:T(2,128)(2,1)}, bf16[2,2,256,256]{3,1,2,0:T(2,128)(2,1)S(1)}, u32[]{:S(2)}, u32[]{:S(2)}) collective-permute-start(bf16[2,2,256,256]{3,1,2,0:T(2,128)(2,1)} %bitcast.98), channel_id=1, source_target_pairs={{48,0},{96,48},{144,96},{192,144},{240,192},{288,240},{336,288},{3... | collective-permute-start | bytes 1572872 | tf_op jit(solution)/shard_map/ppermute | solution.py:16
  28.6 33.2 %collective-permute-start.2 = (s32[2,2]{1,0:T(2,128)}, s32[2,2]{1,0:T(2,128)S(1)}, u32[]{:S(2)}, u32[]{:S(2)}) collective-permute-start(s32[2,2]{1,0:T(2,128)} %bitcast.101), channel_id=1, source_target_pairs={{48,0},{96,48},{144,96},{192,144},{240,192},{288,240},{336,288},{3... | collective-permute-start | bytes 56 | tf_op jit(solution)/shard_map/ppermute | solution.py:16
  33.3 1.4 copy-start
  33.3 68.2 %collective-permute-start.1 = (bf16[6,256,256]{2,1,0:T(8,128)(2,1)}, bf16[6,256,256]{2,1,0:T(8,128)(2,1)}, u32[]{:S(2)}, u32[]{:S(2)}) collective-permute-start(bf16[6,256,256]{2,1,0:T(8,128)(2,1)} %get-tuple-element.7), channel_id=1, source_target_pairs={{6,0},{12,6},{18,12},{24,18},{30,24},{36,30},{42,36},{0,42},{7,1},... | collective-permute-start | bytes 2359304 | tf_op jit(solution)/shard_map/ppermute | solution.py:16
  40.5 63.6 %copy-start.2 = (bf16[1,6,256,256]{3,2,1,0:T(8,128)(2,1)S(1)}, bf16[1,6,256,256]{3,2,1,0:T(8,128)(2,1)}, u32[]{:S(2)}) copy-start(bf16[1,6,256,256]{3,2,1,0:T(8,128)(2,1)} %get-tuple-element.5) | copy-start | bytes 2359300
  61.8 13.0 %collective-permute-start.6 = (s32[2,2]{1,0:T(2,128)S(1)}, s32[2,2]{1,0:T(2,128)S(1)}, u32[]{:S(2)}, u32[]{:S(2)}) collective-permute-start(s32[2,2]{1,0:T(2,128)S(1)} %collective-permute-done.2), channel_id=1, source_target_pairs={{48,0},{96,48},{144,96},{192,144},{240,192},{288,240},{336,288},{3... | collective-permute-start | bytes 56 | tf_op jit(solution)/shard_map/ppermute | solution.py:16
  74.9 70.3 %collective-permute-start.5 = (bf16[6,256,256]{2,1,0:T(8,128)(2,1)S(1)}, bf16[6,256,256]{2,1,0:T(8,128)(2,1)S(1)}, u32[]{:S(2)}, u32[]{:S(2)}) collective-permute-start(bf16[6,256,256]{2,1,0:T(8,128)(2,1)S(1)} %get-tuple-element.6), channel_id=1, source_target_pairs={{6,0},{12,6},{18,12},{24,18},{30,24},{36,30},{42,36},{0,42},{7,1},... | collective-permute-start | bytes 2359304 | tf_op jit(solution)/shard_map/ppermute | solution.py:16
  74.9 13.0 %collective-permute-start.10 = (s32[2,2]{1,0:T(2,128)S(1)}, s32[2,2]{1,0:T(2,128)S(1)}, u32[]{:S(2)}, u32[]{:S(2)}) collective-permute-start(s32[2,2]{1,0:T(2,128)S(1)} %collective-permute-done.6), channel_id=1, source_target_pairs={{48,0},{96,48},{144,96},{192,144},{240,192},{288,240},{336,288},{3... | collective-permute-start | bytes 56 | tf_op jit(solution)/shard_map/ppermute | solution.py:16
  87.8 3.0 %collective-permute-start.8 = (s32[6]{0:T(128)S(1)}, s32[6]{0:T(128)S(1)}, u32[]{:S(2)}, u32[]{:S(2)}) collective-permute-start(s32[6]{0:T(128)S(1)} %collective-permute-done), channel_id=1, source_target_pairs={{6,0},{12,6},{18,12},{24,18},{30,24},{36,30},{42,36},{0,42},{7,1},... | collective-permute-start | bytes 80 | tf_op jit(solution)/shard_map/ppermute | solution.py:16
  90.8 45.0 %collective-permute-start.7 = (bf16[2,2,256,256]{3,1,2,0:T(2,128)(2,1)S(1)}, bf16[2,2,256,256]{3,1,2,0:T(2,128)(2,1)S(1)}, u32[]{:S(2)}, u32[]{:S(2)}) collective-permute-start(bf16[2,2,256,256]{3,1,2,0:T(2,128)(2,1)S(1)} %collective-permute-done.3), channel_id=1, source_target_pairs={{48,0},{96,48},{144,96},{192,144},{240,192},{288,240},{336,288},{3... | collective-permute-start | bytes 1572872 | tf_op jit(solution)/shard_map/ppermute | solution.py:16
  101.5 71.0 %collective-permute-start.9 = (bf16[6,256,256]{2,1,0:T(8,128)(2,1)}, bf16[6,256,256]{2,1,0:T(8,128)(2,1)S(1)}, u32[]{:S(2)}, u32[]{:S(2)}) collective-permute-start(bf16[6,256,256]{2,1,0:T(8,128)(2,1)} %collective-permute-done.1), channel_id=1, source_target_pairs={{6,0},{12,6},{18,12},{24,18},{30,24},{36,30},{42,36},{0,42},{7,1},... | collective-permute-start | bytes 2359304 | tf_op jit(solution)/shard_map/ppermute | solution.py:16
  135.8 35.4 %collective-permute-start.11 = (bf16[2,2,256,256]{3,1,2,0:T(2,128)(2,1)S(1)}, bf16[2,2,256,256]{3,1,2,0:T(2,128)(2,1)S(1)}, u32[]{:S(2)}, u32[]{:S(2)}) collective-permute-start(bf16[2,2,256,256]{3,1,2,0:T(2,128)(2,1)S(1)} %collective-permute-done.7), channel_id=1, source_target_pairs={{48,0},{96,48},{144,96},{192,144},{240,192},{288,240},{336,288},{3... | collective-permute-start | bytes 1572872 | tf_op jit(solution)/shard_map/ppermute | solution.py:16
Sparse Core Ops, SparseCore 0:
  177.6 57.6 reduce-scatter.3
where the time goes:
time: 243 us; the launch traced here: 242 us
  waiting for transfers between devices  137 us (56%)
  starting transfers between devices  65.8 us (27%)
  matrix products  15.4 us (6%)
  between operations  13.6 us (6%)
  local copies, waits for them, and re-layouts  10.8 us (4%)
    ppermute x12, waiting for transfers between devices, shifted(): return lax.ppermute(block, axis, route)  78.6 us
    ppermute x12, starting transfers between devices, shifted(): return lax.ppermute(block, axis, route)  65.8 us
    reduce_scatter x1, waiting for transfers between devices, body(): lax.psum_scatter(summand.astype(jnp.bfloat16), 'layer', scatter_dimension...  57.9 us
    dot_general x4, matrix products, block_product(): jnp.einsum('axy,ayz->axz', left_block, right_strip, preferred_element_typ...  5.99 us
  transfers between devices with their start and end apart: 13, of which 7 were waited for; matrix products, arithmetic and copies ran while one was open for 8% of the time, Pallas kernels for 0%

commit v1 on v0

v1 whole, which is shorter than its diff:
```python
import functools

import jax
import jax.numpy as jnp
from jax import lax
from jax.experimental import pallas as pl
from jax.experimental.pallas import tpu as pltpu
from jax.sharding import PartitionSpec as P

TS = 256
KT = 8
RT = 3
SA = 6
SB = 2
STEPS = 4
GRID = 16
N_LAYER = 6
HELD = 2


def shifted(block, axis, distance):
    size = lax.axis_size(axis)
    return lax.ppermute(block, axis, [((i - distance) % size, i) for i in range(size)])


def add_term(total, at_ref, left_table, right_table, left_ref, right_ref, column, step):
    left_at = lax.rem(at_ref[0] + (column + step), GRID)
    right_at = lax.rem(at_ref[1] + step, GRID) * HELD + column
    first = right_table[right_at * SB]
    second = right_table[right_at * SB + 1]

    def slot(q, carry):
        place = left_table[left_at * SA + q]
        inner = lax.rem(place, KT)
        used = place >= 0
        hits_first = used & (first == inner)
        hits_second = used & (second == inner)

        @pl.when(hits_first | hits_second)
        def _():
            rows = pl.ds(pl.multiple_of((place // KT) * TS, TS), TS)
            tile = jnp.where(hits_first, 0, 1)
            total[rows, :] += jnp.dot(left_ref[q], right_ref[tile], preferred_element_type=jnp.float32)

        return carry

    lax.fori_loop(0, SA, slot, 0)


def early_kernel(at_ref, left_table, right_table, *refs, terms):
    operands, total = refs[:-1], refs[-1]
    total[...] = jnp.zeros_like(total)
    for n, (column, step) in enumerate(terms):
        add_term(total.at[column], at_ref, left_table, right_table, operands[2 * n], operands[2 * n + 1], column, step)


def late_kernel(at_ref, left_table, right_table, start_ref, *refs, terms):
    operands, out_ref, total = refs[:-2], refs[-2], refs[-1]
    total[...] = start_ref[...]
    for n, (column, step) in enumerate(terms):
        add_term(total, at_ref, left_table, right_table, operands[2 * n], operands[2 * n + 1], column, step)
    out_ref[...] = total[...].astype(out_ref.dtype)


SMEM = pl.BlockSpec(memory_space=pltpu.SMEM)
VMEM = pl.BlockSpec(memory_space=pltpu.VMEM)
PARAMS = pltpu.CompilerParams(vmem_limit_bytes=32 * 1024 * 1024)


def early(tables, terms, operands):
    return pl.pallas_call(
        functools.partial(early_kernel, terms=terms),
        out_shape=jax.ShapeDtypeStruct((HELD, RT * TS, TS), jnp.float32),
        in_specs=[SMEM] * 3 + [VMEM] * len(operands),
        out_specs=VMEM,
        compiler_params=PARAMS,
        cost_estimate=pl.CostEstimate(flops=len(terms) * 3 * 2 * TS**3, bytes_accessed=6 << 20, transcendentals=0),
    )(*tables, *operands)


def late(tables, terms, start, operands):
    return pl.pallas_call(
        functools.partial(late_kernel, terms=terms),
        out_shape=jax.ShapeDtypeStruct((RT * TS, TS), jnp.bfloat16),
        in_specs=[SMEM] * 3 + [VMEM] * (1 + len(operands)),
        out_specs=VMEM,
        scratch_shapes=[pltpu.VMEM((RT * TS, TS), jnp.float32)],
        compiler_params=PARAMS,
        cost_estimate=pl.CostEstimate(flops=len(terms) * 3 * 2 * TS**3, bytes_accessed=4 << 20, transcendentals=0),
    )(*tables, start, *operands)


def body(left_tiles, left_place, right_tiles, right_place):
    left = left_tiles[0, 0]
    right = right_tiles[0, 0]
    with jax.named_scope("cross"):
        right_one = [shifted(right[j], "row", -1) for j in range(HELD)]
    with jax.named_scope("left"):
        left_next = shifted(left, "col", -1)
        left_last = shifted(left_next[0], "col", -1)
    with jax.named_scope("right_two"):
        right_two = shifted(right, "row", -2)
    with jax.named_scope("tables"):
        left_table = lax.all_gather(left_place[0, 0], "col", tiled=True).reshape(-1)
        right_table = lax.all_gather(right_place[0, 0], "row", tiled=True).reshape(-1)
    at = jnp.stack([lax.axis_index("col") * HELD, lax.axis_index("row")]).astype(jnp.int32)
    tables = (at, left_table, right_table)
    lefts = [left[0], left[1], left_next[0], left_next[1], left_last]
    first = [(j, s) for j in range(HELD) for s in (0, 2)]
    totals = early(
        tables, first, [x for j, s in first for x in (lefts[j + s], (right if s == 0 else right_two)[j])]
    )
    parts = []
    for j in range(HELD):
        right_three = shifted(right_one[j], "row", -2)
        partial = late(
            tables, [(j, 1), (j, 3)], totals[j], [lefts[j + 1], right_one[j], lefts[j + 3], right_three]
        )
        shares = lax.all_to_all(partial.reshape(N_LAYER, -1, TS), "layer", 0, 0, tiled=True)
        parts.append(jnp.sum(shares.astype(jnp.float32), axis=0).astype(jnp.bfloat16))
    return jnp.concatenate(parts, axis=1)


def solution(mesh):
    return jax.shard_map(
        body,
        mesh=mesh,
        in_specs=(
            P("layer", "row", "col", None, None, None),
            P("layer", "row", "col", None),
            P("layer", "row", "col", None, None, None),
            P("layer", "row", "col", None),
        ),
        out_specs=P(("row", "layer"), "col"),
        check_vma=False,
    )
```

time: 243 us -> 189 us (0.78)
  waiting for transfers between devices: 137 us -> 54.7 us
  blocking collectives: 0 us -> 76.5 us
  starting transfers between devices: 65.8 us -> 45.5 us
  matrix products: 15.4 us -> 0 us
  between operations: 13.6 us -> 0.15 us
  local copies, waits for them, and re-layouts: 10.8 us -> 3.49 us
  Pallas kernels: 0 us -> 4.98 us
    all_gather x0 -> x2, blocking collectives: none -> 76.5 us  [the longest x1 65.1 us: body(): lax.all_gather(right_place[0, 0], 'row', tiled=True).reshape(-1)]
    reduce_scatter x1 -> x0, waiting for transfers between devices: 57.9 us -> none  [body(): lax.psum_scatter(summand.astype(jnp.bfloat16), 'layer', scatter_dimension...]
    ppermute x12 -> x7, waiting for transfers between devices: 78.6 us -> 34 us  [shifted(): lax.ppermute(block, axis, [((i - distance) % size, i) for i in range(size)])]
    ppermute x12 -> x7, starting transfers between devices: 65.8 us -> 27.1 us  [shifted(): lax.ppermute(block, axis, [((i - distance) % size, i) for i in range(size)])]
    all_to_all x0 -> x2, waiting for transfers between devices: none -> 20.7 us  [body(): lax.all_to_all(partial.reshape(N_LAYER, -1, TS), 'layer', 0, 0, tiled=True)]
    all_to_all x0 -> x2, starting transfers between devices: none -> 18.4 us  [body(): lax.all_to_all(partial.reshape(N_LAYER, -1, TS), 'layer', 0, 0, tiled=True)]
    dot_general x12 -> x0, matrix products: 15.4 us -> none  [the longest x4 5.99 us: block_product(): jnp.einsum('axy,ayz->axz', left_block, right_strip, preferred_element_typ...]
    pallas_call x0 -> x3, Pallas kernels: none -> 4.98 us  [the longest x2 3.46 us: late(): pl.pallas_call(functools.partial(late_kernel, terms=terms), out_shape=jax...]
  transfers between devices with their start and end apart: 13 -> 9, of which waited for: 7 -> 5; matrix products, arithmetic and copies ran while one was open for 8% -> 3% of each run, Pallas kernels for 0% -> 2%
where the time goes in v1:
time: 189 us; the launch traced here: 187 us
  blocking collectives  76.5 us (40%)
  waiting for transfers between devices  54.7 us (29%)
  starting transfers between devices  45.5 us (24%)
  Pallas kernels  4.98 us (3%)
  local copies, waits for them, and re-layouts  3.49 us (2%)
  other arithmetic  2.16 us (1%)
    all_gather x1, blocking collectives, body(): lax.all_gather(right_place[0, 0], 'row', tiled=True).reshape(-1)  65.1 us
    ppermute x7, waiting for transfers between devices, shifted(): lax.ppermute(block, axis, [((i - distance) % size, i) for i in range(size)])  34 us
    ppermute x7, starting transfers between devices, shifted(): lax.ppermute(block, axis, [((i - distance) % size, i) for i in range(size)])  27.1 us
    all_to_all x2, waiting for transfers between devices, body(): lax.all_to_all(partial.reshape(N_LAYER, -1, TS), 'layer', 0, 0, tiled=True)  20.7 us
    all_to_all x2, starting transfers between devices, body(): lax.all_to_all(partial.reshape(N_LAYER, -1, TS), 'layer', 0, 0, tiled=True)  18.4 us
    all_gather x1, blocking collectives, body(): left_table = lax.all_gather(left_place[0, 0], 'col', tiled=True).reshape(-1)  11.4 us
  transfers between devices with their start and end apart: 9, of which 5 were waited for; matrix products, arithmetic and copies ran while one was open for 3% of the time, Pallas kernels for 2%

profile of v1, /device:TPU:56, one launch (start us, length us, event | category | flops | bytes accessed | tf_op | source)
XLA Modules:
  0.0 187.5 jit_solution(17015011136453713039)
XLA Ops:
  0.0 2.2 %collective-permute-start = (bf16[2,6,256,256]{3,2,1,0:T(8,128)(2,1)}, bf16[2,6,256,256]{3,2,1,0:T(8,128)(2,1)S(1)}, u32[]{:S(2)}, u32[]{:S(2)}) collective-permute-start(bf16[2,6,256,256]{3,2,1,0:T(8,128)(2,1)} %bitcast.30), channel_id=1, source_target_pairs={{6,0},{12,6},{18,12},{24,18},{30,24},{36,30},{42,36},{0,42},{7,1},... | collective-permute-start | bytes 4718600 | tf_op jit(solution)/shard_map/left/ppermute | solution.py:23
  2.2 3.2 %collective-permute-start.1 = (bf16[2,2,256,256]{3,2,1,0:T(8,128)(2,1)}, bf16[2,2,256,256]{3,2,1,0:T(8,128)(2,1)S(1)}, u32[]{:S(2)}, u32[]{:S(2)}) collective-permute-start(bf16[2,2,256,256]{3,2,1,0:T(8,128)(2,1)} %bitcast.31), channel_id=1, source_target_pairs={{96,0},{144,48},{192,96},{240,144},{288,192},{336,240},{384,288},{... | collective-permute-start | bytes 1572872 | tf_op jit(solution)/shard_map/right_two/ppermute | solution.py:23
  5.5 1.1 slice_bitcast_fusion.8
  6.5 15.9 %collective-permute-start.2 = (bf16[2,256,256]{2,1,0:T(8,128)(2,1)S(1)}, bf16[2,256,256]{2,1,0:T(8,128)(2,1)S(1)}, u32[]{:S(2)}, u32[]{:S(2)}) collective-permute-start(bf16[2,256,256]{2,1,0:T(8,128)(2,1)S(1)} %get-tuple-element.14.refs_1_), channel_id=1, source_target_pairs={{48,0},{96,48},{144,96},{192,144},{240,192},{288,240},{336,288},{3... | collective-permute-start | bytes 786440 | tf_op jit(solution)/shard_map/cross/ppermute | solution.py:23
  22.5 65.1 %all-gather.1 = s32[1,1,32,2]{3,1,0,2:T(1,128)S(1)} all-gather(s32[1,1,2,2]{3,1,0,2:T(1,128)} %bitcast.32), channel_id=3, replica_groups=mesh['row'=16,'col'=8,'layer'=6] {'row'}, dimensions={2}, use_global_device_ids=true | all-gather | bytes 272 | tf_op jit(solution)/shard_map/tables/all_gather | solution.py:105
  87.6 0.5 broadcast.6
  88.1 0.7 reduce.9
  88.8 0.1 reshape.21.right_table
  88.9 11.4 %all-gather = s32[1,1,16,6]{3,1,0,2:T(1,128)S(1)} all-gather(s32[1,1,2,6]{3,1,0,2:T(1,128)} %bitcast.33), channel_id=2, replica_groups=mesh['row'=16,'col'=8,'layer'=6] {'col'}, dimensions={2}, use_global_device_ids=true | all-gather | bytes 432 | tf_op jit(solution)/shard_map/tables/all_gather | solution.py:104
  100.3 0.6 reduce.8
  100.9 0.1 reshape.20.left_table
  101.0 0.1 pad_add_fusion.at_ref
  101.1 1.5 slice_bitcast_fusion.4
  102.6 0.0 collective-permute-done.2.refs_1_
  102.6 1.9 %collective-permute-start.3 = (bf16[2,256,256]{2,1,0:T(8,128)(2,1)S(1)}, bf16[2,256,256]{2,1,0:T(8,128)(2,1)S(1)}, u32[]{:S(2)}, u32[]{:S(2)}) collective-permute-start(bf16[2,256,256]{2,1,0:T(8,128)(2,1)S(1)} %collective-permute-done.2.refs_1_), channel_id=1, source_target_pairs={{96,0},{144,48},{192,96},{240,144},{288,192},{336,240},{384,288},{... | collective-permute-start | bytes 786440 | tf_op jit(solution)/shard_map/ppermute | solution.py:23
  104.5 0.0 collective-permute-done.1
  104.5 0.0 collective-permute-done
  104.6 0.1 slice_bitcast_fusion.2
  104.7 1.5 shard_map.46
  106.2 0.1 slice_bitcast_fusion.1
  106.3 8.8 %collective-permute-done.3.refs_3_ = bf16[2,256,256]{2,1,0:T(8,128)(2,1)S(1)} collective-permute-done((bf16[2,256,256]{2,1,0:T(8,128)(2,1)S(1)}, bf16[2,256,256]{2,1,0:T(8,128)(2,1)S(1)}, u32[]{:S(2)}, u32[]{:S(2)}) %collective-permute-start.3) | collective-permute-done | bytes 262176 | tf_op jit(solution)/shard_map/ppermute | solution.py:23
  115.1 1.6 shard_map.47
  116.8 5.9 %all-to-all-start = ((bf16[6,128,256]{2,1,0:T(8,128)(2,1)}), bf16[6,128,256]{2,1,0:T(8,128)(2,1)S(1)}, u32[]{:S(2)}, u32[]{:S(2)}) async-start(bf16[6,128,256]{2,1,0:T(8,128)(2,1)} %bitcast.15), calls=%async_computation | async-start | bytes 786432 | tf_op jit(solution)/shard_map/all_to_all | solution.py:119
  122.6 0.0 collective-permute-start.5
  122.6 1.9 %collective-permute-start.4 = (bf16[2,256,256]{2,1,0:T(8,128)(2,1)S(1)}, bf16[2,256,256]{2,1,0:T(8,128)(2,1)S(1)}, u32[]{:S(2)}, u32[]{:S(2)}) collective-permute-start(bf16[2,256,256]{2,1,0:T(8,128)(2,1)S(1)} %get-tuple-element.13.refs_5_), channel_id=1, source_target_pairs={{48,0},{96,48},{144,96},{192,144},{240,192},{288,240},{336,288},{3... | collective-permute-start | bytes 786440 | tf_op jit(solution)/shard_map/cross/ppermute | solution.py:23
  124.6 16.1 %collective-permute-done.4.refs_1_ = bf16[2,256,256]{2,1,0:T(8,128)(2,1)S(1)} collective-permute-done((bf16[2,256,256]{2,1,0:T(8,128)(2,1)S(1)}, bf16[2,256,256]{2,1,0:T(8,128)(2,1)S(1)}, u32[]{:S(2)}, u32[]{:S(2)}) %collective-permute-start.4) | collective-permute-done | bytes 262176 | tf_op jit(solution)/shard_map/cross/ppermute | solution.py:23
  140.7 1.9 %collective-permute-start.6 = (bf16[2,256,256]{2,1,0:T(8,128)(2,1)S(1)}, bf16[2,256,256]{2,1,0:T(8,128)(2,1)S(1)}, u32[]{:S(2)}, u32[]{:S(2)}) collective-permute-start(bf16[2,256,256]{2,1,0:T(8,128)(2,1)S(1)} %collective-permute-done.4.refs_1_), channel_id=1, source_target_pairs={{96,0},{144,48},{192,96},{240,144},{288,192},{336,240},{384,288},{... | collective-permute-start | bytes 786440 | tf_op jit(solution)/shard_map/ppermute | solution.py:23
  142.6 9.1 %collective-permute-done.6.refs_3_ = bf16[2,256,256]{2,1,0:T(8,128)(2,1)S(1)} collective-permute-done((bf16[2,256,256]{2,1,0:T(8,128)(2,1)S(1)}, bf16[2,256,256]{2,1,0:T(8,128)(2,1)S(1)}, u32[]{:S(2)}, u32[]{:S(2)}) %collective-permute-start.6) | collective-permute-done | bytes 262176 | tf_op jit(solution)/shard_map/ppermute | solution.py:23
  151.7 0.0 collective-permute-done.5.refs_2_
  151.7 1.8 shard_map.48
  153.5 4.0 %all-to-all-done = bf16[6,128,256]{2,1,0:T(8,128)(2,1)S(1)} async-done(((bf16[6,128,256]{2,1,0:T(8,128)(2,1)}), bf16[6,128,256]{2,1,0:T(8,128)(2,1)S(1)}, u32[]{:S(2)}, u32[]{:S(2)}) %all-to-all-start) | async-done | bytes 393248 | tf_op jit(solution)/shard_map/all_to_all | solution.py:119
  157.5 12.5 %all-to-all-start.1 = ((bf16[6,128,256]{2,1,0:T(8,128)(2,1)}), bf16[6,128,256]{2,1,0:T(8,128)(2,1)S(1)}, u32[]{:S(2)}, u32[]{:S(2)}) async-start(bf16[6,128,256]{2,1,0:T(8,128)(2,1)} %bitcast.17), calls=%async_computation.1 | async-start | bytes 786432 | tf_op jit(solution)/shard_map/all_to_all | solution.py:119
  170.0 0.1 reduce_sum.24
  170.1 16.7 %all-to-all-done.1 = bf16[6,128,256]{2,1,0:T(8,128)(2,1)S(1)} async-done(((bf16[6,128,256]{2,1,0:T(8,128)(2,1)}), bf16[6,128,256]{2,1,0:T(8,128)(2,1)S(1)}, u32[]{:S(2)}, u32[]{:S(2)}) %all-to-all-start.1) | async-done | bytes 393248 | tf_op jit(solution)/shard_map/all_to_all | solution.py:119
  186.8 0.1 reduce_sum.25
  186.8 0.7 pad_maximum_fusion
  (1 shorter events, 0.0 us)
Async XLA Ops:
  0.0 104.5 %collective-permute-start = (bf16[2,6,256,256]{3,2,1,0:T(8,128)(2,1)}, bf16[2,6,256,256]{3,2,1,0:T(8,128)(2,1)S(1)}, u32[]{:S(2)}, u32[]{:S(2)}) collective-permute-start(bf16[2,6,256,256]{3,2,1,0:T(8,128)(2,1)} %bitcast.30), channel_id=1, source_target_pairs={{6,0},{12,6},{18,12},{24,18},{30,24},{36,30},{42,36},{0,42},{7,1},... | collective-permute-start | bytes 4718600 | tf_op jit(solution)/shard_map/left/ppermute | solution.py:23
  2.2 102.3 %collective-permute-start.1 = (bf16[2,2,256,256]{3,2,1,0:T(8,128)(2,1)}, bf16[2,2,256,256]{3,2,1,0:T(8,128)(2,1)S(1)}, u32[]{:S(2)}, u32[]{:S(2)}) collective-permute-start(bf16[2,2,256,256]{3,2,1,0:T(8,128)(2,1)} %bitcast.31), channel_id=1, source_target_pairs={{96,0},{144,48},{192,96},{240,144},{288,192},{336,240},{384,288},{... | collective-permute-start | bytes 1572872 | tf_op jit(solution)/shard_map/right_two/ppermute | solution.py:23
  6.5 96.0 %collective-permute-start.2 = (bf16[2,256,256]{2,1,0:T(8,128)(2,1)S(1)}, bf16[2,256,256]{2,1,0:T(8,128)(2,1)S(1)}, u32[]{:S(2)}, u32[]{:S(2)}) collective-permute-start(bf16[2,256,256]{2,1,0:T(8,128)(2,1)S(1)} %get-tuple-element.14.refs_1_), channel_id=1, source_target_pairs={{48,0},{96,48},{144,96},{192,144},{240,192},{288,240},{336,288},{3... | collective-permute-start | bytes 786440 | tf_op jit(solution)/shard_map/cross/ppermute | solution.py:23
  102.6 12.6 %collective-permute-start.3 = (bf16[2,256,256]{2,1,0:T(8,128)(2,1)S(1)}, bf16[2,256,256]{2,1,0:T(8,128)(2,1)S(1)}, u32[]{:S(2)}, u32[]{:S(2)}) collective-permute-start(bf16[2,256,256]{2,1,0:T(8,128)(2,1)S(1)} %collective-permute-done.2.refs_1_), channel_id=1, source_target_pairs={{96,0},{144,48},{192,96},{240,144},{288,192},{336,240},{384,288},{... | collective-permute-start | bytes 786440 | tf_op jit(solution)/shard_map/ppermute | solution.py:23
  116.8 40.7 %all-to-all-start = ((bf16[6,128,256]{2,1,0:T(8,128)(2,1)}), bf16[6,128,256]{2,1,0:T(8,128)(2,1)S(1)}, u32[]{:S(2)}, u32[]{:S(2)}) async-start(bf16[6,128,256]{2,1,0:T(8,128)(2,1)} %bitcast.15), calls=%async_computation | async-start | bytes 786432 | tf_op jit(solution)/shard_map/all_to_all | solution.py:119
  122.6 29.1 %collective-permute-start.5 = (bf16[6,256,256]{2,1,0:T(8,128)(2,1)S(1)}, bf16[6,256,256]{2,1,0:T(8,128)(2,1)S(1)}, u32[]{:S(2)}, u32[]{:S(2)}) collective-permute-start(bf16[6,256,256]{2,1,0:T(8,128)(2,1)S(1)} %get-tuple-element.8.refs_2_.refs_0_), channel_id=1, source_target_pairs={{6,0},{12,6},{18,12},{24,18},{30,24},{36,30},{42,36},{0,42},{7,1},... | collective-permute-start | bytes 2359304 | tf_op jit(solution)/shard_map/left/ppermute | solution.py:23
  122.6 18.1 %collective-permute-start.4 = (bf16[2,256,256]{2,1,0:T(8,128)(2,1)S(1)}, bf16[2,256,256]{2,1,0:T(8,128)(2,1)S(1)}, u32[]{:S(2)}, u32[]{:S(2)}) collective-permute-start(bf16[2,256,256]{2,1,0:T(8,128)(2,1)S(1)} %get-tuple-element.13.refs_5_), channel_id=1, source_target_pairs={{48,0},{96,48},{144,96},{192,144},{240,192},{288,240},{336,288},{3... | collective-permute-start | bytes 786440 | tf_op jit(solution)/shard_map/cross/ppermute | solution.py:23
  140.7 11.0 %collective-permute-start.6 = (bf16[2,256,256]{2,1,0:T(8,128)(2,1)S(1)}, bf16[2,256,256]{2,1,0:T(8,128)(2,1)S(1)}, u32[]{:S(2)}, u32[]{:S(2)}) collective-permute-start(bf16[2,256,256]{2,1,0:T(8,128)(2,1)S(1)} %collective-permute-done.4.refs_1_), channel_id=1, source_target_pairs={{96,0},{144,48},{192,96},{240,144},{288,192},{336,240},{384,288},{... | collective-permute-start | bytes 786440 | tf_op jit(solution)/shard_map/ppermute | solution.py:23
  157.5 29.3 %all-to-all-start.1 = ((bf16[6,128,256]{2,1,0:T(8,128)(2,1)}), bf16[6,128,256]{2,1,0:T(8,128)(2,1)S(1)}, u32[]{:S(2)}, u32[]{:S(2)}) async-start(bf16[6,128,256]{2,1,0:T(8,128)(2,1)} %bitcast.17), calls=%async_computation.1 | async-start | bytes 786432 | tf_op jit(solution)/shard_map/all_to_all | solution.py:119

commit v2 on v1

v2 whole, which is shorter than its diff:
```python
import functools

import jax
import jax.numpy as jnp
from jax import lax
from jax.experimental import pallas as pl
from jax.experimental.pallas import tpu as pltpu
from jax.sharding import PartitionSpec as P

TS = 256
KT = 8
RT = 3
SA = 6
SB = 2
TRIO = 3
SHARE = 128
HELD = 2
NOTE = 16
PIECE = SB * TS + NOTE
BLOCK = SA * TS + NOTE


def shifted(block, axis, distance):
    size = lax.axis_size(axis)
    return lax.ppermute(block, axis, [((i - distance) % size, i) for i in range(size)])


def add_term(total, place_ref, left_ref, right_ref):
    first, second = noted(right_ref, SB)
    for q, place in enumerate(noted(left_ref, SA)):
        place_ref[q] = place

    def slot(q, carry):
        place = place_ref[q]
        inner = lax.rem(place, KT)
        used = place >= 0
        hits_first = used & (first == inner)
        hits_second = used & (second == inner)

        @pl.when(hits_first | hits_second)
        def _():
            left_rows = pl.ds(pl.multiple_of(q * TS, TS), TS)
            right_rows = pl.ds(pl.multiple_of(jnp.where(hits_first, 0, TS), TS), TS)
            rows = pl.ds(pl.multiple_of((place // KT) * TS, TS), TS)
            total[rows, :] += jnp.dot(
                left_ref[left_rows, :], right_ref[right_rows, :], preferred_element_type=jnp.float32
            )

        return carry

    lax.fori_loop(0, SA, slot, 0)


def noted(packed_ref, slots):
    note = packed_ref[slots * TS : slots * TS + NOTE, :128].astype(jnp.float32).astype(jnp.int32)
    return [note[0, p] for p in range(slots)]


def write_note(packed_ref, place_ref, column, slots):
    shape = (NOTE, packed_ref.shape[1])
    lane = lax.broadcasted_iota(jnp.int32, shape, 1)
    note = jnp.full(shape, -1, jnp.int32)
    for p in range(slots):
        note = jnp.where(lane == p, place_ref[column, p], note)
    packed_ref[slots * TS :, :] = note.astype(jnp.float32).astype(jnp.bfloat16)


def pack_right_kernel(place_ref, right_ref, *pieces):
    for column, piece in enumerate(pieces):
        for p in range(SB):
            piece[p * TS : (p + 1) * TS, :] = right_ref[column, p]
        write_note(piece, place_ref, column, SB)


def pack_left_kernel(place_ref, left_ref, right_zero, right_one, lefts, left_zero, rights):
    for column in range(HELD):
        targets = [lefts.at[column * BLOCK : (column + 1) * BLOCK]] + [left_zero] * (column == 0)
        for target in targets:
            for q in range(SA):
                target[q * TS : (q + 1) * TS, :] = left_ref[column, q]
            write_note(target, place_ref, column, SA)
    rights[:PIECE, :] = right_zero[...]
    rights[PIECE:, :] = right_one[...]


def early_kernel(own, after, rights, twos, *refs):
    totals, place_ref = refs[:-1], refs[-1]
    for column, total in enumerate(totals):
        left = pl.ds(column * BLOCK, BLOCK)
        right = pl.ds(column * PIECE, PIECE)
        total[...] = jnp.zeros_like(total)
        add_term(total, place_ref, own.at[left], rights.at[right])
        add_term(total, place_ref, after.at[left], twos.at[right])


def late_kernel(layer, start_ref, left_one, left_three, right_one, right_three, *refs, blocks):
    share_refs, total, place_ref = refs[:-2], refs[-2], refs[-1]
    total[...] = start_ref[...]
    for left, block, right in ((left_one, blocks[0], right_one), (left_three, blocks[1], right_three)):
        add_term(total, place_ref, left.at[pl.ds(block * BLOCK, BLOCK)], right)
    half = layer[0] // TRIO
    for turn, share in enumerate(share_refs):
        spot = lax.rem(layer[0] + turn, TRIO)
        for n, side in enumerate((half, 1 - half)):
            rows = pl.ds(pl.multiple_of((side * TRIO + spot) * SHARE, SHARE), SHARE)
            share[n * SHARE : (n + 1) * SHARE, :] = total[rows, :].astype(share.dtype)


def gather_kernel(own, one, two, near, far):
    added = own[...].astype(jnp.float32) + one[...].astype(jnp.float32) + two[...].astype(jnp.float32)
    near[...] = added[:SHARE]
    far[...] = added[SHARE:].astype(far.dtype)


def final_kernel(*refs):
    out_ref = refs[-1]
    for n in range(HELD):
        added = refs[2 * n][...] + refs[2 * n + 1][...].astype(jnp.float32)
        out_ref[:, n * TS : (n + 1) * TS] = added.astype(out_ref.dtype)


AHEAD = 10**12
SMEM = pl.BlockSpec(memory_space=pltpu.SMEM)
VMEM = pl.BlockSpec(memory_space=pltpu.VMEM)
PARAMS = pltpu.CompilerParams(vmem_limit_bytes=32 * 1024 * 1024)


def call(kernel, out_shape, in_specs, operands, scratch=(), cost=0):
    return pl.pallas_call(
        kernel,
        out_shape=out_shape,
        in_specs=in_specs,
        out_specs=jax.tree.map(lambda _: VMEM, out_shape),
        scratch_shapes=scratch,
        compiler_params=PARAMS,
        cost_estimate=pl.CostEstimate(flops=cost, bytes_accessed=0, transcendentals=0),
    )(*operands)


def array(rows, columns, dtype=jnp.bfloat16):
    return jax.ShapeDtypeStruct((rows, columns), dtype)


def body(left_tiles, left_place, right_tiles, right_place):
    layer = lax.axis_index("layer").astype(jnp.int32).reshape(1)
    places = pltpu.SMEM((SA,), jnp.int32)
    pieces = call(
        pack_right_kernel,
        [array(PIECE, TS)] * HELD,
        [SMEM, VMEM],
        (right_place[0, 0], right_tiles[0, 0]),
    )
    right_one = [shifted(piece, "row", -1) for piece in pieces]
    lefts, left_zero, rights = call(
        pack_left_kernel,
        [array(HELD * BLOCK, TS), array(BLOCK, TS), array(HELD * PIECE, TS)],
        [SMEM] + [VMEM] * 3,
        (left_place[0, 0], left_tiles[0, 0], *pieces),
    )
    right_two = shifted(rights, "row", -2)
    left_next = shifted(lefts, "col", -1)
    left_last = shifted(left_zero, "col", -2)
    totals = call(
        early_kernel,
        [array(RT * TS, TS, jnp.float32)] * HELD,
        [VMEM] * 4,
        (lefts, left_next, rights, right_two),
        [places],
    )
    right_one[1], totals = lax.optimization_barrier((right_one[1], totals))
    right_three = [shifted(piece, "row", -2) for piece in right_one]
    held = [(lefts, 0), (lefts, 1), (left_next, 0), (left_next, 1), (left_last, 0)]
    trio = [[(p, p // TRIO * TRIO + (p + turn) % TRIO) for p in range(2 * TRIO)] for turn in range(TRIO)]
    across = [(p, (p + TRIO) % (2 * TRIO)) for p in range(2 * TRIO)]
    shares = []
    for j in range(HELD):
        if j:
            right_three[j], shares[j - 1] = lax.optimization_barrier((right_three[j], shares[j - 1]))
        (one, block_one), (three, block_three) = held[j + 1], held[j + 3]
        shares.append(
            call(
                functools.partial(late_kernel, blocks=(block_one, block_three)),
                [array(2 * SHARE, TS)] * TRIO,
                [SMEM] + [VMEM] * 5,
                (layer, totals[j], one, three, right_one[j], right_three[j]),
                [pltpu.VMEM((RT * TS, TS), jnp.float32), places],
            )
        )
    ends = []
    for j, (own_share, *others) in enumerate(shares):
        arrived = [lax.ppermute(share, "layer", trio[turn]) for turn, share in enumerate(others, 1)]
        if j:
            arrived, ends = lax.optimization_barrier((arrived, ends))
        near, far = call(
            gather_kernel,
            [array(SHARE, TS, jnp.float32), array(SHARE, TS)],
            [VMEM] * TRIO,
            (own_share, *arrived),
            cost=(1 - j) * AHEAD,
        )
        ends.append(near)
        shares[j] = far
    for j, far in enumerate(shares):
        ends.insert(2 * j + 1, lax.ppermute(far, "layer", across))
    return call(final_kernel, array(SHARE, HELD * TS), [VMEM] * len(ends), ends)


def solution(mesh):
    return jax.shard_map(
        body,
        mesh=mesh,
        in_specs=(
            P("layer", "row", "col", None, None, None),
            P("layer", "row", "col", None),
            P("layer", "row", "col", None, None, None),
            P("layer", "row", "col", None),
        ),
        out_specs=P(("row", "layer"), "col"),
        check_vma=False,
    )
```

time: 189 us -> 115 us (0.61)
  blocking collectives: 76.5 us -> 0 us
  waiting for transfers between devices: 54.7 us -> 40.1 us
  starting transfers between devices: 45.5 us -> 56.8 us
  Pallas kernels: 4.98 us -> 10.3 us
  local copies, waits for them, and re-layouts: 3.49 us -> 6.7 us
  other arithmetic: 2.16 us -> 0 us
    all_gather x2 -> x0, blocking collectives: 76.5 us -> none  [the longest x1 65.1 us: body(): lax.all_gather(right_place[0, 0], 'row', tiled=True).reshape(-1)]
    ppermute x0 -> x6, starting transfers between devices: none -> 24.3 us  [the longest x4 13.9 us: body(): lax.ppermute(share, 'layer', trio[turn])]
    all_to_all x2 -> x0, waiting for transfers between devices: 20.7 us -> none  [body(): lax.all_to_all(partial.reshape(N_LAYER, -1, TS), 'layer', 0, 0, tiled=True)]
    all_to_all x2 -> x0, starting transfers between devices: 18.4 us -> none  [body(): lax.all_to_all(partial.reshape(N_LAYER, -1, TS), 'layer', 0, 0, tiled=True)]
    ppermute x0 -> x6, waiting for transfers between devices: none -> 11.5 us  [the longest x2 7.43 us: body(): ends.insert(2 * j + 1, lax.ppermute(far, 'layer', across))]
    unnamed x0 -> x16, local copies, waits for them, and re-layouts: none -> 6.7 us
    ppermute x7, waiting for transfers between devices: 34 us -> 28.6 us  [shifted(): lax.ppermute(block, axis, [((i - distance) % size, i) for i in range(size)])]
    ppermute x7, starting transfers between devices: 27.1 us -> 32.5 us  [shifted(): lax.ppermute(block, axis, [((i - distance) % size, i) for i in range(size)])]
  transfers between devices with their start and end apart: 9 -> 13, of which waited for: 5 -> 7; matrix products, arithmetic and copies ran while one was open for 3% -> 0% of each run, Pallas kernels for 2% -> 6%
where the time goes in v2:
time: 115 us; the launch traced here: 114 us
  starting transfers between devices  56.8 us (49%)
  waiting for transfers between devices  40.1 us (35%)
  Pallas kernels  10.3 us (9%)
  local copies, waits for them, and re-layouts  6.7 us (6%)
    ppermute x7, starting transfers between devices, shifted(): lax.ppermute(block, axis, [((i - distance) % size, i) for i in range(size)])  32.5 us
    ppermute x7, waiting for transfers between devices, shifted(): lax.ppermute(block, axis, [((i - distance) % size, i) for i in range(size)])  28.6 us
    ppermute x4, starting transfers between devices, body(): lax.ppermute(share, 'layer', trio[turn])  13.9 us
    ppermute x2, starting transfers between devices, body(): ends.insert(2 * j + 1, lax.ppermute(far, 'layer', across))  10.4 us
    pallas_call x8, Pallas kernels, call(): pl.pallas_call(kernel, out_shape=out_shape, in_specs=in_specs, out_specs=...  10.3 us
    ppermute x2, waiting for transfers between devices, body(): ends.insert(2 * j + 1, lax.ppermute(far, 'layer', across))  7.43 us
    unnamed x16, local copies, waits for them, and re-layouts  6.7 us
    ppermute x4, waiting for transfers between devices, body(): lax.ppermute(share, 'layer', trio[turn])  4.09 us
  transfers between devices with their start and end apart: 13, of which 7 were waited for; matrix products, arithmetic and copies ran while one was open for 0% of the time, Pallas kernels for 6%

profile of v2, /device:TPU:56, one launch (start us, length us, event | category | flops | bytes accessed | tf_op | source)
XLA Modules:
  0.0 114.2 jit_solution(6686883703927462114)
XLA Ops:
  0.0 0.0 copy-start.5
  0.0 1.0 copy-done.5
  1.0 0.0 copy-start.6
  1.0 0.7 copy-done.6
  1.7 0.6 shard_map.46
  2.3 0.0 copy-start
  2.3 1.4 %copy-done = bf16[1,1,2,6,256,256]{5,4,3,2,1,0:T(8,128)(2,1)S(1)} copy-done((bf16[1,1,2,6,256,256]{5,4,3,2,1,0:T(8,128)(2,1)S(1)}, bf16[1,1,2,6,256,256]{5,4,3,2,1,0:T(8,128)(2,1)}, u32[]{:S(2)}) %copy-start) | copy-done | bytes 1572888
  3.7 0.0 copy-start.7
  3.7 0.7 copy-done.7
  4.4 1.7 %shard_map.47 = (bf16[3104,256]{1,0:T(8,128)(2,1)S(1)}, bf16[1552,256]{1,0:T(8,128)(2,1)}, bf16[1056,256]{1,0:T(8,128)(2,1)S(1)}) custom-call(s32[2,6]{1,0:T(2,128)S(1)} %bitcast.8, bf16[2,6,256,256]{3,2,1,0:T(8,128)(2,1)S(1)} %bitcast.5, bf16[528,256]{1,0:T(8,128)(2,1)S(1)} %get-tuple-element.33.right_zero, bf16[528,256]{1,0:T(8,128)(2,1)S(1)} %get-tuple-element.32.right_one), custom_call_target="tpu_custom_call" | custom-call | tf_op jit(solution)/shard_map/pallas_call | solution.py:129
  6.1 2.2 %collective-permute-start.1 = (bf16[3104,256]{1,0:T(8,128)(2,1)S(1)}, bf16[3104,256]{1,0:T(8,128)(2,1)S(1)}, u32[]{:S(2)}, u32[]{:S(2)}) collective-permute-start(bf16[3104,256]{1,0:T(8,128)(2,1)S(1)} %get-tuple-element.34.own.left_one), channel_id=1, source_target_pairs={{6,0},{12,6},{18,12},{24,18},{30,24},{36,30},{42,36},{0,42},{7,1},... | collective-permute-start | bytes 4767752 | tf_op jit(solution)/shard_map/ppermute | solution.py:25
  8.3 3.2 %collective-permute-start.2 = (bf16[1056,256]{1,0:T(8,128)(2,1)S(1)}, bf16[1056,256]{1,0:T(8,128)(2,1)S(1)}, u32[]{:S(2)}, u32[]{:S(2)}) collective-permute-start(bf16[1056,256]{1,0:T(8,128)(2,1)S(1)} %get-tuple-element.35.rights), channel_id=1, source_target_pairs={{96,0},{144,48},{192,96},{240,144},{288,192},{336,240},{384,288},{... | collective-permute-start | bytes 1622024 | tf_op jit(solution)/shard_map/ppermute | solution.py:25
  11.5 2.7 %collective-permute-start.3 = (bf16[1552,256]{1,0:T(8,128)(2,1)}, bf16[1552,256]{1,0:T(8,128)(2,1)}, u32[]{:S(2)}, u32[]{:S(2)}) collective-permute-start(bf16[1552,256]{1,0:T(8,128)(2,1)} %get-tuple-element.39), channel_id=1, source_target_pairs={{12,0},{18,6},{24,12},{30,18},{36,24},{42,30},{0,36},{6,42},{13,1}... | collective-permute-start | bytes 2383880 | tf_op jit(solution)/shard_map/ppermute | solution.py:25
  14.3 15.9 %collective-permute-start.5 = (bf16[528,256]{1,0:T(8,128)(2,1)S(1)}, bf16[528,256]{1,0:T(8,128)(2,1)}, u32[]{:S(2)}, u32[]{:S(2)}) collective-permute-start(bf16[528,256]{1,0:T(8,128)(2,1)S(1)} %get-tuple-element.33.right_zero), channel_id=1, source_target_pairs={{48,0},{96,48},{144,96},{192,144},{240,192},{288,240},{336,288},{3... | collective-permute-start | bytes 811016 | tf_op jit(solution)/shard_map/ppermute | solution.py:25
  30.2 1.9 %collective-permute-start = (bf16[528,256]{1,0:T(8,128)(2,1)S(1)}, bf16[528,256]{1,0:T(8,128)(2,1)S(1)}, u32[]{:S(2)}, u32[]{:S(2)}) collective-permute-start(bf16[528,256]{1,0:T(8,128)(2,1)S(1)} %get-tuple-element.32.right_one), channel_id=1, source_target_pairs={{48,0},{96,48},{144,96},{192,144},{240,192},{288,240},{336,288},{3... | collective-permute-start | bytes 811016 | tf_op jit(solution)/shard_map/ppermute | solution.py:25
  32.1 9.6 %collective-permute-done.5.right_one = bf16[528,256]{1,0:T(8,128)(2,1)} collective-permute-done((bf16[528,256]{1,0:T(8,128)(2,1)S(1)}, bf16[528,256]{1,0:T(8,128)(2,1)}, u32[]{:S(2)}, u32[]{:S(2)}) %collective-permute-start.5) | collective-permute-done | bytes 270368 | tf_op jit(solution)/shard_map/ppermute | solution.py:25
  41.7 3.2 %collective-permute-start.6 = (bf16[528,256]{1,0:T(8,128)(2,1)}, bf16[528,256]{1,0:T(8,128)(2,1)}, u32[]{:S(2)}, u32[]{:S(2)}) collective-permute-start(bf16[528,256]{1,0:T(8,128)(2,1)} %collective-permute-done.5.right_one), channel_id=1, source_target_pairs={{96,0},{144,48},{192,96},{240,144},{288,192},{336,240},{384,288},{... | collective-permute-start | bytes 811016 | tf_op jit(solution)/shard_map/ppermute | solution.py:25
  45.0 0.0 collective-permute-done.2.twos
  45.0 0.0 collective-permute-done.1.after.left_three.left_one
  45.0 1.4 %shard_map.48 = (f32[768,256]{1,0:T(8,128)S(1)}, f32[768,256]{1,0:T(8,128)S(1)}) custom-call(bf16[3104,256]{1,0:T(8,128)(2,1)S(1)} %get-tuple-element.34.own.left_one, bf16[3104,256]{1,0:T(8,128)(2,1)S(1)} %collective-permute-done.1.after.left_three.left_one, bf16[1056,256]{1,0:T(8,128)(2,1)S(1)} %get-tuple-element.35.rights, ...), custom_call_target="tpu_custom_call" | custom-call | tf_op jit(solution)/shard_map/pallas_call | solution.py:129
  46.5 0.0 copy-start.1
  46.5 0.9 copy-done.1
  47.3 0.0 copy-start.3
  47.3 0.9 copy-done.3
  48.2 15.8 %collective-permute-done.right_one = bf16[528,256]{1,0:T(8,128)(2,1)S(1)} collective-permute-done((bf16[528,256]{1,0:T(8,128)(2,1)S(1)}, bf16[528,256]{1,0:T(8,128)(2,1)S(1)}, u32[]{:S(2)}, u32[]{:S(2)}) %collective-permute-start) | collective-permute-done | bytes 270368 | tf_op jit(solution)/shard_map/ppermute | solution.py:25
  64.0 3.2 %collective-permute-start.4 = (bf16[528,256]{1,0:T(8,128)(2,1)S(1)}, bf16[528,256]{1,0:T(8,128)(2,1)}, u32[]{:S(2)}, u32[]{:S(2)}) collective-permute-start(bf16[528,256]{1,0:T(8,128)(2,1)S(1)} %collective-permute-done.right_one), channel_id=1, source_target_pairs={{96,0},{144,48},{192,96},{240,144},{288,192},{336,240},{384,288},{... | collective-permute-start | bytes 811016 | tf_op jit(solution)/shard_map/ppermute | solution.py:25
  67.3 0.0 collective-permute-done.6.right_three
  67.3 0.0 copy-start.2
  67.3 1.1 copy-done.2
  68.4 0.0 copy-start.4
  68.4 2.0 %shard_map.49 = (bf16[256,256]{1,0:T(8,128)(2,1)S(1)}, bf16[256,256]{1,0:T(8,128)(2,1)S(1)}, bf16[256,256]{1,0:T(8,128)(2,1)S(1)}) custom-call(s32[1]{0:T(128)} %bitcast.layer, f32[768,256]{1,0:T(8,128)S(1)} %copy-done.2, bf16[3104,256]{1,0:T(8,128)(2,1)S(1)} %get-tuple-element.34.own.left_one, ...), custom_call_target="tpu_custom_call" | custom-call | tf_op jit(solution)/shard_map/pallas_call | solution.py:129
  70.5 3.2 %collective-permute-done.4.right_three = bf16[528,256]{1,0:T(8,128)(2,1)} collective-permute-done((bf16[528,256]{1,0:T(8,128)(2,1)S(1)}, bf16[528,256]{1,0:T(8,128)(2,1)}, u32[]{:S(2)}, u32[]{:S(2)}) %collective-permute-start.4) | collective-permute-done | bytes 270368 | tf_op jit(solution)/shard_map/ppermute | solution.py:25
  73.7 1.9 %collective-permute-start.10 = (bf16[256,256]{1,0:T(8,128)(2,1)S(1)}, bf16[256,256]{1,0:T(8,128)(2,1)S(1)}, u32[]{:S(2)}, u32[]{:S(2)}) collective-permute-start(bf16[256,256]{1,0:T(8,128)(2,1)S(1)} %get-tuple-element.50), channel_id=1, source_target_pairs={{0,2},{1,0},{2,1},{3,5},{4,3},{5,4},{6,8},{7,6},{8,7},{9,11},{10,9... | collective-permute-start | bytes 393224 | tf_op jit(solution)/shard_map/ppermute | solution.py:191
  75.6 5.3 %collective-permute-start.9 = (bf16[256,256]{1,0:T(8,128)(2,1)S(1)}, bf16[256,256]{1,0:T(8,128)(2,1)S(1)}, u32[]{:S(2)}, u32[]{:S(2)}) collective-permute-start(bf16[256,256]{1,0:T(8,128)(2,1)S(1)} %get-tuple-element.49), channel_id=1, source_target_pairs={{0,1},{1,2},{2,0},{3,4},{4,5},{5,3},{6,7},{7,8},{8,6},{9,10},{10,1... | collective-permute-start | bytes 393224 | tf_op jit(solution)/shard_map/ppermute | solution.py:191
  80.9 0.0 collective-permute-done.3.left_three
  80.9 0.0 copy-done.4
  80.9 2.8 %shard_map.50 = (bf16[256,256]{1,0:T(8,128)(2,1)S(1)}, bf16[256,256]{1,0:T(8,128)(2,1)}, bf16[256,256]{1,0:T(8,128)(2,1)}) custom-call(s32[1]{0:T(128)} %bitcast.layer, f32[768,256]{1,0:T(8,128)S(1)} %copy-done.4, bf16[3104,256]{1,0:T(8,128)(2,1)S(1)} %collective-permute-done.1.after.left_three.left_one, ...), custom_call_target="tpu_custom_call" | custom-call | tf_op jit(solution)/shard_map/pallas_call | solution.py:129
  83.7 3.7 %collective-permute-start.7 = (bf16[256,256]{1,0:T(8,128)(2,1)}, bf16[256,256]{1,0:T(8,128)(2,1)}, u32[]{:S(2)}, u32[]{:S(2)}) collective-permute-start(bf16[256,256]{1,0:T(8,128)(2,1)} %get-tuple-element.46), channel_id=1, source_target_pairs={{0,1},{1,2},{2,0},{3,4},{4,5},{5,3},{6,7},{7,8},{8,6},{9,10},{10,1... | collective-permute-start | bytes 393224 | tf_op jit(solution)/shard_map/ppermute | solution.py:191
  87.4 3.0 %collective-permute-start.8 = (bf16[256,256]{1,0:T(8,128)(2,1)}, bf16[256,256]{1,0:T(8,128)(2,1)}, u32[]{:S(2)}, u32[]{:S(2)}) collective-permute-start(bf16[256,256]{1,0:T(8,128)(2,1)} %get-tuple-element.47), channel_id=1, source_target_pairs={{0,2},{1,0},{2,1},{3,5},{4,3},{5,4},{6,8},{7,6},{8,7},{9,11},{10,9... | collective-permute-start | bytes 393224 | tf_op jit(solution)/shard_map/ppermute | solution.py:191
  90.5 0.0 collective-permute-done.10.two
  90.5 0.0 collective-permute-done.9.one
  90.5 0.1 shard_map.51
  90.5 1.7 %collective-permute-done.7.one = bf16[256,256]{1,0:T(8,128)(2,1)} collective-permute-done((bf16[256,256]{1,0:T(8,128)(2,1)}, bf16[256,256]{1,0:T(8,128)(2,1)}, u32[]{:S(2)}, u32[]{:S(2)}) %collective-permute-start.7) | collective-permute-done | bytes 131104 | tf_op jit(solution)/shard_map/ppermute | solution.py:191
  92.3 2.4 %collective-permute-done.8.two = bf16[256,256]{1,0:T(8,128)(2,1)} collective-permute-done((bf16[256,256]{1,0:T(8,128)(2,1)}, bf16[256,256]{1,0:T(8,128)(2,1)}, u32[]{:S(2)}, u32[]{:S(2)}) %collective-permute-start.8) | collective-permute-done | bytes 131104 | tf_op jit(solution)/shard_map/ppermute | solution.py:191
  94.6 1.0 shard_map.52
  95.7 8.5 %collective-permute-start.12 = (bf16[128,256]{1,0:T(8,128)(2,1)S(1)}, bf16[128,256]{1,0:T(8,128)(2,1)S(1)}, u32[]{:S(2)}, u32[]{:S(2)}) collective-permute-start(bf16[128,256]{1,0:T(8,128)(2,1)S(1)} %get-tuple-element.58), channel_id=1, source_target_pairs={{0,3},{1,4},{2,5},{3,0},{4,1},{5,2},{6,9},{7,10},{8,11},{9,6},{10,... | collective-permute-start | bytes 196616 | tf_op jit(solution)/shard_map/ppermute | solution.py:204
  104.1 1.9 %collective-permute-start.11 = (bf16[128,256]{1,0:T(8,128)(2,1)S(1)}, bf16[128,256]{1,0:T(8,128)(2,1)S(1)}, u32[]{:S(2)}, u32[]{:S(2)}) collective-permute-start(bf16[128,256]{1,0:T(8,128)(2,1)S(1)} %get-tuple-element.53), channel_id=1, source_target_pairs={{0,3},{1,4},{2,5},{3,0},{4,1},{5,2},{6,9},{7,10},{8,11},{9,6},{10,... | collective-permute-start | bytes 196616 | tf_op jit(solution)/shard_map/ppermute | solution.py:204
  106.0 1.2 %collective-permute-done.12.refs_3_ = bf16[128,256]{1,0:T(8,128)(2,1)S(1)} collective-permute-done((bf16[128,256]{1,0:T(8,128)(2,1)S(1)}, bf16[128,256]{1,0:T(8,128)(2,1)S(1)}, u32[]{:S(2)}, u32[]{:S(2)}) %collective-permute-start.12) | collective-permute-done | bytes 65568 | tf_op jit(solution)/shard_map/ppermute | solution.py:204
  107.2 6.3 %collective-permute-done.11.refs_1_ = bf16[128,256]{1,0:T(8,128)(2,1)S(1)} collective-permute-done((bf16[128,256]{1,0:T(8,128)(2,1)S(1)}, bf16[128,256]{1,0:T(8,128)(2,1)S(1)}, u32[]{:S(2)}, u32[]{:S(2)}) %collective-permute-start.11) | collective-permute-done | bytes 65568 | tf_op jit(solution)/shard_map/ppermute | solution.py:204
  113.5 0.7 shard_map.53
Async XLA Ops:
  0.0 1.0 copy-start.5
  1.0 0.7 copy-start.6
  2.3 1.4 %copy-start = (bf16[1,1,2,6,256,256]{5,4,3,2,1,0:T(8,128)(2,1)S(1)}, bf16[1,1,2,6,256,256]{5,4,3,2,1,0:T(8,128)(2,1)}, u32[]{:S(2)}) copy-start(bf16[1,1,2,6,256,256]{5,4,3,2,1,0:T(8,128)(2,1)} %param.4) | copy-start | bytes 4718596
  3.7 0.7 copy-start.7
  6.1 38.9 %collective-permute-start.1 = (bf16[3104,256]{1,0:T(8,128)(2,1)S(1)}, bf16[3104,256]{1,0:T(8,128)(2,1)S(1)}, u32[]{:S(2)}, u32[]{:S(2)}) collective-permute-start(bf16[3104,256]{1,0:T(8,128)(2,1)S(1)} %get-tuple-element.34.own.left_one), channel_id=1, source_target_pairs={{6,0},{12,6},{18,12},{24,18},{30,24},{36,30},{42,36},{0,42},{7,1},... | collective-permute-start | bytes 4767752 | tf_op jit(solution)/shard_map/ppermute | solution.py:25
  8.3 36.7 %collective-permute-start.2 = (bf16[1056,256]{1,0:T(8,128)(2,1)S(1)}, bf16[1056,256]{1,0:T(8,128)(2,1)S(1)}, u32[]{:S(2)}, u32[]{:S(2)}) collective-permute-start(bf16[1056,256]{1,0:T(8,128)(2,1)S(1)} %get-tuple-element.35.rights), channel_id=1, source_target_pairs={{96,0},{144,48},{192,96},{240,144},{288,192},{336,240},{384,288},{... | collective-permute-start | bytes 1622024 | tf_op jit(solution)/shard_map/ppermute | solution.py:25
  11.5 69.4 %collective-permute-start.3 = (bf16[1552,256]{1,0:T(8,128)(2,1)}, bf16[1552,256]{1,0:T(8,128)(2,1)}, u32[]{:S(2)}, u32[]{:S(2)}) collective-permute-start(bf16[1552,256]{1,0:T(8,128)(2,1)} %get-tuple-element.39), channel_id=1, source_target_pairs={{12,0},{18,6},{24,12},{30,18},{36,24},{42,30},{0,36},{6,42},{13,1}... | collective-permute-start | bytes 2383880 | tf_op jit(solution)/shard_map/ppermute | solution.py:25
  14.3 27.5 %collective-permute-start.5 = (bf16[528,256]{1,0:T(8,128)(2,1)S(1)}, bf16[528,256]{1,0:T(8,128)(2,1)}, u32[]{:S(2)}, u32[]{:S(2)}) collective-permute-start(bf16[528,256]{1,0:T(8,128)(2,1)S(1)} %get-tuple-element.33.right_zero), channel_id=1, source_target_pairs={{48,0},{96,48},{144,96},{192,144},{240,192},{288,240},{336,288},{3... | collective-permute-start | bytes 811016 | tf_op jit(solution)/shard_map/ppermute | solution.py:25
  30.2 33.8 %collective-permute-start = (bf16[528,256]{1,0:T(8,128)(2,1)S(1)}, bf16[528,256]{1,0:T(8,128)(2,1)S(1)}, u32[]{:S(2)}, u32[]{:S(2)}) collective-permute-start(bf16[528,256]{1,0:T(8,128)(2,1)S(1)} %get-tuple-element.32.right_one), channel_id=1, source_target_pairs={{48,0},{96,48},{144,96},{192,144},{240,192},{288,240},{336,288},{3... | collective-permute-start | bytes 811016 | tf_op jit(solution)/shard_map/ppermute | solution.py:25
  41.7 25.5 %collective-permute-start.6 = (bf16[528,256]{1,0:T(8,128)(2,1)}, bf16[528,256]{1,0:T(8,128)(2,1)}, u32[]{:S(2)}, u32[]{:S(2)}) collective-permute-start(bf16[528,256]{1,0:T(8,128)(2,1)} %collective-permute-done.5.right_one), channel_id=1, source_target_pairs={{96,0},{144,48},{192,96},{240,144},{288,192},{336,240},{384,288},{... | collective-permute-start | bytes 811016 | tf_op jit(solution)/shard_map/ppermute | solution.py:25
  46.5 0.9 copy-start.1
  47.3 0.9 copy-start.3
  64.0 9.7 %collective-permute-start.4 = (bf16[528,256]{1,0:T(8,128)(2,1)S(1)}, bf16[528,256]{1,0:T(8,128)(2,1)}, u32[]{:S(2)}, u32[]{:S(2)}) collective-permute-start(bf16[528,256]{1,0:T(8,128)(2,1)S(1)} %collective-permute-done.right_one), channel_id=1, source_target_pairs={{96,0},{144,48},{192,96},{240,144},{288,192},{336,240},{384,288},{... | collective-permute-start | bytes 811016 | tf_op jit(solution)/shard_map/ppermute | solution.py:25
  67.3 1.1 copy-start.2
  68.4 12.5 %copy-start.4 = (f32[768,256]{1,0:T(8,128)S(1)}, f32[768,256]{1,0:T(8,128)}, u32[]{:S(2)}) copy-start(f32[768,256]{1,0:T(8,128)} %copy-done.3) | copy-start | bytes 2359300
  73.7 16.8 %collective-permute-start.10 = (bf16[256,256]{1,0:T(8,128)(2,1)S(1)}, bf16[256,256]{1,0:T(8,128)(2,1)S(1)}, u32[]{:S(2)}, u32[]{:S(2)}) collective-permute-start(bf16[256,256]{1,0:T(8,128)(2,1)S(1)} %get-tuple-element.50), channel_id=1, source_target_pairs={{0,2},{1,0},{2,1},{3,5},{4,3},{5,4},{6,8},{7,6},{8,7},{9,11},{10,9... | collective-permute-start | bytes 393224 | tf_op jit(solution)/shard_map/ppermute | solution.py:191
  75.6 14.9 %collective-permute-start.9 = (bf16[256,256]{1,0:T(8,128)(2,1)S(1)}, bf16[256,256]{1,0:T(8,128)(2,1)S(1)}, u32[]{:S(2)}, u32[]{:S(2)}) collective-permute-start(bf16[256,256]{1,0:T(8,128)(2,1)S(1)} %get-tuple-element.49), channel_id=1, source_target_pairs={{0,1},{1,2},{2,0},{3,4},{4,5},{5,3},{6,7},{7,8},{8,6},{9,10},{10,1... | collective-permute-start | bytes 393224 | tf_op jit(solution)/shard_map/ppermute | solution.py:191
  83.7 8.6 %collective-permute-start.7 = (bf16[256,256]{1,0:T(8,128)(2,1)}, bf16[256,256]{1,0:T(8,128)(2,1)}, u32[]{:S(2)}, u32[]{:S(2)}) collective-permute-start(bf16[256,256]{1,0:T(8,128)(2,1)} %get-tuple-element.46), channel_id=1, source_target_pairs={{0,1},{1,2},{2,0},{3,4},{4,5},{5,3},{6,7},{7,8},{8,6},{9,10},{10,1... | collective-permute-start | bytes 393224 | tf_op jit(solution)/shard_map/ppermute | solution.py:191
  87.4 7.2 %collective-permute-start.8 = (bf16[256,256]{1,0:T(8,128)(2,1)}, bf16[256,256]{1,0:T(8,128)(2,1)}, u32[]{:S(2)}, u32[]{:S(2)}) collective-permute-start(bf16[256,256]{1,0:T(8,128)(2,1)} %get-tuple-element.47), channel_id=1, source_target_pairs={{0,2},{1,0},{2,1},{3,5},{4,3},{5,4},{6,8},{7,6},{8,7},{9,11},{10,9... | collective-permute-start | bytes 393224 | tf_op jit(solution)/shard_map/ppermute | solution.py:191
  95.7 11.5 %collective-permute-start.12 = (bf16[128,256]{1,0:T(8,128)(2,1)S(1)}, bf16[128,256]{1,0:T(8,128)(2,1)S(1)}, u32[]{:S(2)}, u32[]{:S(2)}) collective-permute-start(bf16[128,256]{1,0:T(8,128)(2,1)S(1)} %get-tuple-element.58), channel_id=1, source_target_pairs={{0,3},{1,4},{2,5},{3,0},{4,1},{5,2},{6,9},{7,10},{8,11},{9,6},{10,... | collective-permute-start | bytes 196616 | tf_op jit(solution)/shard_map/ppermute | solution.py:204
  104.1 9.4 %collective-permute-start.11 = (bf16[128,256]{1,0:T(8,128)(2,1)S(1)}, bf16[128,256]{1,0:T(8,128)(2,1)S(1)}, u32[]{:S(2)}, u32[]{:S(2)}) collective-permute-start(bf16[128,256]{1,0:T(8,128)(2,1)S(1)} %get-tuple-element.53), channel_id=1, source_target_pairs={{0,3},{1,4},{2,5},{3,0},{4,1},{5,2},{6,9},{7,10},{8,11},{9,6},{10,... | collective-permute-start | bytes 196616 | tf_op jit(solution)/shard_map/ppermute | solution.py:204

commit v3 on v2

--- a/solution.py
+++ b/solution.py
@@ -65,39 +65,47 @@
     packed_ref[slots * TS :, :] = note.astype(jnp.float32).astype(jnp.bfloat16)
 
 
-def pack_right_kernel(place_ref, right_ref, *pieces):
-    for column, piece in enumerate(pieces):
+def pack_right_kernel(place_ref, right_ref, rights):
+    for column in range(HELD):
+        piece = rights.at[column * PIECE : (column + 1) * PIECE]
         for p in range(SB):
             piece[p * TS : (p + 1) * TS, :] = right_ref[column, p]
         write_note(piece, place_ref, column, SB)
 
 
-def pack_left_kernel(place_ref, left_ref, right_zero, right_one, lefts, left_zero, rights):
+def pack_left_kernel(place_ref, left_ref, lefts, left_zero):
     for column in range(HELD):
         targets = [lefts.at[column * BLOCK : (column + 1) * BLOCK]] + [left_zero] * (column == 0)
         for target in targets:
             for q in range(SA):
                 target[q * TS : (q + 1) * TS, :] = left_ref[column, q]
             write_note(target, place_ref, column, SA)
-    rights[:PIECE, :] = right_zero[...]
-    rights[PIECE:, :] = right_one[...]
-
-
-def early_kernel(own, after, rights, twos, *refs):
+
+
+def part(ref, column, rows):
+    return ref.at[column * rows : (column + 1) * rows]
+
+
+def local_kernel(lefts, rights, *refs):
     totals, place_ref = refs[:-1], refs[-1]
     for column, total in enumerate(totals):
-        left = pl.ds(column * BLOCK, BLOCK)
-        right = pl.ds(column * PIECE, PIECE)
         total[...] = jnp.zeros_like(total)
-        add_term(total, place_ref, own.at[left], rights.at[right])
-        add_term(total, place_ref, after.at[left], twos.at[right])
-
-
-def late_kernel(layer, start_ref, left_one, left_three, right_one, right_three, *refs, blocks):
+        add_term(total, place_ref, part(lefts, column, BLOCK), part(rights, column, PIECE))
+
+
+def early_kernel(lefts, left_next, right_one, right_two, *refs):
+    starts, totals, place_ref = refs[:HELD], refs[HELD:-1], refs[-1]
+    for column, (start, total) in enumerate(zip(starts, totals)):
+        total[...] = start[...]
+        after = part(left_next, 0, BLOCK) if column else part(lefts, 1, BLOCK)
+        add_term(total, place_ref, after, part(right_one, column, PIECE))
+        add_term(total, place_ref, part(left_next, column, BLOCK), part(right_two, column, PIECE))
+
+
+def late_kernel(layer, total_ref, left, right, *refs, block):
     share_refs, total, place_ref = refs[:-2], refs[-2], refs[-1]
-    total[...] = start_ref[...]
-    for left, block, right in ((left_one, blocks[0], right_one), (left_three, blocks[1], right_three)):
-        add_term(total, place_ref, left.at[pl.ds(block * BLOCK, BLOCK)], right)
+    total[...] = total_ref[...]
+    add_term(total, place_ref, part(left, block, BLOCK), right)
     half = layer[0] // TRIO
     for turn, share in enumerate(share_refs):
         spot = lax.rem(layer[0] + turn, TRIO)
@@ -119,7 +127,7 @@
         out_ref[:, n * TS : (n + 1) * TS] = added.astype(out_ref.dtype)
 
 
-AHEAD = 10**12
+AHEAD = 10**10
 SMEM = pl.BlockSpec(memory_space=pltpu.SMEM)
 VMEM = pl.BlockSpec(memory_space=pltpu.VMEM)
 PARAMS = pltpu.CompilerParams(vmem_limit_bytes=32 * 1024 * 1024)
@@ -144,45 +152,36 @@
 def body(left_tiles, left_place, right_tiles, right_place):
     layer = lax.axis_index("layer").astype(jnp.int32).reshape(1)
     places = pltpu.SMEM((SA,), jnp.int32)
-    pieces = call(
-        pack_right_kernel,
-        [array(PIECE, TS)] * HELD,
+    sums = [array(RT * TS, TS, jnp.float32)] * HELD
+    rights = call(pack_right_kernel, array(HELD * PIECE, TS), [SMEM, VMEM], (right_place[0, 0], right_tiles[0, 0]))
+    right_one = shifted(rights, "row", -1)
+    lefts, left_zero = call(
+        pack_left_kernel,
+        [array(HELD * BLOCK, TS), array(BLOCK, TS)],
         [SMEM, VMEM],
-        (right_place[0, 0], right_tiles[0, 0]),
-    )
-    right_one = [shifted(piece, "row", -1) for piece in pieces]
-    lefts, left_zero, rights = call(
-        pack_left_kernel,
-        [array(HELD * BLOCK, TS), array(BLOCK, TS), array(HELD * PIECE, TS)],
-        [SMEM] + [VMEM] * 3,
-        (left_place[0, 0], left_tiles[0, 0], *pieces),
+        (left_place[0, 0], left_tiles[0, 0]),
     )
     right_two = shifted(rights, "row", -2)
     left_next = shifted(lefts, "col", -1)
     left_last = shifted(left_zero, "col", -2)
-    totals = call(
-        early_kernel,
-        [array(RT * TS, TS, jnp.float32)] * HELD,
-        [VMEM] * 4,
-        (lefts, left_next, rights, right_two),
-        [places],
-    )
-    right_one[1], totals = lax.optimization_barrier((right_one[1], totals))
-    right_three = [shifted(piece, "row", -2) for piece in right_one]
-    held = [(lefts, 0), (lefts, 1), (left_next, 0), (left_next, 1), (left_last, 0)]
+    right_one, own = lax.optimization_barrier((right_one, rights))
+    totals = call(local_kernel, sums, [VMEM] * 2, (lefts, own), [places], cost=AHEAD)
+    totals = call(early_kernel, sums, [VMEM] * (4 + HELD), (lefts, left_next, right_one, right_two, *totals), [places])
+    right_three = [shifted(right_one[j * PIECE : (j + 1) * PIECE], "row", -2) for j in range(HELD)]
+    held = [(left_next, 1), (left_last, 0)]
     trio = [[(p, p // TRIO * TRIO + (p + turn) % TRIO) for p in range(2 * TRIO)] for turn in range(TRIO)]
     across = [(p, (p + TRIO) % (2 * TRIO)) for p in range(2 * TRIO)]
     shares = []
     for j in range(HELD):
         if j:
             right_three[j], shares[j - 1] = lax.optimization_barrier((right_three[j], shares[j - 1]))
-        (one, block_one), (three, block_three) = held[j + 1], held[j + 3]
+        left, block = held[j]
         shares.append(
             call(
-                functools.partial(late_kernel, blocks=(block_one, block_three)),
+                functools.partial(late_kernel, block=block),
                 [array(2 * SHARE, TS)] * TRIO,
-                [SMEM] + [VMEM] * 5,
-                (layer, totals[j], one, three, right_one[j], right_three[j]),
+                [SMEM] + [VMEM] * 3,
+                (layer, totals[j], left, right_three[j]),
                 [pltpu.VMEM((RT * TS, TS), jnp.float32), places],
             )
         )
@@ -196,7 +195,7 @@
             [array(SHARE, TS, jnp.float32), array(SHARE, TS)],
             [VMEM] * TRIO,
             (own_share, *arrived),
-            cost=(1 - j) * AHEAD,
+            cost=(1 - j) * 10**12,
         )
         ends.append(near)
         shares[j] = far

time: 115 us -> 108 us (0.939)
  waiting for transfers between devices: 40.1 us -> 36.2 us
  local copies, waits for them, and re-layouts: 6.7 us -> 3.84 us
  starting transfers between devices: 56.8 us -> 55.2 us
    ppermute x7 -> x6, waiting for transfers between devices: 28.6 us -> 24.7 us  [shifted(): lax.ppermute(block, axis, [((i - distance) % size, i) for i in range(size)])]
    unnamed x16 -> x8, local copies, waits for them, and re-layouts: 6.7 us -> 3.8 us
    ppermute x7 -> x6, starting transfers between devices: 32.5 us -> 30.4 us  [shifted(): lax.ppermute(block, axis, [((i - distance) % size, i) for i in range(size)])]
    pallas_call x8 -> x9, Pallas kernels: 10.3 us -> 11.1 us  [call(): pl.pallas_call(kernel, out_shape=out_shape, in_specs=in_specs, out_specs=...]
  transfers between devices with their start and end apart: 13 -> 12, of which waited for: 7 -> 7; matrix products, arithmetic and copies ran while one was open for 0% -> 0% of each run, Pallas kernels for 6% -> 8%
where the time goes in v3:
time: 108 us; the launch traced here: 107 us
  starting transfers between devices  55.2 us (51%)
  waiting for transfers between devices  36.2 us (34%)
  Pallas kernels  11.1 us (10%)
  local copies, waits for them, and re-layouts  3.84 us (4%)
    ppermute x6, starting transfers between devices, shifted(): lax.ppermute(block, axis, [((i - distance) % size, i) for i in range(size)])  30.4 us
    ppermute x6, waiting for transfers between devices, shifted(): lax.ppermute(block, axis, [((i - distance) % size, i) for i in range(size)])  24.7 us
    ppermute x4, starting transfers between devices, body(): lax.ppermute(share, 'layer', trio[turn])  14.5 us
    pallas_call x9, Pallas kernels, call(): pl.pallas_call(kernel, out_shape=out_shape, in_specs=in_specs, out_specs=...  11.1 us
    ppermute x2, starting transfers between devices, body(): ends.insert(2 * j + 1, lax.ppermute(far, 'layer', across))  10.3 us
    ppermute x2, waiting for transfers between devices, body(): ends.insert(2 * j + 1, lax.ppermute(far, 'layer', across))  7.04 us
    ppermute x4, waiting for transfers between devices, body(): lax.ppermute(share, 'layer', trio[turn])  4.46 us
    unnamed x8, local copies, waits for them, and re-layouts  3.8 us
  transfers between devices with their start and end apart: 12, of which 7 were waited for; matrix products, arithmetic and copies ran while one was open for 0% of the time, Pallas kernels for 8%

profile of v3, /device:TPU:56, one launch (start us, length us, event | category | flops | bytes accessed | tf_op | source)
XLA Modules:
  0.0 106.5 jit_solution(6138992082415753675)
XLA Ops:
  0.0 0.0 copy-start.1
  0.0 1.0 copy-done.1
  1.0 0.0 copy-start.2
  1.0 0.7 copy-done.2
  1.7 0.6 shard_map.47.rights
  2.3 15.9 %collective-permute-start.1 = (bf16[1056,256]{1,0:T(8,128)(2,1)S(1)}, bf16[1056,256]{1,0:T(8,128)(2,1)S(1)}, u32[]{:S(2)}, u32[]{:S(2)}) collective-permute-start(bf16[1056,256]{1,0:T(8,128)(2,1)S(1)} %shard_map.47.rights), channel_id=1, source_target_pairs={{48,0},{96,48},{144,96},{192,144},{240,192},{288,240},{336,288},{3... | collective-permute-start | bytes 1622024 | tf_op jit(solution)/shard_map/ppermute | solution.py:25
  18.2 0.0 copy-start
  18.3 1.4 %copy-done = bf16[1,1,2,6,256,256]{5,4,3,2,1,0:T(8,128)(2,1)S(1)} copy-done((bf16[1,1,2,6,256,256]{5,4,3,2,1,0:T(8,128)(2,1)S(1)}, bf16[1,1,2,6,256,256]{5,4,3,2,1,0:T(8,128)(2,1)}, u32[]{:S(2)}) %copy-start) | copy-done | bytes 1572888
  19.7 0.0 copy-start.3
  19.7 0.7 copy-done.3
  20.3 2.1 %shard_map.46 = (bf16[3104,256]{1,0:T(8,128)(2,1)}, bf16[1552,256]{1,0:T(8,128)(2,1)}) custom-call(s32[2,6]{1,0:T(2,128)S(1)} %bitcast.8, bf16[2,6,256,256]{3,2,1,0:T(8,128)(2,1)S(1)} %bitcast.5), custom_call_target="tpu_custom_call" | custom-call | tf_op jit(solution)/shard_map/pallas_call | solution.py:137
  22.4 1.9 %collective-permute-start = (bf16[3104,256]{1,0:T(8,128)(2,1)}, bf16[3104,256]{1,0:T(8,128)(2,1)S(1)}, u32[]{:S(2)}, u32[]{:S(2)}) collective-permute-start(bf16[3104,256]{1,0:T(8,128)(2,1)} %get-tuple-element.30.lefts), channel_id=1, source_target_pairs={{6,0},{12,6},{18,12},{24,18},{30,24},{36,30},{42,36},{0,42},{7,1},... | collective-permute-start | bytes 4767752 | tf_op jit(solution)/shard_map/ppermute | solution.py:25
  24.3 3.2 %collective-permute-start.2 = (bf16[1056,256]{1,0:T(8,128)(2,1)S(1)}, bf16[1056,256]{1,0:T(8,128)(2,1)}, u32[]{:S(2)}, u32[]{:S(2)}) collective-permute-start(bf16[1056,256]{1,0:T(8,128)(2,1)S(1)} %shard_map.47.rights), channel_id=1, source_target_pairs={{96,0},{144,48},{192,96},{240,144},{288,192},{336,240},{384,288},{... | collective-permute-start | bytes 1622024 | tf_op jit(solution)/shard_map/ppermute | solution.py:25
  27.6 2.8 %collective-permute-start.3 = (bf16[1552,256]{1,0:T(8,128)(2,1)}, bf16[1552,256]{1,0:T(8,128)(2,1)S(1)}, u32[]{:S(2)}, u32[]{:S(2)}) collective-permute-start(bf16[1552,256]{1,0:T(8,128)(2,1)} %get-tuple-element.36), channel_id=1, source_target_pairs={{12,0},{18,6},{24,12},{30,18},{36,24},{42,30},{0,36},{6,42},{13,1}... | collective-permute-start | bytes 2383880 | tf_op jit(solution)/shard_map/ppermute | solution.py:25
  30.4 21.8 %collective-permute-done.1.right_one = bf16[1056,256]{1,0:T(8,128)(2,1)S(1)} collective-permute-done((bf16[1056,256]{1,0:T(8,128)(2,1)S(1)}, bf16[1056,256]{1,0:T(8,128)(2,1)S(1)}, u32[]{:S(2)}, u32[]{:S(2)}) %collective-permute-start.1) | collective-permute-done | bytes 540704 | tf_op jit(solution)/shard_map/ppermute | solution.py:25
  52.2 3.3 %collective-permute-start.5 = (bf16[528,256]{1,0:T(8,128)(2,1)S(1)}, bf16[528,256]{1,0:T(8,128)(2,1)S(1)}, u32[]{:S(2)}, u32[]{:S(2)}) collective-permute-start(bf16[528,256]{1,0:T(8,128)(2,1)S(1)} %get-tuple-element.55), channel_id=1, source_target_pairs={{96,0},{144,48},{192,96},{240,144},{288,192},{336,240},{384,288},{... | collective-permute-start | bytes 811016 | tf_op jit(solution)/shard_map/ppermute | solution.py:25
  55.4 3.3 %collective-permute-start.4 = (bf16[528,256]{1,0:T(8,128)(2,1)S(1)}, bf16[528,256]{1,0:T(8,128)(2,1)S(1)}, u32[]{:S(2)}, u32[]{:S(2)}) collective-permute-start(bf16[528,256]{1,0:T(8,128)(2,1)S(1)} %get-tuple-element.56), channel_id=1, source_target_pairs={{96,0},{144,48},{192,96},{240,144},{288,192},{336,240},{384,288},{... | collective-permute-start | bytes 811016 | tf_op jit(solution)/shard_map/ppermute | solution.py:25
  58.7 2.2 %shard_map.48 = (f32[768,256]{1,0:T(8,128)S(1)}, f32[768,256]{1,0:T(8,128)S(1)}) custom-call(bf16[3104,256]{1,0:T(8,128)(2,1)} %get-tuple-element.30.lefts, bf16[1056,256]{1,0:T(8,128)(2,1)S(1)} %shard_map.47.rights), custom_call_target="tpu_custom_call" | custom-call | flops 10000000000 | tf_op jit(solution)/shard_map/pallas_call | solution.py:137
  61.0 0.0 collective-permute-done.2.right_two
  61.0 0.0 collective-permute-done.left_next.left
  61.0 3.2 %shard_map.49 = (f32[768,256]{1,0:T(8,128)S(1)}, f32[768,256]{1,0:T(8,128)S(1)}) custom-call(bf16[3104,256]{1,0:T(8,128)(2,1)} %get-tuple-element.30.lefts, bf16[3104,256]{1,0:T(8,128)(2,1)S(1)} %collective-permute-done.left_next.left, bf16[1056,256]{1,0:T(8,128)(2,1)S(1)} %collective-permute-done.1.right_one, ...), custom_call_target="tpu_custom_call" | custom-call | tf_op jit(solution)/shard_map/pallas_call | solution.py:137
  64.2 0.3 collective-permute-done.5.right
  64.5 0.3 shard_map.50
  64.8 2.6 %collective-permute-done.4.right = bf16[528,256]{1,0:T(8,128)(2,1)S(1)} collective-permute-done((bf16[528,256]{1,0:T(8,128)(2,1)S(1)}, bf16[528,256]{1,0:T(8,128)(2,1)S(1)}, u32[]{:S(2)}, u32[]{:S(2)}) %collective-permute-start.4) | collective-permute-done | bytes 270368 | tf_op jit(solution)/shard_map/ppermute | solution.py:25
  67.4 5.9 %collective-permute-start.8 = (bf16[256,256]{1,0:T(8,128)(2,1)S(1)}, bf16[256,256]{1,0:T(8,128)(2,1)S(1)}, u32[]{:S(2)}, u32[]{:S(2)}) collective-permute-start(bf16[256,256]{1,0:T(8,128)(2,1)S(1)} %get-tuple-element.45), channel_id=1, source_target_pairs={{0,1},{1,2},{2,0},{3,4},{4,5},{5,3},{6,7},{7,8},{8,6},{9,10},{10,1... | collective-permute-start | bytes 393224 | tf_op jit(solution)/shard_map/ppermute | solution.py:190
  73.3 1.9 %collective-permute-start.9 = (bf16[256,256]{1,0:T(8,128)(2,1)S(1)}, bf16[256,256]{1,0:T(8,128)(2,1)S(1)}, u32[]{:S(2)}, u32[]{:S(2)}) collective-permute-start(bf16[256,256]{1,0:T(8,128)(2,1)S(1)} %get-tuple-element.46), channel_id=1, source_target_pairs={{0,2},{1,0},{2,1},{3,5},{4,3},{5,4},{6,8},{7,6},{8,7},{9,11},{10,9... | collective-permute-start | bytes 393224 | tf_op jit(solution)/shard_map/ppermute | solution.py:190
  75.2 0.0 collective-permute-done.3.left
  75.2 1.0 shard_map.51
  76.2 4.1 %collective-permute-start.6 = (bf16[256,256]{1,0:T(8,128)(2,1)}, bf16[256,256]{1,0:T(8,128)(2,1)}, u32[]{:S(2)}, u32[]{:S(2)}) collective-permute-start(bf16[256,256]{1,0:T(8,128)(2,1)} %get-tuple-element.42), channel_id=1, source_target_pairs={{0,1},{1,2},{2,0},{3,4},{4,5},{5,3},{6,7},{7,8},{8,6},{9,10},{10,1... | collective-permute-start | bytes 393224 | tf_op jit(solution)/shard_map/ppermute | solution.py:190
  80.3 2.6 %collective-permute-start.7 = (bf16[256,256]{1,0:T(8,128)(2,1)}, bf16[256,256]{1,0:T(8,128)(2,1)}, u32[]{:S(2)}, u32[]{:S(2)}) collective-permute-start(bf16[256,256]{1,0:T(8,128)(2,1)} %get-tuple-element.43), channel_id=1, source_target_pairs={{0,2},{1,0},{2,1},{3,5},{4,3},{5,4},{6,8},{7,6},{8,7},{9,11},{10,9... | collective-permute-start | bytes 393224 | tf_op jit(solution)/shard_map/ppermute | solution.py:190
  82.9 0.0 collective-permute-done.8.one
  82.9 0.0 collective-permute-done.9.two
  83.0 0.1 shard_map.52
  83.0 1.9 %collective-permute-done.6.one = bf16[256,256]{1,0:T(8,128)(2,1)} collective-permute-done((bf16[256,256]{1,0:T(8,128)(2,1)}, bf16[256,256]{1,0:T(8,128)(2,1)}, u32[]{:S(2)}, u32[]{:S(2)}) %collective-permute-start.6) | collective-permute-done | bytes 131104 | tf_op jit(solution)/shard_map/ppermute | solution.py:190
  84.9 2.6 %collective-permute-done.7.two = bf16[256,256]{1,0:T(8,128)(2,1)} collective-permute-done((bf16[256,256]{1,0:T(8,128)(2,1)}, bf16[256,256]{1,0:T(8,128)(2,1)}, u32[]{:S(2)}, u32[]{:S(2)}) %collective-permute-start.7) | collective-permute-done | bytes 131104 | tf_op jit(solution)/shard_map/ppermute | solution.py:190
  87.5 1.0 shard_map.53
  88.5 8.4 %collective-permute-start.11 = (bf16[128,256]{1,0:T(8,128)(2,1)S(1)}, bf16[128,256]{1,0:T(8,128)(2,1)S(1)}, u32[]{:S(2)}, u32[]{:S(2)}) collective-permute-start(bf16[128,256]{1,0:T(8,128)(2,1)S(1)} %get-tuple-element.54), channel_id=1, source_target_pairs={{0,3},{1,4},{2,5},{3,0},{4,1},{5,2},{6,9},{7,10},{8,11},{9,6},{10,... | collective-permute-start | bytes 196616 | tf_op jit(solution)/shard_map/ppermute | solution.py:203
  96.9 1.9 %collective-permute-start.10 = (bf16[128,256]{1,0:T(8,128)(2,1)S(1)}, bf16[128,256]{1,0:T(8,128)(2,1)S(1)}, u32[]{:S(2)}, u32[]{:S(2)}) collective-permute-start(bf16[128,256]{1,0:T(8,128)(2,1)S(1)} %get-tuple-element.49), channel_id=1, source_target_pairs={{0,3},{1,4},{2,5},{3,0},{4,1},{5,2},{6,9},{7,10},{8,11},{9,6},{10,... | collective-permute-start | bytes 196616 | tf_op jit(solution)/shard_map/ppermute | solution.py:203
  98.8 0.7 collective-permute-done.11.refs_3_
  99.5 6.4 %collective-permute-done.10.refs_1_ = bf16[128,256]{1,0:T(8,128)(2,1)S(1)} collective-permute-done((bf16[128,256]{1,0:T(8,128)(2,1)S(1)}, bf16[128,256]{1,0:T(8,128)(2,1)S(1)}, u32[]{:S(2)}, u32[]{:S(2)}) %collective-permute-start.10) | collective-permute-done | bytes 65568 | tf_op jit(solution)/shard_map/ppermute | solution.py:203
  105.8 0.7 shard_map.54
  (1 shorter events, 0.0 us)
Async XLA Ops:
  0.0 1.0 copy-start.1
  1.0 0.7 copy-start.2
  2.3 49.8 %collective-permute-start.1 = (bf16[1056,256]{1,0:T(8,128)(2,1)S(1)}, bf16[1056,256]{1,0:T(8,128)(2,1)S(1)}, u32[]{:S(2)}, u32[]{:S(2)}) collective-permute-start(bf16[1056,256]{1,0:T(8,128)(2,1)S(1)} %shard_map.47.rights), channel_id=1, source_target_pairs={{48,0},{96,48},{144,96},{192,144},{240,192},{288,240},{336,288},{3... | collective-permute-start | bytes 1622024 | tf_op jit(solution)/shard_map/ppermute | solution.py:25
  18.2 1.4 %copy-start = (bf16[1,1,2,6,256,256]{5,4,3,2,1,0:T(8,128)(2,1)S(1)}, bf16[1,1,2,6,256,256]{5,4,3,2,1,0:T(8,128)(2,1)}, u32[]{:S(2)}) copy-start(bf16[1,1,2,6,256,256]{5,4,3,2,1,0:T(8,128)(2,1)} %param.4) | copy-start | bytes 4718596
  19.7 0.7 copy-start.3
  22.4 38.5 %collective-permute-start = (bf16[3104,256]{1,0:T(8,128)(2,1)}, bf16[3104,256]{1,0:T(8,128)(2,1)S(1)}, u32[]{:S(2)}, u32[]{:S(2)}) collective-permute-start(bf16[3104,256]{1,0:T(8,128)(2,1)} %get-tuple-element.30.lefts), channel_id=1, source_target_pairs={{6,0},{12,6},{18,12},{24,18},{30,24},{36,30},{42,36},{0,42},{7,1},... | collective-permute-start | bytes 4767752 | tf_op jit(solution)/shard_map/ppermute | solution.py:25
  24.3 36.6 %collective-permute-start.2 = (bf16[1056,256]{1,0:T(8,128)(2,1)S(1)}, bf16[1056,256]{1,0:T(8,128)(2,1)}, u32[]{:S(2)}, u32[]{:S(2)}) collective-permute-start(bf16[1056,256]{1,0:T(8,128)(2,1)S(1)} %shard_map.47.rights), channel_id=1, source_target_pairs={{96,0},{144,48},{192,96},{240,144},{288,192},{336,240},{384,288},{... | collective-permute-start | bytes 1622024 | tf_op jit(solution)/shard_map/ppermute | solution.py:25
  27.6 47.6 %collective-permute-start.3 = (bf16[1552,256]{1,0:T(8,128)(2,1)}, bf16[1552,256]{1,0:T(8,128)(2,1)S(1)}, u32[]{:S(2)}, u32[]{:S(2)}) collective-permute-start(bf16[1552,256]{1,0:T(8,128)(2,1)} %get-tuple-element.36), channel_id=1, source_target_pairs={{12,0},{18,6},{24,12},{30,18},{36,24},{42,30},{0,36},{6,42},{13,1}... | collective-permute-start | bytes 2383880 | tf_op jit(solution)/shard_map/ppermute | solution.py:25
  52.2 12.3 %collective-permute-start.5 = (bf16[528,256]{1,0:T(8,128)(2,1)S(1)}, bf16[528,256]{1,0:T(8,128)(2,1)S(1)}, u32[]{:S(2)}, u32[]{:S(2)}) collective-permute-start(bf16[528,256]{1,0:T(8,128)(2,1)S(1)} %get-tuple-element.55), channel_id=1, source_target_pairs={{96,0},{144,48},{192,96},{240,144},{288,192},{336,240},{384,288},{... | collective-permute-start | bytes 811016 | tf_op jit(solution)/shard_map/ppermute | solution.py:25
  55.4 11.9 %collective-permute-start.4 = (bf16[528,256]{1,0:T(8,128)(2,1)S(1)}, bf16[528,256]{1,0:T(8,128)(2,1)S(1)}, u32[]{:S(2)}, u32[]{:S(2)}) collective-permute-start(bf16[528,256]{1,0:T(8,128)(2,1)S(1)} %get-tuple-element.56), channel_id=1, source_target_pairs={{96,0},{144,48},{192,96},{240,144},{288,192},{336,240},{384,288},{... | collective-permute-start | bytes 811016 | tf_op jit(solution)/shard_map/ppermute | solution.py:25
  67.4 15.6 %collective-permute-start.8 = (bf16[256,256]{1,0:T(8,128)(2,1)S(1)}, bf16[256,256]{1,0:T(8,128)(2,1)S(1)}, u32[]{:S(2)}, u32[]{:S(2)}) collective-permute-start(bf16[256,256]{1,0:T(8,128)(2,1)S(1)} %get-tuple-element.45), channel_id=1, source_target_pairs={{0,1},{1,2},{2,0},{3,4},{4,5},{5,3},{6,7},{7,8},{8,6},{9,10},{10,1... | collective-permute-start | bytes 393224 | tf_op jit(solution)/shard_map/ppermute | solution.py:190
  73.3 9.7 %collective-permute-start.9 = (bf16[256,256]{1,0:T(8,128)(2,1)S(1)}, bf16[256,256]{1,0:T(8,128)(2,1)S(1)}, u32[]{:S(2)}, u32[]{:S(2)}) collective-permute-start(bf16[256,256]{1,0:T(8,128)(2,1)S(1)} %get-tuple-element.46), channel_id=1, source_target_pairs={{0,2},{1,0},{2,1},{3,5},{4,3},{5,4},{6,8},{7,6},{8,7},{9,11},{10,9... | collective-permute-start | bytes 393224 | tf_op jit(solution)/shard_map/ppermute | solution.py:190
  76.2 8.7 %collective-permute-start.6 = (bf16[256,256]{1,0:T(8,128)(2,1)}, bf16[256,256]{1,0:T(8,128)(2,1)}, u32[]{:S(2)}, u32[]{:S(2)}) collective-permute-start(bf16[256,256]{1,0:T(8,128)(2,1)} %get-tuple-element.42), channel_id=1, source_target_pairs={{0,1},{1,2},{2,0},{3,4},{4,5},{5,3},{6,7},{7,8},{8,6},{9,10},{10,1... | collective-permute-start | bytes 393224 | tf_op jit(solution)/shard_map/ppermute | solution.py:190
  80.3 7.2 %collective-permute-start.7 = (bf16[256,256]{1,0:T(8,128)(2,1)}, bf16[256,256]{1,0:T(8,128)(2,1)}, u32[]{:S(2)}, u32[]{:S(2)}) collective-permute-start(bf16[256,256]{1,0:T(8,128)(2,1)} %get-tuple-element.43), channel_id=1, source_target_pairs={{0,2},{1,0},{2,1},{3,5},{4,3},{5,4},{6,8},{7,6},{8,7},{9,11},{10,9... | collective-permute-start | bytes 393224 | tf_op jit(solution)/shard_map/ppermute | solution.py:190
  88.5 11.0 %collective-permute-start.11 = (bf16[128,256]{1,0:T(8,128)(2,1)S(1)}, bf16[128,256]{1,0:T(8,128)(2,1)S(1)}, u32[]{:S(2)}, u32[]{:S(2)}) collective-permute-start(bf16[128,256]{1,0:T(8,128)(2,1)S(1)} %get-tuple-element.54), channel_id=1, source_target_pairs={{0,3},{1,4},{2,5},{3,0},{4,1},{5,2},{6,9},{7,10},{8,11},{9,6},{10,... | collective-permute-start | bytes 196616 | tf_op jit(solution)/shard_map/ppermute | solution.py:203
  96.9 9.0 %collective-permute-start.10 = (bf16[128,256]{1,0:T(8,128)(2,1)S(1)}, bf16[128,256]{1,0:T(8,128)(2,1)S(1)}, u32[]{:S(2)}, u32[]{:S(2)}) collective-permute-start(bf16[128,256]{1,0:T(8,128)(2,1)S(1)} %get-tuple-element.49), channel_id=1, source_target_pairs={{0,3},{1,4},{2,5},{3,0},{4,1},{5,2},{6,9},{7,10},{8,11},{9,6},{10,... | collective-permute-start | bytes 196616 | tf_op jit(solution)/shard_map/ppermute | solution.py:203

commit v4 on v3

--- a/solution.py
+++ b/solution.py
@@ -65,25 +65,30 @@
     packed_ref[slots * TS :, :] = note.astype(jnp.float32).astype(jnp.bfloat16)
 
 
-def pack_right_kernel(place_ref, right_ref, rights):
-    for column in range(HELD):
-        piece = rights.at[column * PIECE : (column + 1) * PIECE]
+def pack_right_kernel(place_ref, right_ref, *pieces):
+    for column, piece in enumerate(pieces):
         for p in range(SB):
             piece[p * TS : (p + 1) * TS, :] = right_ref[column, p]
         write_note(piece, place_ref, column, SB)
 
 
-def pack_left_kernel(place_ref, left_ref, lefts, left_zero):
+def pack_left_kernel(place_ref, left_ref, right_zero, right_one, lefts, left_zero, rights):
     for column in range(HELD):
-        targets = [lefts.at[column * BLOCK : (column + 1) * BLOCK]] + [left_zero] * (column == 0)
+        targets = [part(lefts, column, BLOCK)] + [left_zero] * (column == 0)
         for target in targets:
             for q in range(SA):
                 target[q * TS : (q + 1) * TS, :] = left_ref[column, q]
             write_note(target, place_ref, column, SA)
+    rights[:PIECE, :] = right_zero[...]
+    rights[PIECE:, :] = right_one[...]
 
 
 def part(ref, column, rows):
     return ref.at[column * rows : (column + 1) * rows]
+
+
+def mark_kernel(right_one, mark):
+    mark[...] = jnp.zeros_like(mark)
 
 
 def local_kernel(lefts, rights, *refs):
@@ -93,13 +98,10 @@
         add_term(total, place_ref, part(lefts, column, BLOCK), part(rights, column, PIECE))
 
 
-def early_kernel(lefts, left_next, right_one, right_two, *refs):
-    starts, totals, place_ref = refs[:HELD], refs[HELD:-1], refs[-1]
-    for column, (start, total) in enumerate(zip(starts, totals)):
-        total[...] = start[...]
-        after = part(left_next, 0, BLOCK) if column else part(lefts, 1, BLOCK)
-        add_term(total, place_ref, after, part(right_one, column, PIECE))
-        add_term(total, place_ref, part(left_next, column, BLOCK), part(right_two, column, PIECE))
+def middle_kernel(mark, start, left_one, right_one, left_two, right_two, total, place_ref, *, column):
+    total[...] = start[...]
+    add_term(total, place_ref, part(left_one, 1 - column, BLOCK), right_one)
+    add_term(total, place_ref, part(left_two, column, BLOCK), part(right_two, column, PIECE))
 
 
 def late_kernel(layer, total_ref, left, right, *refs, block):
@@ -127,9 +129,10 @@
         out_ref[:, n * TS : (n + 1) * TS] = added.astype(out_ref.dtype)
 
 
-AHEAD = 10**10
+AHEAD = 4 * 10**10
 SMEM = pl.BlockSpec(memory_space=pltpu.SMEM)
 VMEM = pl.BlockSpec(memory_space=pltpu.VMEM)
+ANY = pl.BlockSpec(memory_space=pl.ANY)
 PARAMS = pltpu.CompilerParams(vmem_limit_bytes=32 * 1024 * 1024)
 
 
@@ -152,36 +155,46 @@
 def body(left_tiles, left_place, right_tiles, right_place):
     layer = lax.axis_index("layer").astype(jnp.int32).reshape(1)
     places = pltpu.SMEM((SA,), jnp.int32)
-    sums = [array(RT * TS, TS, jnp.float32)] * HELD
-    rights = call(pack_right_kernel, array(HELD * PIECE, TS), [SMEM, VMEM], (right_place[0, 0], right_tiles[0, 0]))
-    right_one = shifted(rights, "row", -1)
-    lefts, left_zero = call(
+    total = array(RT * TS, TS, jnp.float32)
+    pieces = call(pack_right_kernel, [array(PIECE, TS)] * HELD, [SMEM, VMEM], (right_place[0, 0], right_tiles[0, 0]))
+    right_one = [shifted(piece, "row", -1) for piece in pieces]
+    lefts, left_zero, rights = call(
         pack_left_kernel,
-        [array(HELD * BLOCK, TS), array(BLOCK, TS)],
-        [SMEM, VMEM],
-        (left_place[0, 0], left_tiles[0, 0]),
+        [array(HELD * BLOCK, TS), array(BLOCK, TS), array(HELD * PIECE, TS)],
+        [SMEM] + [VMEM] * 3,
+        (left_place[0, 0], left_tiles[0, 0], *pieces),
     )
     right_two = shifted(rights, "row", -2)
     left_next = shifted(lefts, "col", -1)
     left_last = shifted(left_zero, "col", -2)
-    right_one, own = lax.optimization_barrier((right_one, rights))
-    totals = call(local_kernel, sums, [VMEM] * 2, (lefts, own), [places], cost=AHEAD)
-    totals = call(early_kernel, sums, [VMEM] * (4 + HELD), (lefts, left_next, right_one, right_two, *totals), [places])
-    right_three = [shifted(right_one[j * PIECE : (j + 1) * PIECE], "row", -2) for j in range(HELD)]
-    held = [(left_next, 1), (left_last, 0)]
+    totals = list(call(local_kernel, [total] * HELD, [VMEM] * 2, (lefts, rights), [places]))
+    right_one[0], totals = lax.optimization_barrier((right_one[0], totals))
+    mark = call(mark_kernel, array(8, 128, jnp.float32), [ANY], (right_one[1],), cost=AHEAD)
+    right_two, left_next, left_last, mark = lax.optimization_barrier((right_two, left_next, left_last, mark))
+    right_three = [shifted(piece, "row", -2) for piece in right_one]
+    ones, held = (lefts, left_next), ((left_next, 1), (left_last, 0))
     trio = [[(p, p // TRIO * TRIO + (p + turn) % TRIO) for p in range(2 * TRIO)] for turn in range(TRIO)]
     across = [(p, (p + TRIO) % (2 * TRIO)) for p in range(2 * TRIO)]
     shares = []
     for j in range(HELD):
         if j:
-            right_three[j], shares[j - 1] = lax.optimization_barrier((right_three[j], shares[j - 1]))
+            totals[j], shares[j - 1] = lax.optimization_barrier((totals[j], shares[j - 1]))
         left, block = held[j]
+        start = call(
+            functools.partial(middle_kernel, column=j),
+            total,
+            [ANY] + [VMEM] * 5,
+            (mark, totals[j], ones[j], right_one[j], left_next, right_two),
+            [places],
+        )
+        if j:
+            right_three[j], start = lax.optimization_barrier((right_three[j], start))
         shares.append(
             call(
                 functools.partial(late_kernel, block=block),
                 [array(2 * SHARE, TS)] * TRIO,
                 [SMEM] + [VMEM] * 3,
-                (layer, totals[j], left, right_three[j]),
+                (layer, start, left, right_three[j]),
                 [pltpu.VMEM((RT * TS, TS), jnp.float32), places],
             )
         )

time: 108 us -> 108 us (level)
  the two profiles are of different devices: /device:TPU:56 before, /device:TPU:128 now
where the time goes in v4:
time: 108 us
  starting transfers between devices  57.6 us (53%)
  waiting for transfers between devices  30.2 us (28%)
  Pallas kernels  13.9 us (13%)
  local copies, waits for them, and re-layouts  5.58 us (5%)
    ppermute x7, starting transfers between devices, shifted(): lax.ppermute(block, axis, [((i - distance) % size, i) for i in range(size)])  32.3 us
    ppermute x7, waiting for transfers between devices, shifted(): lax.ppermute(block, axis, [((i - distance) % size, i) for i in range(size)])  18.9 us
    pallas_call x11, Pallas kernels, call(): pl.pallas_call(kernel, out_shape=out_shape, in_specs=in_specs, out_specs=...  13.9 us
    ppermute x2, starting transfers between devices, body(): ends.insert(2 * j + 1, lax.ppermute(far, 'layer', across))  12.7 us
    ppermute x4, starting transfers between devices, body(): lax.ppermute(share, 'layer', trio[turn])  12.6 us
    ppermute x2, waiting for transfers between devices, body(): ends.insert(2 * j + 1, lax.ppermute(far, 'layer', across))  7.24 us
    unnamed x16, local copies, waits for them, and re-layouts  5.58 us
    ppermute x4, waiting for transfers between devices, body(): lax.ppermute(share, 'layer', trio[turn])  4.07 us
  transfers between devices with their start and end apart: 13, of which 6 were waited for; matrix products, arithmetic and copies ran while one was open for 0% of the time, Pallas kernels for 10%

profile of v4, /device:TPU:128, one launch (start us, length us, event | category | flops | bytes accessed | tf_op | source)
XLA Modules:
  0.0 107.6 jit_solution(2259985739623012802)
XLA Ops:
  0.0 0.0 copy-start.5
  0.0 1.0 copy-done.5
  1.0 0.0 copy-start.6
  1.0 0.7 copy-done.6
  1.7 1.4 %shard_map.46 = (bf16[528,256]{1,0:T(8,128)(2,1)}, bf16[528,256]{1,0:T(8,128)(2,1)}) custom-call(s32[2,2]{1,0:T(2,128)S(1)} %bitcast.7, bf16[2,2,256,256]{3,2,1,0:T(8,128)(2,1)S(1)} %bitcast.6), custom_call_target="tpu_custom_call" | custom-call | tf_op jit(solution)/shard_map/pallas_call | solution.py:140
  3.1 15.6 %collective-permute-start.5 = (bf16[528,256]{1,0:T(8,128)(2,1)}, bf16[528,256]{1,0:T(8,128)(2,1)}, u32[]{:S(2)}, u32[]{:S(2)}) collective-permute-start(bf16[528,256]{1,0:T(8,128)(2,1)} %get-tuple-element.39.right_zero), channel_id=1, source_target_pairs={{48,0},{96,48},{144,96},{192,144},{240,192},{288,240},{336,288},{3... | collective-permute-start | bytes 811016 | tf_op jit(solution)/shard_map/ppermute | solution.py:25
  18.8 1.9 %collective-permute-start = (bf16[528,256]{1,0:T(8,128)(2,1)}, bf16[528,256]{1,0:T(8,128)(2,1)S(1)}, u32[]{:S(2)}, u32[]{:S(2)}) collective-permute-start(bf16[528,256]{1,0:T(8,128)(2,1)} %get-tuple-element.38.right_one), channel_id=1, source_target_pairs={{48,0},{96,48},{144,96},{192,144},{240,192},{288,240},{336,288},{3... | collective-permute-start | bytes 811016 | tf_op jit(solution)/shard_map/ppermute | solution.py:25
  20.7 0.0 copy-start
  20.7 1.4 %copy-done = bf16[1,1,2,6,256,256]{5,4,3,2,1,0:T(8,128)(2,1)S(1)} copy-done((bf16[1,1,2,6,256,256]{5,4,3,2,1,0:T(8,128)(2,1)S(1)}, bf16[1,1,2,6,256,256]{5,4,3,2,1,0:T(8,128)(2,1)}, u32[]{:S(2)}) %copy-start) | copy-done | bytes 1572888
  22.1 0.0 copy-start.7
  22.1 0.7 copy-done.7
  22.8 2.2 %shard_map.47 = (bf16[3104,256]{1,0:T(8,128)(2,1)S(1)}, bf16[1552,256]{1,0:T(8,128)(2,1)}, bf16[1056,256]{1,0:T(8,128)(2,1)}) custom-call(s32[2,6]{1,0:T(2,128)S(1)} %bitcast.8, bf16[2,6,256,256]{3,2,1,0:T(8,128)(2,1)S(1)} %bitcast.5, bf16[528,256]{1,0:T(8,128)(2,1)} %get-tuple-element.39.right_zero, bf16[528,256]{1,0:T(8,128)(2,1)} %get-tuple-element.38.right_one), custom_call_target="tpu_custom_call" | custom-call | tf_op jit(solution)/shard_map/pallas_call | solution.py:140
  25.0 1.9 %collective-permute-start.3 = (bf16[3104,256]{1,0:T(8,128)(2,1)S(1)}, bf16[3104,256]{1,0:T(8,128)(2,1)S(1)}, u32[]{:S(2)}, u32[]{:S(2)}) collective-permute-start(bf16[3104,256]{1,0:T(8,128)(2,1)S(1)} %get-tuple-element.41.lefts.left_one), channel_id=1, source_target_pairs={{6,0},{12,6},{18,12},{24,18},{30,24},{36,30},{42,36},{0,42},{7,1},... | collective-permute-start | bytes 4767752 | tf_op jit(solution)/shard_map/ppermute | solution.py:25
  26.9 3.2 %collective-permute-start.2 = (bf16[1056,256]{1,0:T(8,128)(2,1)}, bf16[1056,256]{1,0:T(8,128)(2,1)}, u32[]{:S(2)}, u32[]{:S(2)}) collective-permute-start(bf16[1056,256]{1,0:T(8,128)(2,1)} %get-tuple-element.40.rights), channel_id=1, source_target_pairs={{96,0},{144,48},{192,96},{240,144},{288,192},{336,240},{384,288},{... | collective-permute-start | bytes 1622024 | tf_op jit(solution)/shard_map/ppermute | solution.py:25
  30.2 2.8 %collective-permute-start.4 = (bf16[1552,256]{1,0:T(8,128)(2,1)}, bf16[1552,256]{1,0:T(8,128)(2,1)}, u32[]{:S(2)}, u32[]{:S(2)}) collective-permute-start(bf16[1552,256]{1,0:T(8,128)(2,1)} %get-tuple-element.42), channel_id=1, source_target_pairs={{12,0},{18,6},{24,12},{30,18},{36,24},{42,30},{0,36},{6,42},{13,1}... | collective-permute-start | bytes 2383880 | tf_op jit(solution)/shard_map/ppermute | solution.py:25
  32.9 1.7 %shard_map.49 = (f32[768,256]{1,0:T(8,128)S(1)}, f32[768,256]{1,0:T(8,128)S(1)}) custom-call(bf16[3104,256]{1,0:T(8,128)(2,1)S(1)} %get-tuple-element.41.lefts.left_one, bf16[1056,256]{1,0:T(8,128)(2,1)} %get-tuple-element.40.rights), custom_call_target="tpu_custom_call" | custom-call | tf_op jit(solution)/shard_map/pallas_call | solution.py:140
  34.6 0.0 copy-start.1
  34.6 0.9 copy-done.1
  35.5 0.0 copy-start.3
  35.5 0.9 copy-done.3
  36.4 0.0 collective-permute-done.5.right_one
  36.4 0.0 copy-start.4
  36.4 3.6 %collective-permute-start.6 = (bf16[528,256]{1,0:T(8,128)(2,1)}, bf16[528,256]{1,0:T(8,128)(2,1)S(1)}, u32[]{:S(2)}, u32[]{:S(2)}) collective-permute-start(bf16[528,256]{1,0:T(8,128)(2,1)} %collective-permute-done.5.right_one), channel_id=1, source_target_pairs={{96,0},{144,48},{192,96},{240,144},{288,192},{336,240},{384,288},{... | collective-permute-start | bytes 811016 | tf_op jit(solution)/shard_map/ppermute | solution.py:25
  40.0 2.3 %collective-permute-done.right_one = bf16[528,256]{1,0:T(8,128)(2,1)S(1)} collective-permute-done((bf16[528,256]{1,0:T(8,128)(2,1)}, bf16[528,256]{1,0:T(8,128)(2,1)S(1)}, u32[]{:S(2)}, u32[]{:S(2)}) %collective-permute-start) | collective-permute-done | bytes 270368 | tf_op jit(solution)/shard_map/ppermute | solution.py:25
  42.3 3.3 %collective-permute-start.1 = (bf16[528,256]{1,0:T(8,128)(2,1)S(1)}, bf16[528,256]{1,0:T(8,128)(2,1)S(1)}, u32[]{:S(2)}, u32[]{:S(2)}) collective-permute-start(bf16[528,256]{1,0:T(8,128)(2,1)S(1)} %collective-permute-done.right_one), channel_id=1, source_target_pairs={{96,0},{144,48},{192,96},{240,144},{288,192},{336,240},{384,288},{... | collective-permute-start | bytes 811016 | tf_op jit(solution)/shard_map/ppermute | solution.py:25
  45.6 0.0 collective-permute-done.2.right_two
  45.6 16.5 %collective-permute-done.4.left = bf16[1552,256]{1,0:T(8,128)(2,1)} collective-permute-done((bf16[1552,256]{1,0:T(8,128)(2,1)}, bf16[1552,256]{1,0:T(8,128)(2,1)}, u32[]{:S(2)}, u32[]{:S(2)}) %collective-permute-start.4) | collective-permute-done | bytes 794656 | tf_op jit(solution)/shard_map/ppermute | solution.py:25
  62.2 0.0 collective-permute-done.3.left_two.left.left_one
  62.2 0.0 copy-done.4
  62.2 2.0 %shard_map.50.total_ref = f32[768,256]{1,0:T(8,128)S(1)} custom-call(f32[8,128]{1,0:T(8,128)S(1)} %shard_map.48.mark, f32[768,256]{1,0:T(8,128)S(1)} %copy-done.4, bf16[3104,256]{1,0:T(8,128)(2,1)S(1)} %get-tuple-element.41.lefts.left_one, bf16[528,256]{1,0:T(8,128)(2,1)} %collective-permute-done.5.right_one, ...), custom_call_target="tpu_custom_call" | custom-call | tf_op jit(solution)/shard_map/pallas_call | solution.py:140
  64.2 0.0 copy-start.2
  64.2 0.0 collective-permute-done.6.right
  64.2 0.5 shard_map.51
  64.7 3.4 %collective-permute-start.10 = (bf16[256,256]{1,0:T(8,128)(2,1)S(1)}, bf16[256,256]{1,0:T(8,128)(2,1)S(1)}, u32[]{:S(2)}, u32[]{:S(2)}) collective-permute-start(bf16[256,256]{1,0:T(8,128)(2,1)S(1)} %get-tuple-element.62), channel_id=1, source_target_pairs={{0,2},{1,0},{2,1},{3,5},{4,3},{5,4},{6,8},{7,6},{8,7},{9,11},{10,9... | collective-permute-start | bytes 393224 | tf_op jit(solution)/shard_map/ppermute | solution.py:203
  68.1 3.3 %collective-permute-start.9 = (bf16[256,256]{1,0:T(8,128)(2,1)S(1)}, bf16[256,256]{1,0:T(8,128)(2,1)S(1)}, u32[]{:S(2)}, u32[]{:S(2)}) collective-permute-start(bf16[256,256]{1,0:T(8,128)(2,1)S(1)} %get-tuple-element.61), channel_id=1, source_target_pairs={{0,1},{1,2},{2,0},{3,4},{4,5},{5,3},{6,7},{7,8},{8,6},{9,10},{10,1... | collective-permute-start | bytes 393224 | tf_op jit(solution)/shard_map/ppermute | solution.py:203
  71.4 0.0 copy-done.2
  71.4 2.3 %shard_map.52.total_ref = f32[768,256]{1,0:T(8,128)S(1)} custom-call(f32[8,128]{1,0:T(8,128)S(1)} %shard_map.48.mark, f32[768,256]{1,0:T(8,128)S(1)} %copy-done.2, bf16[3104,256]{1,0:T(8,128)(2,1)S(1)} %collective-permute-done.3.left_two.left.left_one, bf16[528,256]{1,0:T(8,128)(2,1)S(1)} %collective-permute-done.right_one, ...), custom_call_target="tpu_custom_call" | custom-call | tf_op jit(solution)/shard_map/pallas_call | solution.py:140
  73.7 0.0 collective-permute-done.1.right
  73.7 2.2 %shard_map.53 = (bf16[256,256]{1,0:T(8,128)(2,1)S(1)}, bf16[256,256]{1,0:T(8,128)(2,1)}, bf16[256,256]{1,0:T(8,128)(2,1)}) custom-call(s32[1]{0:T(128)} %bitcast.layer, f32[768,256]{1,0:T(8,128)S(1)} %shard_map.52.total_ref, bf16[1552,256]{1,0:T(8,128)(2,1)} %collective-permute-done.4.left, bf16[528,256]{1,0:T(8,128)(2,1)S(1)} %collective-permute-done.1.right), custom_call_target="tpu_custom_call" | custom-call | tf_op jit(solution)/shard_map/pallas_call | solution.py:140
  75.9 1.9 %collective-permute-start.7 = (bf16[256,256]{1,0:T(8,128)(2,1)}, bf16[256,256]{1,0:T(8,128)(2,1)}, u32[]{:S(2)}, u32[]{:S(2)}) collective-permute-start(bf16[256,256]{1,0:T(8,128)(2,1)} %get-tuple-element.58), channel_id=1, source_target_pairs={{0,1},{1,2},{2,0},{3,4},{4,5},{5,3},{6,7},{7,8},{8,6},{9,10},{10,1... | collective-permute-start | bytes 393224 | tf_op jit(solution)/shard_map/ppermute | solution.py:203
  77.8 3.9 %collective-permute-start.8 = (bf16[256,256]{1,0:T(8,128)(2,1)}, bf16[256,256]{1,0:T(8,128)(2,1)}, u32[]{:S(2)}, u32[]{:S(2)}) collective-permute-start(bf16[256,256]{1,0:T(8,128)(2,1)} %get-tuple-element.59), channel_id=1, source_target_pairs={{0,2},{1,0},{2,1},{3,5},{4,3},{5,4},{6,8},{7,6},{8,7},{9,11},{10,9... | collective-permute-start | bytes 393224 | tf_op jit(solution)/shard_map/ppermute | solution.py:203
  81.8 0.0 collective-permute-done.10.two
  81.8 0.0 collective-permute-done.9.one
  81.8 0.1 shard_map.54
  81.8 1.2 %collective-permute-done.7.one = bf16[256,256]{1,0:T(8,128)(2,1)} collective-permute-done((bf16[256,256]{1,0:T(8,128)(2,1)}, bf16[256,256]{1,0:T(8,128)(2,1)}, u32[]{:S(2)}, u32[]{:S(2)}) %collective-permute-start.7) | collective-permute-done | bytes 131104 | tf_op jit(solution)/shard_map/ppermute | solution.py:203
  83.1 2.8 %collective-permute-done.8.two = bf16[256,256]{1,0:T(8,128)(2,1)} collective-permute-done((bf16[256,256]{1,0:T(8,128)(2,1)}, bf16[256,256]{1,0:T(8,128)(2,1)}, u32[]{:S(2)}, u32[]{:S(2)}) %collective-permute-start.8) | collective-permute-done | bytes 131104 | tf_op jit(solution)/shard_map/ppermute | solution.py:203
  85.9 1.0 shard_map.55
  86.9 10.8 %collective-permute-start.12 = (bf16[128,256]{1,0:T(8,128)(2,1)S(1)}, bf16[128,256]{1,0:T(8,128)(2,1)S(1)}, u32[]{:S(2)}, u32[]{:S(2)}) collective-permute-start(bf16[128,256]{1,0:T(8,128)(2,1)S(1)} %get-tuple-element.70), channel_id=1, source_target_pairs={{0,3},{1,4},{2,5},{3,0},{4,1},{5,2},{6,9},{7,10},{8,11},{9,6},{10,... | collective-permute-start | bytes 196616 | tf_op jit(solution)/shard_map/ppermute | solution.py:216
  97.7 1.9 %collective-permute-start.11 = (bf16[128,256]{1,0:T(8,128)(2,1)S(1)}, bf16[128,256]{1,0:T(8,128)(2,1)S(1)}, u32[]{:S(2)}, u32[]{:S(2)}) collective-permute-start(bf16[128,256]{1,0:T(8,128)(2,1)S(1)} %get-tuple-element.65), channel_id=1, source_target_pairs={{0,3},{1,4},{2,5},{3,0},{4,1},{5,2},{6,9},{7,10},{8,11},{9,6},{10,... | collective-permute-start | bytes 196616 | tf_op jit(solution)/shard_map/ppermute | solution.py:216
  99.6 0.3 collective-permute-done.12.refs_3_
  99.9 6.9 %collective-permute-done.11.refs_1_ = bf16[128,256]{1,0:T(8,128)(2,1)S(1)} collective-permute-done((bf16[128,256]{1,0:T(8,128)(2,1)S(1)}, bf16[128,256]{1,0:T(8,128)(2,1)S(1)}, u32[]{:S(2)}, u32[]{:S(2)}) %collective-permute-start.11) | collective-permute-done | bytes 65568 | tf_op jit(solution)/shard_map/ppermute | solution.py:216
  106.9 0.7 shard_map.56
  (1 shorter events, 0.0 us)
Async XLA Ops:
  0.0 1.0 copy-start.5
  1.0 0.7 copy-start.6
  3.1 33.3 %collective-permute-start.5 = (bf16[528,256]{1,0:T(8,128)(2,1)}, bf16[528,256]{1,0:T(8,128)(2,1)}, u32[]{:S(2)}, u32[]{:S(2)}) collective-permute-start(bf16[528,256]{1,0:T(8,128)(2,1)} %get-tuple-element.39.right_zero), channel_id=1, source_target_pairs={{48,0},{96,48},{144,96},{192,144},{240,192},{288,240},{336,288},{3... | collective-permute-start | bytes 811016 | tf_op jit(solution)/shard_map/ppermute | solution.py:25
  18.8 23.5 %collective-permute-start = (bf16[528,256]{1,0:T(8,128)(2,1)}, bf16[528,256]{1,0:T(8,128)(2,1)S(1)}, u32[]{:S(2)}, u32[]{:S(2)}) collective-permute-start(bf16[528,256]{1,0:T(8,128)(2,1)} %get-tuple-element.38.right_one), channel_id=1, source_target_pairs={{48,0},{96,48},{144,96},{192,144},{240,192},{288,240},{336,288},{3... | collective-permute-start | bytes 811016 | tf_op jit(solution)/shard_map/ppermute | solution.py:25
  20.7 1.4 %copy-start = (bf16[1,1,2,6,256,256]{5,4,3,2,1,0:T(8,128)(2,1)S(1)}, bf16[1,1,2,6,256,256]{5,4,3,2,1,0:T(8,128)(2,1)}, u32[]{:S(2)}) copy-start(bf16[1,1,2,6,256,256]{5,4,3,2,1,0:T(8,128)(2,1)} %param.4) | copy-start | bytes 4718596
  22.1 0.7 copy-start.7
  25.0 37.2 %collective-permute-start.3 = (bf16[3104,256]{1,0:T(8,128)(2,1)S(1)}, bf16[3104,256]{1,0:T(8,128)(2,1)S(1)}, u32[]{:S(2)}, u32[]{:S(2)}) collective-permute-start(bf16[3104,256]{1,0:T(8,128)(2,1)S(1)} %get-tuple-element.41.lefts.left_one), channel_id=1, source_target_pairs={{6,0},{12,6},{18,12},{24,18},{30,24},{36,30},{42,36},{0,42},{7,1},... | collective-permute-start | bytes 4767752 | tf_op jit(solution)/shard_map/ppermute | solution.py:25
  26.9 18.7 %collective-permute-start.2 = (bf16[1056,256]{1,0:T(8,128)(2,1)}, bf16[1056,256]{1,0:T(8,128)(2,1)}, u32[]{:S(2)}, u32[]{:S(2)}) collective-permute-start(bf16[1056,256]{1,0:T(8,128)(2,1)} %get-tuple-element.40.rights), channel_id=1, source_target_pairs={{96,0},{144,48},{192,96},{240,144},{288,192},{336,240},{384,288},{... | collective-permute-start | bytes 1622024 | tf_op jit(solution)/shard_map/ppermute | solution.py:25
  30.2 32.0 %collective-permute-start.4 = (bf16[1552,256]{1,0:T(8,128)(2,1)}, bf16[1552,256]{1,0:T(8,128)(2,1)}, u32[]{:S(2)}, u32[]{:S(2)}) collective-permute-start(bf16[1552,256]{1,0:T(8,128)(2,1)} %get-tuple-element.42), channel_id=1, source_target_pairs={{12,0},{18,6},{24,12},{30,18},{36,24},{42,30},{0,36},{6,42},{13,1}... | collective-permute-start | bytes 2383880 | tf_op jit(solution)/shard_map/ppermute | solution.py:25
  34.6 0.9 copy-start.1
  35.5 0.9 copy-start.3
  36.4 25.8 %copy-start.4 = (f32[768,256]{1,0:T(8,128)S(1)}, f32[768,256]{1,0:T(8,128)}, u32[]{:S(2)}) copy-start(f32[768,256]{1,0:T(8,128)} %copy-done.3) | copy-start | bytes 2359300
  36.4 27.8 %collective-permute-start.6 = (bf16[528,256]{1,0:T(8,128)(2,1)}, bf16[528,256]{1,0:T(8,128)(2,1)S(1)}, u32[]{:S(2)}, u32[]{:S(2)}) collective-permute-start(bf16[528,256]{1,0:T(8,128)(2,1)} %collective-permute-done.5.right_one), channel_id=1, source_target_pairs={{96,0},{144,48},{192,96},{240,144},{288,192},{336,240},{384,288},{... | collective-permute-start | bytes 811016 | tf_op jit(solution)/shard_map/ppermute | solution.py:25
  42.3 31.4 %collective-permute-start.1 = (bf16[528,256]{1,0:T(8,128)(2,1)S(1)}, bf16[528,256]{1,0:T(8,128)(2,1)S(1)}, u32[]{:S(2)}, u32[]{:S(2)}) collective-permute-start(bf16[528,256]{1,0:T(8,128)(2,1)S(1)} %collective-permute-done.right_one), channel_id=1, source_target_pairs={{96,0},{144,48},{192,96},{240,144},{288,192},{336,240},{384,288},{... | collective-permute-start | bytes 811016 | tf_op jit(solution)/shard_map/ppermute | solution.py:25
  64.2 7.3 %copy-start.2 = (f32[768,256]{1,0:T(8,128)S(1)}, f32[768,256]{1,0:T(8,128)}, u32[]{:S(2)}) copy-start(f32[768,256]{1,0:T(8,128)} %copy-done.1) | copy-start | bytes 2359300
  64.7 17.1 %collective-permute-start.10 = (bf16[256,256]{1,0:T(8,128)(2,1)S(1)}, bf16[256,256]{1,0:T(8,128)(2,1)S(1)}, u32[]{:S(2)}, u32[]{:S(2)}) collective-permute-start(bf16[256,256]{1,0:T(8,128)(2,1)S(1)} %get-tuple-element.62), channel_id=1, source_target_pairs={{0,2},{1,0},{2,1},{3,5},{4,3},{5,4},{6,8},{7,6},{8,7},{9,11},{10,9... | collective-permute-start | bytes 393224 | tf_op jit(solution)/shard_map/ppermute | solution.py:203
  68.1 13.6 %collective-permute-start.9 = (bf16[256,256]{1,0:T(8,128)(2,1)S(1)}, bf16[256,256]{1,0:T(8,128)(2,1)S(1)}, u32[]{:S(2)}, u32[]{:S(2)}) collective-permute-start(bf16[256,256]{1,0:T(8,128)(2,1)S(1)} %get-tuple-element.61), channel_id=1, source_target_pairs={{0,1},{1,2},{2,0},{3,4},{4,5},{5,3},{6,7},{7,8},{8,6},{9,10},{10,1... | collective-permute-start | bytes 393224 | tf_op jit(solution)/shard_map/ppermute | solution.py:203
  75.9 7.2 %collective-permute-start.7 = (bf16[256,256]{1,0:T(8,128)(2,1)}, bf16[256,256]{1,0:T(8,128)(2,1)}, u32[]{:S(2)}, u32[]{:S(2)}) collective-permute-start(bf16[256,256]{1,0:T(8,128)(2,1)} %get-tuple-element.58), channel_id=1, source_target_pairs={{0,1},{1,2},{2,0},{3,4},{4,5},{5,3},{6,7},{7,8},{8,6},{9,10},{10,1... | collective-permute-start | bytes 393224 | tf_op jit(solution)/shard_map/ppermute | solution.py:203
  77.8 8.1 %collective-permute-start.8 = (bf16[256,256]{1,0:T(8,128)(2,1)}, bf16[256,256]{1,0:T(8,128)(2,1)}, u32[]{:S(2)}, u32[]{:S(2)}) collective-permute-start(bf16[256,256]{1,0:T(8,128)(2,1)} %get-tuple-element.59), channel_id=1, source_target_pairs={{0,2},{1,0},{2,1},{3,5},{4,3},{5,4},{6,8},{7,6},{8,7},{9,11},{10,9... | collective-permute-start | bytes 393224 | tf_op jit(solution)/shard_map/ppermute | solution.py:203
  86.9 13.0 %collective-permute-start.12 = (bf16[128,256]{1,0:T(8,128)(2,1)S(1)}, bf16[128,256]{1,0:T(8,128)(2,1)S(1)}, u32[]{:S(2)}, u32[]{:S(2)}) collective-permute-start(bf16[128,256]{1,0:T(8,128)(2,1)S(1)} %get-tuple-element.70), channel_id=1, source_target_pairs={{0,3},{1,4},{2,5},{3,0},{4,1},{5,2},{6,9},{7,10},{8,11},{9,6},{10,... | collective-permute-start | bytes 196616 | tf_op jit(solution)/shard_map/ppermute | solution.py:216
  97.7 9.2 %collective-permute-start.11 = (bf16[128,256]{1,0:T(8,128)(2,1)S(1)}, bf16[128,256]{1,0:T(8,128)(2,1)S(1)}, u32[]{:S(2)}, u32[]{:S(2)}) collective-permute-start(bf16[128,256]{1,0:T(8,128)(2,1)S(1)} %get-tuple-element.65), channel_id=1, source_target_pairs={{0,3},{1,4},{2,5},{3,0},{4,1},{5,2},{6,9},{7,10},{8,11},{9,6},{10,... | collective-permute-start | bytes 196616 | tf_op jit(solution)/shard_map/ppermute | solution.py:216

commit v5 on v4

--- a/solution.py
+++ b/solution.py
@@ -65,22 +65,35 @@
     packed_ref[slots * TS :, :] = note.astype(jnp.float32).astype(jnp.bfloat16)
 
 
-def pack_right_kernel(place_ref, right_ref, *pieces):
-    for column, piece in enumerate(pieces):
-        for p in range(SB):
-            piece[p * TS : (p + 1) * TS, :] = right_ref[column, p]
-        write_note(piece, place_ref, column, SB)
-
-
-def pack_left_kernel(place_ref, left_ref, right_zero, right_one, lefts, left_zero, rights):
+def pack(copies, place_ref, notes, sem):
+    copies = [pltpu.make_async_copy(source, target, sem.at[n]) for n, (source, target) in enumerate(copies)]
+    for copy in copies:
+        copy.start()
+    for packed, column, slots in notes:
+        write_note(packed, place_ref, column, slots)
+    for copy in copies:
+        copy.wait()
+
+
+def pack_right_kernel(place_ref, right_ref, *refs):
+    pieces, sem = refs[:-1], refs[-1]
+    copies = [
+        (right_ref.at[column, p], piece.at[p * TS : (p + 1) * TS]) for column, piece in enumerate(pieces) for p in range(SB)
+    ]
+    pack(copies, place_ref, [(piece, column, SB) for column, piece in enumerate(pieces)], sem)
+
+
+def pack_left_kernel(right_place, left_place, right_ref, left_ref, lefts, left_zero, rights, sem):
+    copies = []
     for column in range(HELD):
-        targets = [part(lefts, column, BLOCK)] + [left_zero] * (column == 0)
-        for target in targets:
-            for q in range(SA):
-                target[q * TS : (q + 1) * TS, :] = left_ref[column, q]
-            write_note(target, place_ref, column, SA)
-    rights[:PIECE, :] = right_zero[...]
-    rights[PIECE:, :] = right_one[...]
+        for target in [part(lefts, column, BLOCK)] + [left_zero] * (column == 0):
+            copies += [(left_ref.at[column, q], target.at[q * TS : (q + 1) * TS]) for q in range(SA)]
+        target = part(rights, column, PIECE)
+        copies += [(right_ref.at[column, p], target.at[p * TS : (p + 1) * TS]) for p in range(SB)]
+    notes = [(part(lefts, column, BLOCK), column, SA) for column in range(HELD)] + [(left_zero, 0, SA)]
+    pack(copies, left_place, notes, sem)
+    for column in range(HELD):
+        write_note(part(rights, column, PIECE), right_place, column, SB)
 
 
 def part(ref, column, rows):
@@ -116,24 +129,30 @@
             share[n * SHARE : (n + 1) * SHARE, :] = total[rows, :].astype(share.dtype)
 
 
-def gather_kernel(own, one, two, near, far):
-    added = own[...].astype(jnp.float32) + one[...].astype(jnp.float32) + two[...].astype(jnp.float32)
-    near[...] = added[:SHARE]
-    far[...] = added[SHARE:].astype(far.dtype)
-
-
-def final_kernel(*refs):
-    out_ref = refs[-1]
-    for n in range(HELD):
-        added = refs[2 * n][...] + refs[2 * n + 1][...].astype(jnp.float32)
-        out_ref[:, n * TS : (n + 1) * TS] = added.astype(out_ref.dtype)
+def add_trio(own, one, two):
+    return own[...].astype(jnp.float32) + one[...].astype(jnp.float32) + two[...].astype(jnp.float32)
+
+
+def gather_kernel(own, one, two, added):
+    added[...] = add_trio(own, one, two)
+
+
+def join_kernel(first, own, one, two, near, far):
+    for column, added in enumerate((first[...], add_trio(own, one, two))):
+        near[:, column * TS : (column + 1) * TS] = added[:SHARE]
+        far[:, column * TS : (column + 1) * TS] = added[SHARE:].astype(far.dtype)
+
+
+def final_kernel(near, far, out_ref):
+    out_ref[...] = (near[...] + far[...].astype(jnp.float32)).astype(out_ref.dtype)
 
 
 AHEAD = 4 * 10**10
 SMEM = pl.BlockSpec(memory_space=pltpu.SMEM)
 VMEM = pl.BlockSpec(memory_space=pltpu.VMEM)
 ANY = pl.BlockSpec(memory_space=pl.ANY)
-PARAMS = pltpu.CompilerParams(vmem_limit_bytes=32 * 1024 * 1024)
+HBM = pl.BlockSpec(memory_space=pltpu.HBM)
+PARAMS = pltpu.CompilerParams(vmem_limit_bytes=8 * 1024 * 1024)
 
 
 def call(kernel, out_shape, in_specs, operands, scratch=(), cost=0):
@@ -156,13 +175,22 @@
     layer = lax.axis_index("layer").astype(jnp.int32).reshape(1)
     places = pltpu.SMEM((SA,), jnp.int32)
     total = array(RT * TS, TS, jnp.float32)
-    pieces = call(pack_right_kernel, [array(PIECE, TS)] * HELD, [SMEM, VMEM], (right_place[0, 0], right_tiles[0, 0]))
+    right_at, right = right_place[0, 0], right_tiles[0, 0]
+    pieces = call(
+        pack_right_kernel,
+        [array(PIECE, TS)] * HELD,
+        [SMEM, HBM],
+        (right_at, right),
+        [pltpu.SemaphoreType.DMA((HELD * SB,))],
+    )
     right_one = [shifted(piece, "row", -1) for piece in pieces]
+    left_at, left, right_at, right, pieces = lax.optimization_barrier((left_place[0, 0], left_tiles[0, 0], right_at, right, pieces))
     lefts, left_zero, rights = call(
         pack_left_kernel,
         [array(HELD * BLOCK, TS), array(BLOCK, TS), array(HELD * PIECE, TS)],
-        [SMEM] + [VMEM] * 3,
-        (left_place[0, 0], left_tiles[0, 0], *pieces),
+        [SMEM] * 2 + [HBM] * 2,
+        (right_at, left_at, right, left),
+        [pltpu.SemaphoreType.DMA((HELD * (SA + SB) + SA,))],
     )
     right_two = shifted(rights, "row", -2)
     left_next = shifted(lefts, "col", -1)
@@ -170,7 +198,7 @@
     totals = list(call(local_kernel, [total] * HELD, [VMEM] * 2, (lefts, rights), [places]))
     right_one[0], totals = lax.optimization_barrier((right_one[0], totals))
     mark = call(mark_kernel, array(8, 128, jnp.float32), [ANY], (right_one[1],), cost=AHEAD)
-    right_two, left_next, left_last, mark = lax.optimization_barrier((right_two, left_next, left_last, mark))
+    right_two, left_next, mark = lax.optimization_barrier((right_two, left_next, mark))
     right_three = [shifted(piece, "row", -2) for piece in right_one]
     ones, held = (lefts, left_next), ((left_next, 1), (left_last, 0))
     trio = [[(p, p // TRIO * TRIO + (p + turn) % TRIO) for p in range(2 * TRIO)] for turn in range(TRIO)]
@@ -198,23 +226,18 @@
                 [pltpu.VMEM((RT * TS, TS), jnp.float32), places],
             )
         )
-    ends = []
-    for j, (own_share, *others) in enumerate(shares):
-        arrived = [lax.ppermute(share, "layer", trio[turn]) for turn, share in enumerate(others, 1)]
-        if j:
-            arrived, ends = lax.optimization_barrier((arrived, ends))
-        near, far = call(
-            gather_kernel,
-            [array(SHARE, TS, jnp.float32), array(SHARE, TS)],
-            [VMEM] * TRIO,
-            (own_share, *arrived),
-            cost=(1 - j) * 10**12,
-        )
-        ends.append(near)
-        shares[j] = far
-    for j, far in enumerate(shares):
-        ends.insert(2 * j + 1, lax.ppermute(far, "layer", across))
-    return call(final_kernel, array(SHARE, HELD * TS), [VMEM] * len(ends), ends)
+    arrived = [
+        [own] + [lax.ppermute(share, "layer", trio[turn]) for turn, share in enumerate(others, 1)] for own, *others in shares
+    ]
+    first = call(gather_kernel, array(2 * SHARE, TS, jnp.float32), [VMEM] * TRIO, arrived[0], cost=10**12)
+    first, *second = lax.optimization_barrier((first, *arrived[1]))
+    near, far = call(
+        join_kernel,
+        [array(SHARE, HELD * TS, jnp.float32), array(SHARE, HELD * TS)],
+        [VMEM] * (1 + TRIO),
+        (first, *second),
+    )
+    return call(final_kernel, array(SHARE, HELD * TS), [VMEM] * 2, (near, lax.ppermute(far, "layer", across)))
 
 
 def solution(mesh):

time: 108 us -> 104 us (0.963)
  the two profiles are of different devices: /device:TPU:128 before, /device:TPU:7 now
where the time goes in v5:
time: 104 us; the launch traced here: 103 us
  starting transfers between devices  51.3 us (49%)
  waiting for transfers between devices  29.3 us (28%)
  Pallas kernels  16.9 us (16%)
  local copies, waits for them, and re-layouts  5.6 us (5%)
    ppermute x7, starting transfers between devices, shifted(): lax.ppermute(block, axis, [((i - distance) % size, i) for i in range(size)])  30.9 us
    pallas_call x11, Pallas kernels, call(): pl.pallas_call(kernel, out_shape=out_shape, in_specs=in_specs, out_specs=...  16.9 us
    ppermute x7, waiting for transfers between devices, shifted(): lax.ppermute(block, axis, [((i - distance) % size, i) for i in range(size)])  15.8 us
    ppermute x4, starting transfers between devices, body(): lax.ppermute(share, 'layer', trio[turn])  11.5 us
    ppermute x1, waiting for transfers between devices, body(): lax.ppermute(far, 'layer', across)  9.46 us
    ppermute x1, starting transfers between devices, body(): lax.ppermute(far, 'layer', across)  8.92 us
    unnamed x16, local copies, waits for them, and re-layouts  5.6 us
    ppermute x4, waiting for transfers between devices, body(): lax.ppermute(share, 'layer', trio[turn])  4.05 us
  transfers between devices with their start and end apart: 12, of which 4 were waited for; matrix products, arithmetic and copies ran while one was open for 0% of the time, Pallas kernels for 13%

profile of v5, /device:TPU:7, one launch (start us, length us, event | category | flops | bytes accessed | tf_op | source)
XLA Modules:
  0.0 103.3 jit_solution(10959737589589509493)
XLA Ops:
  0.0 0.0 copy-start
  0.0 1.0 %copy-done = bf16[1,1,2,2,256,256]{5,4,3,2,1,0:T(8,128)(2,1)S(1)} copy-done((bf16[1,1,2,2,256,256]{5,4,3,2,1,0:T(8,128)(2,1)S(1)}, bf16[1,1,2,2,256,256]{5,4,3,2,1,0:T(8,128)(2,1)}, u32[]{:S(2)}) %copy-start) | copy-done | bytes 524312
  1.0 0.0 copy-start.6
  1.0 0.7 copy-done.6
  1.7 2.1 %shard_map.46 = (bf16[528,256]{1,0:T(8,128)(2,1)}, bf16[528,256]{1,0:T(8,128)(2,1)}) custom-call(s32[2,2]{1,0:T(2,128)S(1)} %bitcast.8, bf16[2,2,256,256]{3,2,1,0:T(8,128)(2,1)S(1)} %bitcast.5), custom_call_target="tpu_custom_call" | custom-call | tf_op jit(solution)/shard_map/pallas_call | solution.py:159
  3.8 17.8 %collective-permute-start = (bf16[528,256]{1,0:T(8,128)(2,1)}, bf16[528,256]{1,0:T(8,128)(2,1)}, u32[]{:S(2)}, u32[]{:S(2)}) collective-permute-start(bf16[528,256]{1,0:T(8,128)(2,1)} %get-tuple-element.40), channel_id=1, source_target_pairs={{48,0},{96,48},{144,96},{192,144},{240,192},{288,240},{336,288},{3... | collective-permute-start | bytes 811016 | tf_op jit(solution)/shard_map/ppermute | solution.py:25
  21.6 1.9 %collective-permute-start.3 = (bf16[528,256]{1,0:T(8,128)(2,1)}, bf16[528,256]{1,0:T(8,128)(2,1)S(1)}, u32[]{:S(2)}, u32[]{:S(2)}) collective-permute-start(bf16[528,256]{1,0:T(8,128)(2,1)} %get-tuple-element.41), channel_id=1, source_target_pairs={{48,0},{96,48},{144,96},{192,144},{240,192},{288,240},{336,288},{3... | collective-permute-start | bytes 811016 | tf_op jit(solution)/shard_map/ppermute | solution.py:25
  23.5 0.0 copy-start.1
  23.5 1.4 %copy-done.1 = bf16[1,1,2,6,256,256]{5,4,3,2,1,0:T(8,128)(2,1)S(1)} copy-done((bf16[1,1,2,6,256,256]{5,4,3,2,1,0:T(8,128)(2,1)S(1)}, bf16[1,1,2,6,256,256]{5,4,3,2,1,0:T(8,128)(2,1)}, u32[]{:S(2)}) %copy-start.1) | copy-done | bytes 1572888
  24.9 0.0 copy-start.7
  24.9 0.7 copy-done.7
  25.6 5.6 %shard_map.47 = (bf16[3104,256]{1,0:T(8,128)(2,1)S(1)}, bf16[1552,256]{1,0:T(8,128)(2,1)}, bf16[1056,256]{1,0:T(8,128)(2,1)}) custom-call(s32[2,2]{1,0:T(2,128)S(1)} %bitcast.9, s32[2,6]{1,0:T(2,128)S(1)} %bitcast.10, bf16[2,2,256,256]{3,2,1,0:T(8,128)(2,1)S(1)} %bitcast.6, bf16[2,6,256,256]{3,2,1,0:T(8,128)(2,1)S(1)} %bitcast.7), custom_call_target="tpu_custom_call" | custom-call | tf_op jit(solution)/shard_map/pallas_call | solution.py:159
  31.2 1.0 collective-permute-start.2
  32.2 3.0 %collective-permute-start.1 = (bf16[1056,256]{1,0:T(8,128)(2,1)}, bf16[1056,256]{1,0:T(8,128)(2,1)}, u32[]{:S(2)}, u32[]{:S(2)}) collective-permute-start(bf16[1056,256]{1,0:T(8,128)(2,1)} %get-tuple-element.47.rights), channel_id=1, source_target_pairs={{96,0},{144,48},{192,96},{240,144},{288,192},{336,240},{384,288},{... | collective-permute-start | bytes 1622024 | tf_op jit(solution)/shard_map/ppermute | solution.py:25
  35.1 2.5 %collective-permute-start.8 = (bf16[1552,256]{1,0:T(8,128)(2,1)}, bf16[1552,256]{1,0:T(8,128)(2,1)}, u32[]{:S(2)}, u32[]{:S(2)}) collective-permute-start(bf16[1552,256]{1,0:T(8,128)(2,1)} %get-tuple-element.64), channel_id=1, source_target_pairs={{12,0},{18,6},{24,12},{30,18},{36,24},{42,30},{0,36},{6,42},{13,1}... | collective-permute-start | bytes 2383880 | tf_op jit(solution)/shard_map/ppermute | solution.py:25
  37.6 1.7 %shard_map.48 = (f32[768,256]{1,0:T(8,128)S(1)}, f32[768,256]{1,0:T(8,128)S(1)}) custom-call(bf16[3104,256]{1,0:T(8,128)(2,1)S(1)} %get-tuple-element.46.lefts.left_one, bf16[1056,256]{1,0:T(8,128)(2,1)} %get-tuple-element.47.rights), custom_call_target="tpu_custom_call" | custom-call | tf_op jit(solution)/shard_map/pallas_call | solution.py:159
  39.3 0.0 copy-start.2
  39.3 0.9 copy-done.2
  40.2 0.0 copy-start.4
  40.2 0.9 copy-done.4
  41.1 0.0 collective-permute-done.right_one
  41.1 0.0 copy-start.5
  41.1 2.9 %collective-permute-start.4 = (bf16[528,256]{1,0:T(8,128)(2,1)}, bf16[528,256]{1,0:T(8,128)(2,1)S(1)}, u32[]{:S(2)}, u32[]{:S(2)}) collective-permute-start(bf16[528,256]{1,0:T(8,128)(2,1)} %collective-permute-done.right_one), channel_id=1, source_target_pairs={{96,0},{144,48},{192,96},{240,144},{288,192},{336,240},{384,288},{... | collective-permute-start | bytes 811016 | tf_op jit(solution)/shard_map/ppermute | solution.py:25
  44.0 15.8 %collective-permute-done.3.right_one = bf16[528,256]{1,0:T(8,128)(2,1)S(1)} collective-permute-done((bf16[528,256]{1,0:T(8,128)(2,1)}, bf16[528,256]{1,0:T(8,128)(2,1)S(1)}, u32[]{:S(2)}, u32[]{:S(2)}) %collective-permute-start.3) | collective-permute-done | bytes 270368 | tf_op jit(solution)/shard_map/ppermute | solution.py:25
  59.8 1.9 %collective-permute-start.7 = (bf16[528,256]{1,0:T(8,128)(2,1)S(1)}, bf16[528,256]{1,0:T(8,128)(2,1)S(1)}, u32[]{:S(2)}, u32[]{:S(2)}) collective-permute-start(bf16[528,256]{1,0:T(8,128)(2,1)S(1)} %collective-permute-done.3.right_one), channel_id=1, source_target_pairs={{96,0},{144,48},{192,96},{240,144},{288,192},{336,240},{384,288},{... | collective-permute-start | bytes 811016 | tf_op jit(solution)/shard_map/ppermute | solution.py:25
  61.7 0.0 collective-permute-done.1.right_two
  61.8 0.0 collective-permute-done.2.left_two.left.left_one
  61.8 0.0 copy-done.5
  61.8 1.6 %shard_map.50.total_ref = f32[768,256]{1,0:T(8,128)S(1)} custom-call(f32[8,128]{1,0:T(8,128)S(1)} %shard_map.49.mark, f32[768,256]{1,0:T(8,128)S(1)} %copy-done.5, bf16[3104,256]{1,0:T(8,128)(2,1)S(1)} %get-tuple-element.46.lefts.left_one, bf16[528,256]{1,0:T(8,128)(2,1)} %collective-permute-done.right_one, ...), custom_call_target="tpu_custom_call" | custom-call | tf_op jit(solution)/shard_map/pallas_call | solution.py:159
  63.4 0.0 copy-start.3
  63.4 0.0 collective-permute-done.4.right
  63.4 0.3 shard_map.51
  63.7 2.3 %collective-permute-start.5 = (bf16[256,256]{1,0:T(8,128)(2,1)S(1)}, bf16[256,256]{1,0:T(8,128)(2,1)S(1)}, u32[]{:S(2)}, u32[]{:S(2)}) collective-permute-start(bf16[256,256]{1,0:T(8,128)(2,1)S(1)} %get-tuple-element.60), channel_id=1, source_target_pairs={{0,1},{1,2},{2,0},{3,4},{4,5},{5,3},{6,7},{7,8},{8,6},{9,10},{10,1... | collective-permute-start | bytes 393224 | tf_op jit(solution)/shard_map/ppermute | solution.py:230
  66.0 3.9 %collective-permute-start.6 = (bf16[256,256]{1,0:T(8,128)(2,1)S(1)}, bf16[256,256]{1,0:T(8,128)(2,1)S(1)}, u32[]{:S(2)}, u32[]{:S(2)}) collective-permute-start(bf16[256,256]{1,0:T(8,128)(2,1)S(1)} %get-tuple-element.61), channel_id=1, source_target_pairs={{0,2},{1,0},{2,1},{3,5},{4,3},{5,4},{6,8},{7,6},{8,7},{9,11},{10,9... | collective-permute-start | bytes 393224 | tf_op jit(solution)/shard_map/ppermute | solution.py:230
  69.9 0.0 copy-done.3
  69.9 1.7 %shard_map.53.total_ref = f32[768,256]{1,0:T(8,128)S(1)} custom-call(f32[8,128]{1,0:T(8,128)S(1)} %shard_map.49.mark, f32[768,256]{1,0:T(8,128)S(1)} %copy-done.3, bf16[3104,256]{1,0:T(8,128)(2,1)S(1)} %collective-permute-done.2.left_two.left.left_one, bf16[528,256]{1,0:T(8,128)(2,1)S(1)} %collective-permute-done.3.right_one, ...), custom_call_target="tpu_custom_call" | custom-call | tf_op jit(solution)/shard_map/pallas_call | solution.py:159
  71.6 0.0 collective-permute-done.7.right
  71.6 0.0 collective-permute-done.8.left
  71.7 2.1 %shard_map.54 = (bf16[256,256]{1,0:T(8,128)(2,1)S(1)}, bf16[256,256]{1,0:T(8,128)(2,1)}, bf16[256,256]{1,0:T(8,128)(2,1)}) custom-call(s32[1]{0:T(128)} %bitcast.4.layer, f32[768,256]{1,0:T(8,128)S(1)} %shard_map.53.total_ref, bf16[1552,256]{1,0:T(8,128)(2,1)} %collective-permute-done.8.left, bf16[528,256]{1,0:T(8,128)(2,1)S(1)} %collective-permute-done.7.right), custom_call_target="tpu_custom_call" | custom-call | tf_op jit(solution)/shard_map/pallas_call | solution.py:159
  73.8 1.9 %collective-permute-start.10 = (bf16[256,256]{1,0:T(8,128)(2,1)}, bf16[256,256]{1,0:T(8,128)(2,1)}, u32[]{:S(2)}, u32[]{:S(2)}) collective-permute-start(bf16[256,256]{1,0:T(8,128)(2,1)} %get-tuple-element.68), channel_id=1, source_target_pairs={{0,2},{1,0},{2,1},{3,5},{4,3},{5,4},{6,8},{7,6},{8,7},{9,11},{10,9... | collective-permute-start | bytes 393224 | tf_op jit(solution)/shard_map/ppermute | solution.py:230
  75.7 3.4 %collective-permute-start.9 = (bf16[256,256]{1,0:T(8,128)(2,1)}, bf16[256,256]{1,0:T(8,128)(2,1)}, u32[]{:S(2)}, u32[]{:S(2)}) collective-permute-start(bf16[256,256]{1,0:T(8,128)(2,1)} %get-tuple-element.67), channel_id=1, source_target_pairs={{0,1},{1,2},{2,0},{3,4},{4,5},{5,3},{6,7},{7,8},{8,6},{9,10},{10,1... | collective-permute-start | bytes 393224 | tf_op jit(solution)/shard_map/ppermute | solution.py:230
  79.1 0.0 collective-permute-done.5.one
  79.1 0.0 collective-permute-done.6.two
  79.2 0.7 collective-permute-done.10.two
  79.8 3.4 %collective-permute-done.9.one = bf16[256,256]{1,0:T(8,128)(2,1)} collective-permute-done((bf16[256,256]{1,0:T(8,128)(2,1)}, bf16[256,256]{1,0:T(8,128)(2,1)}, u32[]{:S(2)}, u32[]{:S(2)}) %collective-permute-start.9) | collective-permute-done | bytes 131104 | tf_op jit(solution)/shard_map/ppermute | solution.py:230
  83.2 1.0 shard_map.55
  84.3 8.9 %collective-permute-start.11 = (bf16[128,512]{1,0:T(8,128)(2,1)S(1)}, bf16[128,512]{1,0:T(8,128)(2,1)S(1)}, u32[]{:S(2)}, u32[]{:S(2)}) collective-permute-start(bf16[128,512]{1,0:T(8,128)(2,1)S(1)} %get-tuple-element.74), channel_id=1, source_target_pairs={{0,3},{1,4},{2,5},{3,0},{4,1},{5,2},{6,9},{7,10},{8,11},{9,6},{10,... | collective-permute-start | bytes 393224 | tf_op jit(solution)/shard_map/ppermute | solution.py:240
  93.2 9.5 %collective-permute-done.11.far = bf16[128,512]{1,0:T(8,128)(2,1)S(1)} collective-permute-done((bf16[128,512]{1,0:T(8,128)(2,1)S(1)}, bf16[128,512]{1,0:T(8,128)(2,1)S(1)}, u32[]{:S(2)}, u32[]{:S(2)}) %collective-permute-start.11) | collective-permute-done | bytes 131104 | tf_op jit(solution)/shard_map/ppermute | solution.py:240
  102.6 0.7 shard_map.56
  (2 shorter events, 0.0 us)
Async XLA Ops:
  0.0 1.0 %copy-start = (bf16[1,1,2,2,256,256]{5,4,3,2,1,0:T(8,128)(2,1)S(1)}, bf16[1,1,2,2,256,256]{5,4,3,2,1,0:T(8,128)(2,1)}, u32[]{:S(2)}) copy-start(bf16[1,1,2,2,256,256]{5,4,3,2,1,0:T(8,128)(2,1)} %param.6) | copy-start | bytes 1572868
  1.0 0.7 copy-start.6
  3.8 37.3 %collective-permute-start = (bf16[528,256]{1,0:T(8,128)(2,1)}, bf16[528,256]{1,0:T(8,128)(2,1)}, u32[]{:S(2)}, u32[]{:S(2)}) collective-permute-start(bf16[528,256]{1,0:T(8,128)(2,1)} %get-tuple-element.40), channel_id=1, source_target_pairs={{48,0},{96,48},{144,96},{192,144},{240,192},{288,240},{336,288},{3... | collective-permute-start | bytes 811016 | tf_op jit(solution)/shard_map/ppermute | solution.py:25
  21.6 38.2 %collective-permute-start.3 = (bf16[528,256]{1,0:T(8,128)(2,1)}, bf16[528,256]{1,0:T(8,128)(2,1)S(1)}, u32[]{:S(2)}, u32[]{:S(2)}) collective-permute-start(bf16[528,256]{1,0:T(8,128)(2,1)} %get-tuple-element.41), channel_id=1, source_target_pairs={{48,0},{96,48},{144,96},{192,144},{240,192},{288,240},{336,288},{3... | collective-permute-start | bytes 811016 | tf_op jit(solution)/shard_map/ppermute | solution.py:25
  23.5 1.4 %copy-start.1 = (bf16[1,1,2,6,256,256]{5,4,3,2,1,0:T(8,128)(2,1)S(1)}, bf16[1,1,2,6,256,256]{5,4,3,2,1,0:T(8,128)(2,1)}, u32[]{:S(2)}) copy-start(bf16[1,1,2,6,256,256]{5,4,3,2,1,0:T(8,128)(2,1)} %param.4) | copy-start | bytes 4718596
  24.9 0.7 copy-start.7
  31.2 30.6 %collective-permute-start.2 = (bf16[3104,256]{1,0:T(8,128)(2,1)S(1)}, bf16[3104,256]{1,0:T(8,128)(2,1)S(1)}, u32[]{:S(2)}, u32[]{:S(2)}) collective-permute-start(bf16[3104,256]{1,0:T(8,128)(2,1)S(1)} %get-tuple-element.46.lefts.left_one), channel_id=1, source_target_pairs={{6,0},{12,6},{18,12},{24,18},{30,24},{36,30},{42,36},{0,42},{7,1},... | collective-permute-start | bytes 4767752 | tf_op jit(solution)/shard_map/ppermute | solution.py:25
  32.2 29.6 %collective-permute-start.1 = (bf16[1056,256]{1,0:T(8,128)(2,1)}, bf16[1056,256]{1,0:T(8,128)(2,1)}, u32[]{:S(2)}, u32[]{:S(2)}) collective-permute-start(bf16[1056,256]{1,0:T(8,128)(2,1)} %get-tuple-element.47.rights), channel_id=1, source_target_pairs={{96,0},{144,48},{192,96},{240,144},{288,192},{336,240},{384,288},{... | collective-permute-start | bytes 1622024 | tf_op jit(solution)/shard_map/ppermute | solution.py:25
  35.1 36.5 %collective-permute-start.8 = (bf16[1552,256]{1,0:T(8,128)(2,1)}, bf16[1552,256]{1,0:T(8,128)(2,1)}, u32[]{:S(2)}, u32[]{:S(2)}) collective-permute-start(bf16[1552,256]{1,0:T(8,128)(2,1)} %get-tuple-element.64), channel_id=1, source_target_pairs={{12,0},{18,6},{24,12},{30,18},{36,24},{42,30},{0,36},{6,42},{13,1}... | collective-permute-start | bytes 2383880 | tf_op jit(solution)/shard_map/ppermute | solution.py:25
  39.3 0.9 copy-start.2
  40.2 0.9 copy-start.4
  41.1 20.7 %copy-start.5 = (f32[768,256]{1,0:T(8,128)S(1)}, f32[768,256]{1,0:T(8,128)}, u32[]{:S(2)}) copy-start(f32[768,256]{1,0:T(8,128)} %copy-done.4) | copy-start | bytes 2359300
  41.1 22.3 %collective-permute-start.4 = (bf16[528,256]{1,0:T(8,128)(2,1)}, bf16[528,256]{1,0:T(8,128)(2,1)S(1)}, u32[]{:S(2)}, u32[]{:S(2)}) collective-permute-start(bf16[528,256]{1,0:T(8,128)(2,1)} %collective-permute-done.right_one), channel_id=1, source_target_pairs={{96,0},{144,48},{192,96},{240,144},{288,192},{336,240},{384,288},{... | collective-permute-start | bytes 811016 | tf_op jit(solution)/shard_map/ppermute | solution.py:25
  59.8 11.8 %collective-permute-start.7 = (bf16[528,256]{1,0:T(8,128)(2,1)S(1)}, bf16[528,256]{1,0:T(8,128)(2,1)S(1)}, u32[]{:S(2)}, u32[]{:S(2)}) collective-permute-start(bf16[528,256]{1,0:T(8,128)(2,1)S(1)} %collective-permute-done.3.right_one), channel_id=1, source_target_pairs={{96,0},{144,48},{192,96},{240,144},{288,192},{336,240},{384,288},{... | collective-permute-start | bytes 811016 | tf_op jit(solution)/shard_map/ppermute | solution.py:25
  63.4 6.5 %copy-start.3 = (f32[768,256]{1,0:T(8,128)S(1)}, f32[768,256]{1,0:T(8,128)}, u32[]{:S(2)}) copy-start(f32[768,256]{1,0:T(8,128)} %copy-done.2) | copy-start | bytes 2359300
  63.7 15.4 %collective-permute-start.5 = (bf16[256,256]{1,0:T(8,128)(2,1)S(1)}, bf16[256,256]{1,0:T(8,128)(2,1)S(1)}, u32[]{:S(2)}, u32[]{:S(2)}) collective-permute-start(bf16[256,256]{1,0:T(8,128)(2,1)S(1)} %get-tuple-element.60), channel_id=1, source_target_pairs={{0,1},{1,2},{2,0},{3,4},{4,5},{5,3},{6,7},{7,8},{8,6},{9,10},{10,1... | collective-permute-start | bytes 393224 | tf_op jit(solution)/shard_map/ppermute | solution.py:230
  66.0 13.1 %collective-permute-start.6 = (bf16[256,256]{1,0:T(8,128)(2,1)S(1)}, bf16[256,256]{1,0:T(8,128)(2,1)S(1)}, u32[]{:S(2)}, u32[]{:S(2)}) collective-permute-start(bf16[256,256]{1,0:T(8,128)(2,1)S(1)} %get-tuple-element.61), channel_id=1, source_target_pairs={{0,2},{1,0},{2,1},{3,5},{4,3},{5,4},{6,8},{7,6},{8,7},{9,11},{10,9... | collective-permute-start | bytes 393224 | tf_op jit(solution)/shard_map/ppermute | solution.py:230
  73.8 6.0 %collective-permute-start.10 = (bf16[256,256]{1,0:T(8,128)(2,1)}, bf16[256,256]{1,0:T(8,128)(2,1)}, u32[]{:S(2)}, u32[]{:S(2)}) collective-permute-start(bf16[256,256]{1,0:T(8,128)(2,1)} %get-tuple-element.68), channel_id=1, source_target_pairs={{0,2},{1,0},{2,1},{3,5},{4,3},{5,4},{6,8},{7,6},{8,7},{9,11},{10,9... | collective-permute-start | bytes 393224 | tf_op jit(solution)/shard_map/ppermute | solution.py:230
  75.7 7.5 %collective-permute-start.9 = (bf16[256,256]{1,0:T(8,128)(2,1)}, bf16[256,256]{1,0:T(8,128)(2,1)}, u32[]{:S(2)}, u32[]{:S(2)}) collective-permute-start(bf16[256,256]{1,0:T(8,128)(2,1)} %get-tuple-element.67), channel_id=1, source_target_pairs={{0,1},{1,2},{2,0},{3,4},{4,5},{5,3},{6,7},{7,8},{8,6},{9,10},{10,1... | collective-permute-start | bytes 393224 | tf_op jit(solution)/shard_map/ppermute | solution.py:230
  84.3 18.4 %collective-permute-start.11 = (bf16[128,512]{1,0:T(8,128)(2,1)S(1)}, bf16[128,512]{1,0:T(8,128)(2,1)S(1)}, u32[]{:S(2)}, u32[]{:S(2)}) collective-permute-start(bf16[128,512]{1,0:T(8,128)(2,1)S(1)} %get-tuple-element.74), channel_id=1, source_target_pairs={{0,3},{1,4},{2,5},{3,0},{4,1},{5,2},{6,9},{7,10},{8,11},{9,6},{10,... | collective-permute-start | bytes 393224 | tf_op jit(solution)/shard_map/ppermute | solution.py:240

commit v6 on v4

--- a/solution.py
+++ b/solution.py
@@ -12,6 +12,7 @@
 RT = 3
 SA = 6
 SB = 2
+STEPS = 4
 TRIO = 3
 SHARE = 128
 HELD = 2
@@ -91,25 +92,24 @@
     mark[...] = jnp.zeros_like(mark)
 
 
-def local_kernel(lefts, rights, *refs):
-    totals, place_ref = refs[:-1], refs[-1]
-    for column, total in enumerate(totals):
-        total[...] = jnp.zeros_like(total)
-        add_term(total, place_ref, part(lefts, column, BLOCK), part(rights, column, PIECE))
-
-
-def middle_kernel(mark, start, left_one, right_one, left_two, right_two, total, place_ref, *, column):
-    total[...] = start[...]
-    add_term(total, place_ref, part(left_one, 1 - column, BLOCK), right_one)
-    add_term(total, place_ref, part(left_two, column, BLOCK), part(right_two, column, PIECE))
-
-
-def late_kernel(layer, total_ref, left, right, *refs, block):
-    share_refs, total, place_ref = refs[:-2], refs[-2], refs[-1]
-    total[...] = total_ref[...]
-    add_term(total, place_ref, part(left, block, BLOCK), right)
+def block_kernel(layer, mark, lefts, left_next, *refs, column):
+    count = STEPS + column
+    arriving, shares = list(refs[:count]), refs[count : count + TRIO]
+    arriving[2] = part(arriving[2], column, PIECE)
+    total, place_ref, pieces, last, sem = refs[count + TRIO :]
+    targets = [pieces.at[step] for step in range(STEPS)] + [last] * column
+    copies = [pltpu.make_async_copy(source, target, sem.at[n]) for n, (source, target) in enumerate(zip(arriving, targets))]
+    for copy in copies:
+        copy.start()
+    blocks = [part(lefts, 0, BLOCK), part(lefts, 1, BLOCK), part(left_next, 0, BLOCK), part(left_next, 1, BLOCK), last]
+    total[...] = jnp.zeros_like(total)
+    for step in range(STEPS):
+        copies[step].wait()
+        if column and step == STEPS - 1:
+            copies[STEPS].wait()
+        add_term(total, place_ref, blocks[column + step], pieces.at[step])
     half = layer[0] // TRIO
-    for turn, share in enumerate(share_refs):
+    for turn, share in enumerate(shares):
         spot = lax.rem(layer[0] + turn, TRIO)
         for n, side in enumerate((half, 1 - half)):
             rows = pl.ds(pl.multiple_of((side * TRIO + spot) * SHARE, SHARE), SHARE)
@@ -122,18 +122,23 @@
     far[...] = added[SHARE:].astype(far.dtype)
 
 
-def final_kernel(*refs):
-    out_ref = refs[-1]
-    for n in range(HELD):
-        added = refs[2 * n][...] + refs[2 * n + 1][...].astype(jnp.float32)
-        out_ref[:, n * TS : (n + 1) * TS] = added.astype(out_ref.dtype)
+def total_kernel(near, far, out_ref):
+    out_ref[...] = (near[...] + far[...].astype(jnp.float32)).astype(out_ref.dtype)
+
+
+def final_kernel(first, near, far, out_ref):
+    out_ref[:, :TS] = first[...]
+    total_kernel(near, far, out_ref.at[:, TS:])
 
 
 AHEAD = 4 * 10**10
+GATHER = 10**12
+FIRST = 10**12
+AFTER = 0
 SMEM = pl.BlockSpec(memory_space=pltpu.SMEM)
 VMEM = pl.BlockSpec(memory_space=pltpu.VMEM)
 ANY = pl.BlockSpec(memory_space=pl.ANY)
-PARAMS = pltpu.CompilerParams(vmem_limit_bytes=32 * 1024 * 1024)
+PARAMS = pltpu.CompilerParams(vmem_limit_bytes=12 * 1024 * 1024)
 
 
 def call(kernel, out_shape, in_specs, operands, scratch=(), cost=0):
@@ -154,8 +159,6 @@
 
 def body(left_tiles, left_place, right_tiles, right_place):
     layer = lax.axis_index("layer").astype(jnp.int32).reshape(1)
-    places = pltpu.SMEM((SA,), jnp.int32)
-    total = array(RT * TS, TS, jnp.float32)
     pieces = call(pack_right_kernel, [array(PIECE, TS)] * HELD, [SMEM, VMEM], (right_place[0, 0], right_tiles[0, 0]))
     right_one = [shifted(piece, "row", -1) for piece in pieces]
     lefts, left_zero, rights = call(
@@ -167,39 +170,33 @@
     right_two = shifted(rights, "row", -2)
     left_next = shifted(lefts, "col", -1)
     left_last = shifted(left_zero, "col", -2)
-    totals = list(call(local_kernel, [total] * HELD, [VMEM] * 2, (lefts, rights), [places]))
-    right_one[0], totals = lax.optimization_barrier((right_one[0], totals))
     mark = call(mark_kernel, array(8, 128, jnp.float32), [ANY], (right_one[1],), cost=AHEAD)
-    right_two, left_next, left_last, mark = lax.optimization_barrier((right_two, left_next, left_last, mark))
+    right_two, left_next, mark = lax.optimization_barrier((right_two, left_next, mark))
     right_three = [shifted(piece, "row", -2) for piece in right_one]
-    ones, held = (lefts, left_next), ((left_next, 1), (left_last, 0))
     trio = [[(p, p // TRIO * TRIO + (p + turn) % TRIO) for p in range(2 * TRIO)] for turn in range(TRIO)]
     across = [(p, (p + TRIO) % (2 * TRIO)) for p in range(2 * TRIO)]
     shares = []
     for j in range(HELD):
+        arriving = [pieces[j], right_one[j], right_two, right_three[j]] + [left_last] * j
         if j:
-            totals[j], shares[j - 1] = lax.optimization_barrier((totals[j], shares[j - 1]))
-        left, block = held[j]
-        start = call(
-            functools.partial(middle_kernel, column=j),
-            total,
-            [ANY] + [VMEM] * 5,
-            (mark, totals[j], ones[j], right_one[j], left_next, right_two),
-            [places],
-        )
-        if j:
-            right_three[j], start = lax.optimization_barrier((right_three[j], start))
+            arriving[0], shares[j - 1] = lax.optimization_barrier((arriving[0], shares[j - 1]))
         shares.append(
             call(
-                functools.partial(late_kernel, block=block),
+                functools.partial(block_kernel, column=j),
                 [array(2 * SHARE, TS)] * TRIO,
-                [SMEM] + [VMEM] * 3,
-                (layer, start, left, right_three[j]),
-                [pltpu.VMEM((RT * TS, TS), jnp.float32), places],
+                [SMEM, ANY] + [VMEM] * 2 + [ANY] * len(arriving),
+                (layer, mark, lefts, left_next, *arriving),
+                [
+                    pltpu.VMEM((RT * TS, TS), jnp.float32),
+                    pltpu.SMEM((SA,), jnp.int32),
+                    pltpu.VMEM((STEPS, PIECE, TS), jnp.bfloat16),
+                    pltpu.VMEM((BLOCK, TS), jnp.bfloat16),
+                    pltpu.SemaphoreType.DMA((STEPS + 1,)),
+                ],
             )
         )
     ends = []
-    for j, (own_share, *others) in enumerate(shares):
+    for j, (own, *others) in enumerate(shares):
         arrived = [lax.ppermute(share, "layer", trio[turn]) for turn, share in enumerate(others, 1)]
         if j:
             arrived, ends = lax.optimization_barrier((arrived, ends))
@@ -207,14 +204,13 @@
             gather_kernel,
             [array(SHARE, TS, jnp.float32), array(SHARE, TS)],
             [VMEM] * TRIO,
-            (own_share, *arrived),
-            cost=(1 - j) * 10**12,
+            (own, *arrived),
+            cost=(GATHER, AFTER)[j],
         )
         ends.append(near)
-        shares[j] = far
-    for j, far in enumerate(shares):
-        ends.insert(2 * j + 1, lax.ppermute(far, "layer", across))
-    return call(final_kernel, array(SHARE, HELD * TS), [VMEM] * len(ends), ends)
+        shares[j] = lax.ppermute(far, "layer", across)
+    first = call(total_kernel, array(SHARE, TS), [VMEM] * 2, (ends[0], shares[0]), cost=FIRST)
+    return call(final_kernel, array(SHARE, HELD * TS), [VMEM] * 3, (first, ends[1], shares[1]))
 
 
 def solution(mesh):

time: 108 us -> 97.9 us (0.906)
  the two profiles are of different devices: /device:TPU:128 before, /device:TPU:56 now
where the time goes in v6:
time: 97.9 us; the launch traced here: 96.5 us
  starting transfers between devices  60 us (61%)
  waiting for transfers between devices  19.6 us (20%)
  Pallas kernels  12.9 us (13%)
  local copies, waits for them, and re-layouts  3.8 us (4%)
    ppermute x7, starting transfers between devices, shifted(): lax.ppermute(block, axis, [((i - distance) % size, i) for i in range(size)])  32.3 us
    ppermute x7, waiting for transfers between devices, shifted(): lax.ppermute(block, axis, [((i - distance) % size, i) for i in range(size)])  16.8 us
    ppermute x2, starting transfers between devices, body(): shares[j] = lax.ppermute(far, 'layer', across)  15.2 us
    pallas_call x9, Pallas kernels, call(): pl.pallas_call(kernel, out_shape=out_shape, in_specs=in_specs, out_specs=...  12.9 us
    ppermute x4, starting transfers between devices, body(): lax.ppermute(share, 'layer', trio[turn])  12.6 us
    unnamed x8, local copies, waits for them, and re-layouts  3.8 us
    ppermute x2, waiting for transfers between devices, body(): shares[j] = lax.ppermute(far, 'layer', across)  2.73 us
  transfers between devices with their start and end apart: 13, of which 2 were waited for; matrix products, arithmetic and copies ran while one was open for 0% of the time, Pallas kernels for 10%

profile of v6, /device:TPU:56, one launch (start us, length us, event | category | flops | bytes accessed | tf_op | source)
XLA Modules:
  0.0 96.5 jit_solution(13611910656245081946)
XLA Ops:
  0.0 0.0 copy-start.1
  0.0 1.0 %copy-done.1 = bf16[1,1,2,2,256,256]{5,4,3,2,1,0:T(8,128)(2,1)S(1)} copy-done((bf16[1,1,2,2,256,256]{5,4,3,2,1,0:T(8,128)(2,1)S(1)}, bf16[1,1,2,2,256,256]{5,4,3,2,1,0:T(8,128)(2,1)}, u32[]{:S(2)}) %copy-start.1) | copy-done | bytes 524312
  1.0 0.0 copy-start.2
  1.0 0.7 copy-done.2
  1.7 1.3 %shard_map.46 = (bf16[528,256]{1,0:T(8,128)(2,1)}, bf16[528,256]{1,0:T(8,128)(2,1)S(1)}) custom-call(s32[2,2]{1,0:T(2,128)S(1)} %bitcast.7, bf16[2,2,256,256]{3,2,1,0:T(8,128)(2,1)S(1)} %bitcast.6), custom_call_target="tpu_custom_call" | custom-call | tf_op jit(solution)/shard_map/pallas_call | solution.py:145
  3.0 15.9 %collective-permute-start.3 = (bf16[528,256]{1,0:T(8,128)(2,1)}, bf16[528,256]{1,0:T(8,128)(2,1)}, u32[]{:S(2)}, u32[]{:S(2)}) collective-permute-start(bf16[528,256]{1,0:T(8,128)(2,1)} %get-tuple-element.30.right_zero.refs_0_), channel_id=1, source_target_pairs={{48,0},{96,48},{144,96},{192,144},{240,192},{288,240},{336,288},{3... | collective-permute-start | bytes 811016 | tf_op jit(solution)/shard_map/ppermute | solution.py:26
  18.9 1.9 %collective-permute-start.2 = (bf16[528,256]{1,0:T(8,128)(2,1)S(1)}, bf16[528,256]{1,0:T(8,128)(2,1)}, u32[]{:S(2)}, u32[]{:S(2)}) collective-permute-start(bf16[528,256]{1,0:T(8,128)(2,1)S(1)} %get-tuple-element.40.right_one.refs_0_), channel_id=1, source_target_pairs={{48,0},{96,48},{144,96},{192,144},{240,192},{288,240},{336,288},{3... | collective-permute-start | bytes 811016 | tf_op jit(solution)/shard_map/ppermute | solution.py:26
  20.9 0.0 copy-start
  20.9 1.4 %copy-done = bf16[1,1,2,6,256,256]{5,4,3,2,1,0:T(8,128)(2,1)S(1)} copy-done((bf16[1,1,2,6,256,256]{5,4,3,2,1,0:T(8,128)(2,1)S(1)}, bf16[1,1,2,6,256,256]{5,4,3,2,1,0:T(8,128)(2,1)}, u32[]{:S(2)}) %copy-start) | copy-done | bytes 1572888
  22.3 0.0 copy-start.3
  22.3 0.7 copy-done.3
  23.0 2.1 %shard_map.47 = (bf16[3104,256]{1,0:T(8,128)(2,1)S(1)}, bf16[1552,256]{1,0:T(8,128)(2,1)}, bf16[1056,256]{1,0:T(8,128)(2,1)}) custom-call(s32[2,6]{1,0:T(2,128)S(1)} %bitcast.8, bf16[2,6,256,256]{3,2,1,0:T(8,128)(2,1)S(1)} %bitcast.5, bf16[528,256]{1,0:T(8,128)(2,1)} %get-tuple-element.30.right_zero.refs_0_, ...), custom_call_target="tpu_custom_call" | custom-call | tf_op jit(solution)/shard_map/pallas_call | solution.py:145
  25.1 1.9 %collective-permute-start.1 = (bf16[3104,256]{1,0:T(8,128)(2,1)S(1)}, bf16[3104,256]{1,0:T(8,128)(2,1)S(1)}, u32[]{:S(2)}, u32[]{:S(2)}) collective-permute-start(bf16[3104,256]{1,0:T(8,128)(2,1)S(1)} %get-tuple-element.33.lefts), channel_id=1, source_target_pairs={{6,0},{12,6},{18,12},{24,18},{30,24},{36,30},{42,36},{0,42},{7,1},... | collective-permute-start | bytes 4767752 | tf_op jit(solution)/shard_map/ppermute | solution.py:26
  27.0 3.2 %collective-permute-start = (bf16[1056,256]{1,0:T(8,128)(2,1)}, bf16[1056,256]{1,0:T(8,128)(2,1)}, u32[]{:S(2)}, u32[]{:S(2)}) collective-permute-start(bf16[1056,256]{1,0:T(8,128)(2,1)} %get-tuple-element.32), channel_id=1, source_target_pairs={{96,0},{144,48},{192,96},{240,144},{288,192},{336,240},{384,288},{... | collective-permute-start | bytes 1622024 | tf_op jit(solution)/shard_map/ppermute | solution.py:26
  30.3 2.8 %collective-permute-start.6 = (bf16[1552,256]{1,0:T(8,128)(2,1)}, bf16[1552,256]{1,0:T(8,128)(2,1)}, u32[]{:S(2)}, u32[]{:S(2)}) collective-permute-start(bf16[1552,256]{1,0:T(8,128)(2,1)} %get-tuple-element.41), channel_id=1, source_target_pairs={{12,0},{18,6},{24,12},{30,18},{36,24},{42,30},{0,36},{6,42},{13,1}... | collective-permute-start | bytes 2383880 | tf_op jit(solution)/shard_map/ppermute | solution.py:26
  33.0 0.0 collective-permute-done.3.refs_1_
  33.0 3.3 %collective-permute-start.4 = (bf16[528,256]{1,0:T(8,128)(2,1)}, bf16[528,256]{1,0:T(8,128)(2,1)S(1)}, u32[]{:S(2)}, u32[]{:S(2)}) collective-permute-start(bf16[528,256]{1,0:T(8,128)(2,1)} %collective-permute-done.3.refs_1_), channel_id=1, source_target_pairs={{96,0},{144,48},{192,96},{240,144},{288,192},{336,240},{384,288},{... | collective-permute-start | bytes 811016 | tf_op jit(solution)/shard_map/ppermute | solution.py:26
  36.3 16.8 %collective-permute-done.2.right_one.refs_1_ = bf16[528,256]{1,0:T(8,128)(2,1)} collective-permute-done((bf16[528,256]{1,0:T(8,128)(2,1)S(1)}, bf16[528,256]{1,0:T(8,128)(2,1)}, u32[]{:S(2)}, u32[]{:S(2)}) %collective-permute-start.2) | collective-permute-done | bytes 270368 | tf_op jit(solution)/shard_map/ppermute | solution.py:26
  53.1 3.2 %collective-permute-start.5 = (bf16[528,256]{1,0:T(8,128)(2,1)}, bf16[528,256]{1,0:T(8,128)(2,1)S(1)}, u32[]{:S(2)}, u32[]{:S(2)}) collective-permute-start(bf16[528,256]{1,0:T(8,128)(2,1)} %collective-permute-done.2.right_one.refs_1_), channel_id=1, source_target_pairs={{96,0},{144,48},{192,96},{240,144},{288,192},{336,240},{384,288},{... | collective-permute-start | bytes 811016 | tf_op jit(solution)/shard_map/ppermute | solution.py:26
  56.4 0.0 collective-permute-done.refs_2_
  56.4 0.0 collective-permute-done.1.left_next
  56.4 0.0 collective-permute-done.4.refs_3_
  56.4 3.0 %shard_map.49 = (bf16[256,256]{1,0:T(8,128)(2,1)S(1)}, bf16[256,256]{1,0:T(8,128)(2,1)S(1)}, bf16[256,256]{1,0:T(8,128)(2,1)S(1)}) custom-call(s32[1]{0:T(128)} %bitcast.layer, f32[8,128]{1,0:T(8,128)S(1)} %shard_map.48.mark, bf16[3104,256]{1,0:T(8,128)(2,1)S(1)} %get-tuple-element.33.lefts, bf16[3104,256]{1,0:T(8,128)(2,1)S(1)} %collective-permute-done.1.left_next, ...), custom_call_target="tpu_custom_call" | custom-call | tf_op jit(solution)/shard_map/pallas_call | solution.py:145
  59.5 1.9 %collective-permute-start.10 = (bf16[256,256]{1,0:T(8,128)(2,1)S(1)}, bf16[256,256]{1,0:T(8,128)(2,1)S(1)}, u32[]{:S(2)}, u32[]{:S(2)}) collective-permute-start(bf16[256,256]{1,0:T(8,128)(2,1)S(1)} %get-tuple-element.46), channel_id=1, source_target_pairs={{0,2},{1,0},{2,1},{3,5},{4,3},{5,4},{6,8},{7,6},{8,7},{9,11},{10,9... | collective-permute-start | bytes 393224 | tf_op jit(solution)/shard_map/ppermute | solution.py:200
  61.4 3.9 %collective-permute-start.9 = (bf16[256,256]{1,0:T(8,128)(2,1)S(1)}, bf16[256,256]{1,0:T(8,128)(2,1)S(1)}, u32[]{:S(2)}, u32[]{:S(2)}) collective-permute-start(bf16[256,256]{1,0:T(8,128)(2,1)S(1)} %get-tuple-element.45), channel_id=1, source_target_pairs={{0,1},{1,2},{2,0},{3,4},{4,5},{5,3},{6,7},{7,8},{8,6},{9,10},{10,1... | collective-permute-start | bytes 393224 | tf_op jit(solution)/shard_map/ppermute | solution.py:200
  65.3 0.0 collective-permute-done.5.refs_3_
  65.4 0.0 collective-permute-done.6.refs_4_
  65.4 3.2 %shard_map.50 = (bf16[256,256]{1,0:T(8,128)(2,1)S(1)}, bf16[256,256]{1,0:T(8,128)(2,1)}, bf16[256,256]{1,0:T(8,128)(2,1)}) custom-call(s32[1]{0:T(128)} %bitcast.layer, f32[8,128]{1,0:T(8,128)S(1)} %shard_map.48.mark, bf16[3104,256]{1,0:T(8,128)(2,1)S(1)} %get-tuple-element.33.lefts, bf16[3104,256]{1,0:T(8,128)(2,1)S(1)} %collective-permute-done.1.left_next, ...), custom_call_target="tpu_custom_call" | custom-call | tf_op jit(solution)/shard_map/pallas_call | solution.py:145
  68.6 3.4 %collective-permute-start.7 = (bf16[256,256]{1,0:T(8,128)(2,1)}, bf16[256,256]{1,0:T(8,128)(2,1)}, u32[]{:S(2)}, u32[]{:S(2)}) collective-permute-start(bf16[256,256]{1,0:T(8,128)(2,1)} %get-tuple-element.42), channel_id=1, source_target_pairs={{0,1},{1,2},{2,0},{3,4},{4,5},{5,3},{6,7},{7,8},{8,6},{9,10},{10,1... | collective-permute-start | bytes 393224 | tf_op jit(solution)/shard_map/ppermute | solution.py:200
  71.9 3.4 %collective-permute-start.8 = (bf16[256,256]{1,0:T(8,128)(2,1)}, bf16[256,256]{1,0:T(8,128)(2,1)}, u32[]{:S(2)}, u32[]{:S(2)}) collective-permute-start(bf16[256,256]{1,0:T(8,128)(2,1)} %get-tuple-element.43), channel_id=1, source_target_pairs={{0,2},{1,0},{2,1},{3,5},{4,3},{5,4},{6,8},{7,6},{8,7},{9,11},{10,9... | collective-permute-start | bytes 393224 | tf_op jit(solution)/shard_map/ppermute | solution.py:200
  75.3 0.0 collective-permute-done.10.two
  75.3 0.0 collective-permute-done.9.one
  75.3 0.1 shard_map.51
  75.4 9.7 %collective-permute-start.11 = (bf16[128,256]{1,0:T(8,128)(2,1)S(1)}, bf16[128,256]{1,0:T(8,128)(2,1)S(1)}, u32[]{:S(2)}, u32[]{:S(2)}) collective-permute-start(bf16[128,256]{1,0:T(8,128)(2,1)S(1)} %get-tuple-element.49), channel_id=1, source_target_pairs={{0,3},{1,4},{2,5},{3,0},{4,1},{5,2},{6,9},{7,10},{8,11},{9,6},{10,... | collective-permute-start | bytes 196616 | tf_op jit(solution)/shard_map/ppermute | solution.py:211
  85.1 0.0 collective-permute-done.7.one
  85.1 0.0 collective-permute-done.8.two
  85.1 1.6 %shard_map.53 = (f32[128,256]{1,0:T(8,128)S(1)}, bf16[128,256]{1,0:T(8,128)(2,1)}) custom-call(bf16[256,256]{1,0:T(8,128)(2,1)S(1)} %get-tuple-element.50.own, bf16[256,256]{1,0:T(8,128)(2,1)} %collective-permute-done.7.one, bf16[256,256]{1,0:T(8,128)(2,1)} %collective-permute-done.8.two), custom_call_target="tpu_custom_call" | custom-call | tf_op jit(solution)/shard_map/pallas_call | solution.py:145
  86.7 5.5 %collective-permute-start.12 = (bf16[128,256]{1,0:T(8,128)(2,1)}, bf16[128,256]{1,0:T(8,128)(2,1)}, u32[]{:S(2)}, u32[]{:S(2)}) collective-permute-start(bf16[128,256]{1,0:T(8,128)(2,1)} %get-tuple-element.54), channel_id=1, source_target_pairs={{0,3},{1,4},{2,5},{3,0},{4,1},{5,2},{6,9},{7,10},{8,11},{9,6},{10,... | collective-permute-start | bytes 196616 | tf_op jit(solution)/shard_map/ppermute | solution.py:211
  92.2 0.0 collective-permute-done.11.far
  92.3 2.7 %collective-permute-done.12.far = bf16[128,256]{1,0:T(8,128)(2,1)} collective-permute-done((bf16[128,256]{1,0:T(8,128)(2,1)}, bf16[128,256]{1,0:T(8,128)(2,1)}, u32[]{:S(2)}, u32[]{:S(2)}) %collective-permute-start.12) | collective-permute-done | bytes 65568 | tf_op jit(solution)/shard_map/ppermute | solution.py:211
  95.0 1.5 %shard_map.54 = bf16[128,512]{1,0:T(8,128)(2,1)} custom-call(bf16[128,256]{1,0:T(8,128)(2,1)S(1)} %shard_map.52.first, f32[128,256]{1,0:T(8,128)S(1)} %get-tuple-element.53.near, bf16[128,256]{1,0:T(8,128)(2,1)} %collective-permute-done.12.far), custom_call_target="tpu_custom_call" | custom-call | tf_op jit(solution)/shard_map/pallas_call | solution.py:145
  (2 shorter events, 0.0 us)
Async XLA Ops:
  0.0 1.0 %copy-start.1 = (bf16[1,1,2,2,256,256]{5,4,3,2,1,0:T(8,128)(2,1)S(1)}, bf16[1,1,2,2,256,256]{5,4,3,2,1,0:T(8,128)(2,1)}, u32[]{:S(2)}) copy-start(bf16[1,1,2,2,256,256]{5,4,3,2,1,0:T(8,128)(2,1)} %param.6) | copy-start | bytes 1572868
  1.0 0.7 copy-start.2
  3.0 30.0 %collective-permute-start.3 = (bf16[528,256]{1,0:T(8,128)(2,1)}, bf16[528,256]{1,0:T(8,128)(2,1)}, u32[]{:S(2)}, u32[]{:S(2)}) collective-permute-start(bf16[528,256]{1,0:T(8,128)(2,1)} %get-tuple-element.30.right_zero.refs_0_), channel_id=1, source_target_pairs={{48,0},{96,48},{144,96},{192,144},{240,192},{288,240},{336,288},{3... | collective-permute-start | bytes 811016 | tf_op jit(solution)/shard_map/ppermute | solution.py:26
  18.9 34.2 %collective-permute-start.2 = (bf16[528,256]{1,0:T(8,128)(2,1)S(1)}, bf16[528,256]{1,0:T(8,128)(2,1)}, u32[]{:S(2)}, u32[]{:S(2)}) collective-permute-start(bf16[528,256]{1,0:T(8,128)(2,1)S(1)} %get-tuple-element.40.right_one.refs_0_), channel_id=1, source_target_pairs={{48,0},{96,48},{144,96},{192,144},{240,192},{288,240},{336,288},{3... | collective-permute-start | bytes 811016 | tf_op jit(solution)/shard_map/ppermute | solution.py:26
  20.9 1.4 %copy-start = (bf16[1,1,2,6,256,256]{5,4,3,2,1,0:T(8,128)(2,1)S(1)}, bf16[1,1,2,6,256,256]{5,4,3,2,1,0:T(8,128)(2,1)}, u32[]{:S(2)}) copy-start(bf16[1,1,2,6,256,256]{5,4,3,2,1,0:T(8,128)(2,1)} %param.4) | copy-start | bytes 4718596
  22.3 0.7 copy-start.3
  25.1 31.3 %collective-permute-start.1 = (bf16[3104,256]{1,0:T(8,128)(2,1)S(1)}, bf16[3104,256]{1,0:T(8,128)(2,1)S(1)}, u32[]{:S(2)}, u32[]{:S(2)}) collective-permute-start(bf16[3104,256]{1,0:T(8,128)(2,1)S(1)} %get-tuple-element.33.lefts), channel_id=1, source_target_pairs={{6,0},{12,6},{18,12},{24,18},{30,24},{36,30},{42,36},{0,42},{7,1},... | collective-permute-start | bytes 4767752 | tf_op jit(solution)/shard_map/ppermute | solution.py:26
  27.0 29.4 %collective-permute-start = (bf16[1056,256]{1,0:T(8,128)(2,1)}, bf16[1056,256]{1,0:T(8,128)(2,1)}, u32[]{:S(2)}, u32[]{:S(2)}) collective-permute-start(bf16[1056,256]{1,0:T(8,128)(2,1)} %get-tuple-element.32), channel_id=1, source_target_pairs={{96,0},{144,48},{192,96},{240,144},{288,192},{336,240},{384,288},{... | collective-permute-start | bytes 1622024 | tf_op jit(solution)/shard_map/ppermute | solution.py:26
  30.3 35.1 %collective-permute-start.6 = (bf16[1552,256]{1,0:T(8,128)(2,1)}, bf16[1552,256]{1,0:T(8,128)(2,1)}, u32[]{:S(2)}, u32[]{:S(2)}) collective-permute-start(bf16[1552,256]{1,0:T(8,128)(2,1)} %get-tuple-element.41), channel_id=1, source_target_pairs={{12,0},{18,6},{24,12},{30,18},{36,24},{42,30},{0,36},{6,42},{13,1}... | collective-permute-start | bytes 2383880 | tf_op jit(solution)/shard_map/ppermute | solution.py:26
  33.0 23.4 %collective-permute-start.4 = (bf16[528,256]{1,0:T(8,128)(2,1)}, bf16[528,256]{1,0:T(8,128)(2,1)S(1)}, u32[]{:S(2)}, u32[]{:S(2)}) collective-permute-start(bf16[528,256]{1,0:T(8,128)(2,1)} %collective-permute-done.3.refs_1_), channel_id=1, source_target_pairs={{96,0},{144,48},{192,96},{240,144},{288,192},{336,240},{384,288},{... | collective-permute-start | bytes 811016 | tf_op jit(solution)/shard_map/ppermute | solution.py:26
  53.1 12.2 %collective-permute-start.5 = (bf16[528,256]{1,0:T(8,128)(2,1)}, bf16[528,256]{1,0:T(8,128)(2,1)S(1)}, u32[]{:S(2)}, u32[]{:S(2)}) collective-permute-start(bf16[528,256]{1,0:T(8,128)(2,1)} %collective-permute-done.2.right_one.refs_1_), channel_id=1, source_target_pairs={{96,0},{144,48},{192,96},{240,144},{288,192},{336,240},{384,288},{... | collective-permute-start | bytes 811016 | tf_op jit(solution)/shard_map/ppermute | solution.py:26
  59.5 15.9 %collective-permute-start.10 = (bf16[256,256]{1,0:T(8,128)(2,1)S(1)}, bf16[256,256]{1,0:T(8,128)(2,1)S(1)}, u32[]{:S(2)}, u32[]{:S(2)}) collective-permute-start(bf16[256,256]{1,0:T(8,128)(2,1)S(1)} %get-tuple-element.46), channel_id=1, source_target_pairs={{0,2},{1,0},{2,1},{3,5},{4,3},{5,4},{6,8},{7,6},{8,7},{9,11},{10,9... | collective-permute-start | bytes 393224 | tf_op jit(solution)/shard_map/ppermute | solution.py:200
  61.4 13.9 %collective-permute-start.9 = (bf16[256,256]{1,0:T(8,128)(2,1)S(1)}, bf16[256,256]{1,0:T(8,128)(2,1)S(1)}, u32[]{:S(2)}, u32[]{:S(2)}) collective-permute-start(bf16[256,256]{1,0:T(8,128)(2,1)S(1)} %get-tuple-element.45), channel_id=1, source_target_pairs={{0,1},{1,2},{2,0},{3,4},{4,5},{5,3},{6,7},{7,8},{8,6},{9,10},{10,1... | collective-permute-start | bytes 393224 | tf_op jit(solution)/shard_map/ppermute | solution.py:200
  68.6 16.5 %collective-permute-start.7 = (bf16[256,256]{1,0:T(8,128)(2,1)}, bf16[256,256]{1,0:T(8,128)(2,1)}, u32[]{:S(2)}, u32[]{:S(2)}) collective-permute-start(bf16[256,256]{1,0:T(8,128)(2,1)} %get-tuple-element.42), channel_id=1, source_target_pairs={{0,1},{1,2},{2,0},{3,4},{4,5},{5,3},{6,7},{7,8},{8,6},{9,10},{10,1... | collective-permute-start | bytes 393224 | tf_op jit(solution)/shard_map/ppermute | solution.py:200
  71.9 13.2 %collective-permute-start.8 = (bf16[256,256]{1,0:T(8,128)(2,1)}, bf16[256,256]{1,0:T(8,128)(2,1)}, u32[]{:S(2)}, u32[]{:S(2)}) collective-permute-start(bf16[256,256]{1,0:T(8,128)(2,1)} %get-tuple-element.43), channel_id=1, source_target_pairs={{0,2},{1,0},{2,1},{3,5},{4,3},{5,4},{6,8},{7,6},{8,7},{9,11},{10,9... | collective-permute-start | bytes 393224 | tf_op jit(solution)/shard_map/ppermute | solution.py:200
  75.4 16.8 %collective-permute-start.11 = (bf16[128,256]{1,0:T(8,128)(2,1)S(1)}, bf16[128,256]{1,0:T(8,128)(2,1)S(1)}, u32[]{:S(2)}, u32[]{:S(2)}) collective-permute-start(bf16[128,256]{1,0:T(8,128)(2,1)S(1)} %get-tuple-element.49), channel_id=1, source_target_pairs={{0,3},{1,4},{2,5},{3,0},{4,1},{5,2},{6,9},{7,10},{8,11},{9,6},{10,... | collective-permute-start | bytes 196616 | tf_op jit(solution)/shard_map/ppermute | solution.py:211
  86.7 8.3 %collective-permute-start.12 = (bf16[128,256]{1,0:T(8,128)(2,1)}, bf16[128,256]{1,0:T(8,128)(2,1)}, u32[]{:S(2)}, u32[]{:S(2)}) collective-permute-start(bf16[128,256]{1,0:T(8,128)(2,1)} %get-tuple-element.54), channel_id=1, source_target_pairs={{0,3},{1,4},{2,5},{3,0},{4,1},{5,2},{6,9},{7,10},{8,11},{9,6},{10,... | collective-permute-start | bytes 196616 | tf_op jit(solution)/shard_map/ppermute | solution.py:211

commit v7 on v6

--- a/solution.py
+++ b/solution.py
@@ -1,5 +1,3 @@
-import functools
-
 import jax
 import jax.numpy as jnp
 from jax import lax
@@ -66,11 +64,10 @@
     packed_ref[slots * TS :, :] = note.astype(jnp.float32).astype(jnp.bfloat16)
 
 
-def pack_right_kernel(place_ref, right_ref, *pieces):
-    for column, piece in enumerate(pieces):
-        for p in range(SB):
-            piece[p * TS : (p + 1) * TS, :] = right_ref[column, p]
-        write_note(piece, place_ref, column, SB)
+def packed(tiles, places):
+    count = places.shape[0]
+    note = jnp.pad(places.astype(jnp.bfloat16)[None], ((0, NOTE - 1), (0, TS - count)))
+    return jnp.concatenate([tiles.reshape(count * TS, TS), note])
 
 
 def pack_left_kernel(place_ref, left_ref, right_zero, right_one, lefts, left_zero, rights):
@@ -92,11 +89,8 @@
     mark[...] = jnp.zeros_like(mark)
 
 
-def block_kernel(layer, mark, lefts, left_next, *refs, column):
-    count = STEPS + column
-    arriving, shares = list(refs[:count]), refs[count : count + TRIO]
-    arriving[2] = part(arriving[2], column, PIECE)
-    total, place_ref, pieces, last, sem = refs[count + TRIO :]
+def add_steps(total, place_ref, lefts, left_next, arriving, pieces, last, sem, column):
+    arriving = [*arriving[:2], part(arriving[2], column, PIECE), *arriving[3:]]
     targets = [pieces.at[step] for step in range(STEPS)] + [last] * column
     copies = [pltpu.make_async_copy(source, target, sem.at[n]) for n, (source, target) in enumerate(zip(arriving, targets))]
     for copy in copies:
@@ -108,33 +102,40 @@
         if column and step == STEPS - 1:
             copies[STEPS].wait()
         add_term(total, place_ref, blocks[column + step], pieces.at[step])
-    half = layer[0] // TRIO
-    for turn, share in enumerate(shares):
-        spot = lax.rem(layer[0] + turn, TRIO)
-        for n, side in enumerate((half, 1 - half)):
-            rows = pl.ds(pl.multiple_of((side * TRIO + spot) * SHARE, SHARE), SHARE)
-            share[n * SHARE : (n + 1) * SHARE, :] = total[rows, :].astype(share.dtype)
-
-
-def gather_kernel(own, one, two, near, far):
-    added = own[...].astype(jnp.float32) + one[...].astype(jnp.float32) + two[...].astype(jnp.float32)
+
+
+def first_kernel(layer, mark, lefts, left_next, own, one, two, three, keep, send, total, *scratch):
+    add_steps(total, scratch[0], lefts, left_next, [own, one, two, three], *scratch[1:], 0)
+    pair, side = layer[0] // 2, lax.rem(layer[0], 2)
+    for turn in range(TRIO):
+        spot = lax.rem(pair + turn, TRIO)
+        for share, parity in ((keep, side), (send, 1 - side)):
+            rows = pl.ds(pl.multiple_of((2 * spot + parity) * SHARE, SHARE), SHARE)
+            share[turn * SHARE : (turn + 1) * SHARE, :] = total[rows, :].astype(share.dtype)
+
+
+def second_kernel(mark, lefts, left_next, own, one, two, three, left_last, shares, total, *scratch):
+    add_steps(total, scratch[0], lefts, left_next, [own, one, two, three, left_last], *scratch[1:], 1)
+    shares[...] = total[...].astype(shares.dtype)
+
+
+def pair_kernel(keep, came, near, *far):
+    added = keep[...].astype(jnp.float32) + came[...].astype(jnp.float32)
     near[...] = added[:SHARE]
-    far[...] = added[SHARE:].astype(far.dtype)
-
-
-def total_kernel(near, far, out_ref):
-    out_ref[...] = (near[...] + far[...].astype(jnp.float32)).astype(out_ref.dtype)
-
-
-def final_kernel(first, near, far, out_ref):
-    out_ref[:, :TS] = first[...]
-    total_kernel(near, far, out_ref.at[:, TS:])
+    for n, share in enumerate(far, 1):
+        share[...] = added[n * SHARE : (n + 1) * SHARE].astype(share.dtype)
+
+
+def final_kernel(near, one, two, shares, out_ref):
+    out_ref[:, :TS] = (near[...] + one[...].astype(jnp.float32) + two[...].astype(jnp.float32)).astype(out_ref.dtype)
+    total = shares[:SHARE].astype(jnp.float32)
+    for n in range(1, 2 * TRIO):
+        total += shares[n * SHARE : (n + 1) * SHARE].astype(jnp.float32)
+    out_ref[:, TS:] = total.astype(out_ref.dtype)
 
 
 AHEAD = 4 * 10**10
 GATHER = 10**12
-FIRST = 10**12
-AFTER = 0
 SMEM = pl.BlockSpec(memory_space=pltpu.SMEM)
 VMEM = pl.BlockSpec(memory_space=pltpu.VMEM)
 ANY = pl.BlockSpec(memory_space=pl.ANY)
@@ -159,7 +160,8 @@
 
 def body(left_tiles, left_place, right_tiles, right_place):
     layer = lax.axis_index("layer").astype(jnp.int32).reshape(1)
-    pieces = call(pack_right_kernel, [array(PIECE, TS)] * HELD, [SMEM, VMEM], (right_place[0, 0], right_tiles[0, 0]))
+    right, right_at = right_tiles[0, 0], right_place[0, 0]
+    pieces = [packed(right[j], right_at[j]) for j in range(HELD)]
     right_one = [shifted(piece, "row", -1) for piece in pieces]
     lefts, left_zero, rights = call(
         pack_left_kernel,
@@ -173,44 +175,42 @@
     mark = call(mark_kernel, array(8, 128, jnp.float32), [ANY], (right_one[1],), cost=AHEAD)
     right_two, left_next, mark = lax.optimization_barrier((right_two, left_next, mark))
     right_three = [shifted(piece, "row", -2) for piece in right_one]
-    trio = [[(p, p // TRIO * TRIO + (p + turn) % TRIO) for p in range(2 * TRIO)] for turn in range(TRIO)]
-    across = [(p, (p + TRIO) % (2 * TRIO)) for p in range(2 * TRIO)]
-    shares = []
-    for j in range(HELD):
-        arriving = [pieces[j], right_one[j], right_two, right_three[j]] + [left_last] * j
-        if j:
-            arriving[0], shares[j - 1] = lax.optimization_barrier((arriving[0], shares[j - 1]))
-        shares.append(
-            call(
-                functools.partial(block_kernel, column=j),
-                [array(2 * SHARE, TS)] * TRIO,
-                [SMEM, ANY] + [VMEM] * 2 + [ANY] * len(arriving),
-                (layer, mark, lefts, left_next, *arriving),
-                [
-                    pltpu.VMEM((RT * TS, TS), jnp.float32),
-                    pltpu.SMEM((SA,), jnp.int32),
-                    pltpu.VMEM((STEPS, PIECE, TS), jnp.bfloat16),
-                    pltpu.VMEM((BLOCK, TS), jnp.bfloat16),
-                    pltpu.SemaphoreType.DMA((STEPS + 1,)),
-                ],
-            )
-        )
-    ends = []
-    for j, (own, *others) in enumerate(shares):
-        arrived = [lax.ppermute(share, "layer", trio[turn]) for turn, share in enumerate(others, 1)]
-        if j:
-            arrived, ends = lax.optimization_barrier((arrived, ends))
-        near, far = call(
-            gather_kernel,
-            [array(SHARE, TS, jnp.float32), array(SHARE, TS)],
-            [VMEM] * TRIO,
-            (own, *arrived),
-            cost=(GATHER, AFTER)[j],
-        )
-        ends.append(near)
-        shares[j] = lax.ppermute(far, "layer", across)
-    first = call(total_kernel, array(SHARE, TS), [VMEM] * 2, (ends[0], shares[0]), cost=FIRST)
-    return call(final_kernel, array(SHARE, HELD * TS), [VMEM] * 3, (first, ends[1], shares[1]))
+    scratch = [
+        pltpu.VMEM((RT * TS, TS), jnp.float32),
+        pltpu.SMEM((SA,), jnp.int32),
+        pltpu.VMEM((STEPS, PIECE, TS), jnp.bfloat16),
+        pltpu.VMEM((BLOCK, TS), jnp.bfloat16),
+        pltpu.SemaphoreType.DMA((STEPS + 1,)),
+    ]
+    keep, send = call(
+        first_kernel,
+        [array(TRIO * SHARE, TS)] * 2,
+        [SMEM, ANY] + [VMEM] * 2 + [ANY] * STEPS,
+        (layer, mark, lefts, left_next, pieces[0], right_one[0], right_two, right_three[0]),
+        scratch,
+    )
+    came = lax.ppermute(send, "layer", [(p, p ^ 1) for p in range(2 * TRIO)])
+    pieces[1], send = lax.optimization_barrier((pieces[1], send))
+    shares = call(
+        second_kernel,
+        array(RT * TS, TS),
+        [ANY] + [VMEM] * 2 + [ANY] * (STEPS + 1),
+        (mark, lefts, left_next, pieces[1], right_one[1], right_two, right_three[1], left_last),
+        scratch,
+    )
+    shares = lax.all_to_all(shares.reshape(2 * TRIO, SHARE, TS), "layer", 0, 0, tiled=True).reshape(RT * TS, TS)
+    near, *far = call(
+        pair_kernel,
+        [array(SHARE, TS, jnp.float32)] + [array(SHARE, TS)] * 2,
+        [VMEM] * 2,
+        (keep, came),
+        cost=GATHER,
+    )
+    ends = [
+        lax.ppermute(share, "layer", [(p, 2 * ((p // 2 + turn) % TRIO) + p % 2) for p in range(2 * TRIO)])
+        for turn, share in enumerate(far, 1)
+    ]
+    return call(final_kernel, array(SHARE, HELD * TS), [VMEM] * 4, (near, *ends, shares))
 
 
 def solution(mesh):

time: 97.9 us -> 100 us (1.021)
  waiting for transfers between devices: 19.6 us -> 28.6 us
  starting transfers between devices: 60 us -> 54.7 us
  Pallas kernels: 12.9 us -> 10.1 us
  other arithmetic: 0 us -> 1.42 us
    ppermute x6 -> x3, starting transfers between devices: 27.8 us -> 14.6 us  [the longest x2 9.76 us: body(): lax.ppermute(share, 'layer', [(p, 2 * ((p // 2 + turn) % TRIO) + p % 2) f...]
    all_to_all x0 -> x1, starting transfers between devices: none -> 7.8 us  [body(): lax.all_to_all(shares.reshape(2 * TRIO, SHARE, TS), 'layer', 0, 0, tiled=...]
    ppermute x6 -> x3, waiting for transfers between devices: 2.74 us -> 9.7 us  [the longest x2 9.7 us: body(): lax.ppermute(share, 'layer', [(p, 2 * ((p // 2 + turn) % TRIO) + p % 2) f...]
    pallas_call x9 -> x6, Pallas kernels: 12.9 us -> 10.1 us  [call(): pl.pallas_call(kernel, out_shape=out_shape, in_specs=in_specs, out_specs=...]
    ppermute x7, waiting for transfers between devices: 16.8 us -> 18.9 us  [shifted(): lax.ppermute(block, axis, [((i - distance) % size, i) for i in range(size)])]
    unnamed x8 -> x10, local copies, waits for them, and re-layouts: 3.8 us -> 2.35 us
    slice x0 -> x1, local copies, waits for them, and re-layouts: none -> 1.18 us  [body(): pieces = [packed(right[j], right_at[j]) for j in range(HELD)]]
  transfers between devices with their start and end apart: 13 -> 11, of which waited for: 2 -> 2; matrix products, arithmetic and copies ran while one was open for 0% -> 0% of each run, Pallas kernels for 10% -> 8%
where the time goes in v7:
time: 100 us; the launch traced here: 98.5 us
  starting transfers between devices  54.7 us (55%)
  waiting for transfers between devices  28.6 us (29%)
  Pallas kernels  10.1 us (10%)
  local copies, waits for them, and re-layouts  3.54 us (4%)
  other arithmetic  1.42 us (1%)
    ppermute x7, starting transfers between devices, shifted(): lax.ppermute(block, axis, [((i - distance) % size, i) for i in range(size)])  32.3 us
    ppermute x7, waiting for transfers between devices, shifted(): lax.ppermute(block, axis, [((i - distance) % size, i) for i in range(size)])  18.9 us
    pallas_call x6, Pallas kernels, call(): pl.pallas_call(kernel, out_shape=out_shape, in_specs=in_specs, out_specs=...  10.1 us
    ppermute x2, starting transfers between devices, body(): lax.ppermute(share, 'layer', [(p, 2 * ((p // 2 + turn) % TRIO) + p % 2) f...  9.76 us
    ppermute x2, waiting for transfers between devices, body(): lax.ppermute(share, 'layer', [(p, 2 * ((p // 2 + turn) % TRIO) + p % 2) f...  9.7 us
    all_to_all x1, starting transfers between devices, body(): lax.all_to_all(shares.reshape(2 * TRIO, SHARE, TS), 'layer', 0, 0, tiled=...  7.8 us
    ppermute x1, starting transfers between devices, body(): came = lax.ppermute(send, 'layer', [(p, p ^ 1) for p in range(2 * TRIO)])  4.87 us
    unnamed x10, local copies, waits for them, and re-layouts  2.35 us
  transfers between devices with their start and end apart: 11, of which 2 were waited for; matrix products, arithmetic and copies ran while one was open for 0% of the time, Pallas kernels for 8%

profile of v7, /device:TPU:56, one launch (start us, length us, event | category | flops | bytes accessed | tf_op | source)
XLA Modules:
  0.0 98.5 jit_solution(1501626873184389500)
XLA Ops:
  0.0 0.0 copy-start.2
  0.0 0.0 copy-start.1
  0.0 1.2 %fusion.4 = (bf16[1,1,1,2,256,256]{5,4,3,2,1,0:T(8,128)(2,1)S(1)}, bf16[1,1,1,2,256,256]{5,4,3,2,1,0:T(8,128)(2,1)S(1)}) fusion(bf16[1,1,2,2,256,256]{5,4,3,2,1,0:T(8,128)(2,1)} %param.6), kind=kLoop, calls=%fused_computation.7 | loop fusion | bytes 1048576 | tf_op jit(solution)/shard_map/slice | solution.py:164
  1.2 0.7 convert.4
  1.9 0.7 fusion.2.right_zero.own
  2.6 15.9 %collective-permute-start.3 = (bf16[528,256]{1,0:T(8,128)(2,1)}, bf16[528,256]{1,0:T(8,128)(2,1)}, u32[]{:S(2)}, u32[]{:S(2)}) collective-permute-start(bf16[528,256]{1,0:T(8,128)(2,1)} %fusion.2.right_zero.own), channel_id=1, source_target_pairs={{48,0},{96,48},{144,96},{192,144},{240,192},{288,240},{336,288},{3... | collective-permute-start | bytes 811016 | tf_op jit(solution)/shard_map/ppermute | solution.py:24
  18.6 1.9 %collective-permute-start.2 = (bf16[528,256]{1,0:T(8,128)(2,1)S(1)}, bf16[528,256]{1,0:T(8,128)(2,1)}, u32[]{:S(2)}, u32[]{:S(2)}) collective-permute-start(bf16[528,256]{1,0:T(8,128)(2,1)S(1)} %fusion.3.right_one.own), channel_id=1, source_target_pairs={{48,0},{96,48},{144,96},{192,144},{240,192},{288,240},{336,288},{3... | collective-permute-start | bytes 811016 | tf_op jit(solution)/shard_map/ppermute | solution.py:24
  20.5 0.0 copy-done.2
  20.5 0.0 copy-done.1
  20.5 2.1 %shard_map.46 = (bf16[3104,256]{1,0:T(8,128)(2,1)S(1)}, bf16[1552,256]{1,0:T(8,128)(2,1)}, bf16[1056,256]{1,0:T(8,128)(2,1)}) custom-call(s32[2,6]{1,0:T(2,128)S(1)} %bitcast.13, bf16[2,6,256,256]{3,2,1,0:T(8,128)(2,1)S(1)} %bitcast.12, bf16[528,256]{1,0:T(8,128)(2,1)} %fusion.2.right_zero.own, bf16[528,256]{1,0:T(8,128)(2,1)S(1)} %fusion.3.right_one.own), custom_call_target="tpu_custom_call" | custom-call | tf_op jit(solution)/shard_map/pallas_call | solution.py:146
  22.6 1.9 %collective-permute-start.1 = (bf16[3104,256]{1,0:T(8,128)(2,1)S(1)}, bf16[3104,256]{1,0:T(8,128)(2,1)S(1)}, u32[]{:S(2)}, u32[]{:S(2)}) collective-permute-start(bf16[3104,256]{1,0:T(8,128)(2,1)S(1)} %get-tuple-element.18.lefts), channel_id=1, source_target_pairs={{6,0},{12,6},{18,12},{24,18},{30,24},{36,30},{42,36},{0,42},{7,1},... | collective-permute-start | bytes 4767752 | tf_op jit(solution)/shard_map/ppermute | solution.py:24
  24.6 3.2 %collective-permute-start = (bf16[1056,256]{1,0:T(8,128)(2,1)}, bf16[1056,256]{1,0:T(8,128)(2,1)}, u32[]{:S(2)}, u32[]{:S(2)}) collective-permute-start(bf16[1056,256]{1,0:T(8,128)(2,1)} %get-tuple-element.17), channel_id=1, source_target_pairs={{96,0},{144,48},{192,96},{240,144},{288,192},{336,240},{384,288},{... | collective-permute-start | bytes 1622024 | tf_op jit(solution)/shard_map/ppermute | solution.py:24
  27.8 2.8 %collective-permute-start.9 = (bf16[1552,256]{1,0:T(8,128)(2,1)}, bf16[1552,256]{1,0:T(8,128)(2,1)}, u32[]{:S(2)}, u32[]{:S(2)}) collective-permute-start(bf16[1552,256]{1,0:T(8,128)(2,1)} %get-tuple-element.28), channel_id=1, source_target_pairs={{12,0},{18,6},{24,12},{30,18},{36,24},{42,30},{0,36},{6,42},{13,1}... | collective-permute-start | bytes 2383880 | tf_op jit(solution)/shard_map/ppermute | solution.py:24
  30.6 0.0 collective-permute-done.3.one
  30.6 3.3 %collective-permute-start.4 = (bf16[528,256]{1,0:T(8,128)(2,1)}, bf16[528,256]{1,0:T(8,128)(2,1)S(1)}, u32[]{:S(2)}, u32[]{:S(2)}) collective-permute-start(bf16[528,256]{1,0:T(8,128)(2,1)} %collective-permute-done.3.one), channel_id=1, source_target_pairs={{96,0},{144,48},{192,96},{240,144},{288,192},{336,240},{384,288},{... | collective-permute-start | bytes 811016 | tf_op jit(solution)/shard_map/ppermute | solution.py:24
  33.9 18.9 %collective-permute-done.2.right_one.one = bf16[528,256]{1,0:T(8,128)(2,1)} collective-permute-done((bf16[528,256]{1,0:T(8,128)(2,1)S(1)}, bf16[528,256]{1,0:T(8,128)(2,1)}, u32[]{:S(2)}, u32[]{:S(2)}) %collective-permute-start.2) | collective-permute-done | bytes 270368 | tf_op jit(solution)/shard_map/ppermute | solution.py:24
  52.7 3.2 %collective-permute-start.8 = (bf16[528,256]{1,0:T(8,128)(2,1)}, bf16[528,256]{1,0:T(8,128)(2,1)S(1)}, u32[]{:S(2)}, u32[]{:S(2)}) collective-permute-start(bf16[528,256]{1,0:T(8,128)(2,1)} %collective-permute-done.2.right_one.one), channel_id=1, source_target_pairs={{96,0},{144,48},{192,96},{240,144},{288,192},{336,240},{384,288},{... | collective-permute-start | bytes 811016 | tf_op jit(solution)/shard_map/ppermute | solution.py:24
  56.0 0.0 collective-permute-done.two
  56.0 0.0 collective-permute-done.1.left_next
  56.0 0.0 collective-permute-done.4.three
  56.0 3.0 %shard_map.48 = (bf16[384,256]{1,0:T(8,128)(2,1)S(1)}, bf16[384,256]{1,0:T(8,128)(2,1)}) custom-call(s32[1]{0:T(128)} %bitcast.layer, f32[8,128]{1,0:T(8,128)S(1)} %shard_map.47.mark, bf16[3104,256]{1,0:T(8,128)(2,1)S(1)} %get-tuple-element.18.lefts, bf16[3104,256]{1,0:T(8,128)(2,1)S(1)} %collective-permute-done.1.left_next, ...), custom_call_target="tpu_custom_call" | custom-call | tf_op jit(solution)/shard_map/pallas_call | solution.py:146
  59.0 0.0 copy-start.3
  59.0 0.7 copy-done.3
  59.7 4.9 %collective-permute-start.5 = (bf16[384,256]{1,0:T(8,128)(2,1)}, bf16[384,256]{1,0:T(8,128)(2,1)}, u32[]{:S(2)}, u32[]{:S(2)}) collective-permute-start(bf16[384,256]{1,0:T(8,128)(2,1)} %get-tuple-element.23), channel_id=1, source_target_pairs={{0,1},{1,0},{2,3},{3,2},{4,5},{5,4},{6,7},{7,6},{8,9},{9,8},{10,11... | collective-permute-start | bytes 589832 | tf_op jit(solution)/shard_map/ppermute | solution.py:192
  64.6 0.0 collective-permute-done.8.three
  64.6 0.0 collective-permute-done.9.left_last
  64.6 2.3 %shard_map.50 = bf16[768,256]{1,0:T(8,128)(2,1)S(1)} custom-call(f32[8,128]{1,0:T(8,128)S(1)} %shard_map.47.mark, bf16[3104,256]{1,0:T(8,128)(2,1)S(1)} %get-tuple-element.18.lefts, bf16[3104,256]{1,0:T(8,128)(2,1)S(1)} %collective-permute-done.1.left_next, bf16[528,256]{1,0:T(8,128)(2,1)S(1)} %fusion.3.right_one.own, ...), custom_call_target="tpu_custom_call" | custom-call | tf_op jit(solution)/shard_map/pallas_call | solution.py:146
  66.9 0.0 copy-start
  66.9 0.7 copy-done
  67.6 7.8 %all-to-all-start = ((bf16[6,128,256]{2,1,0:T(8,128)(2,1)}), bf16[6,128,256]{2,1,0:T(8,128)(2,1)}, u32[]{:S(2)}, u32[]{:S(2)}) async-start(bf16[6,128,256]{2,1,0:T(8,128)(2,1)} %bitcast.11), calls=%async_computation | async-start | bytes 786432 | tf_op jit(solution)/shard_map/all_to_all | solution.py:201
  75.4 0.0 collective-permute-done.5.came
  75.4 0.0 copy-start.4
  75.4 0.9 copy-done.4
  76.3 1.0 shard_map.49
  77.3 4.8 %collective-permute-start.6 = (bf16[128,256]{1,0:T(8,128)(2,1)S(1)}, bf16[128,256]{1,0:T(8,128)(2,1)S(1)}, u32[]{:S(2)}, u32[]{:S(2)}) collective-permute-start(bf16[128,256]{1,0:T(8,128)(2,1)S(1)} %get-tuple-element.25), channel_id=1, source_target_pairs={{0,2},{1,3},{2,4},{3,5},{4,0},{5,1},{6,8},{7,9},{8,10},{9,11},{10,... | collective-permute-start | bytes 196616 | tf_op jit(solution)/shard_map/ppermute | solution.py:210
  82.1 4.9 %collective-permute-start.7 = (bf16[128,256]{1,0:T(8,128)(2,1)S(1)}, bf16[128,256]{1,0:T(8,128)(2,1)S(1)}, u32[]{:S(2)}, u32[]{:S(2)}) collective-permute-start(bf16[128,256]{1,0:T(8,128)(2,1)S(1)} %get-tuple-element.26), channel_id=1, source_target_pairs={{0,4},{1,5},{2,0},{3,1},{4,2},{5,3},{6,10},{7,11},{8,6},{9,7},{10,... | collective-permute-start | bytes 196616 | tf_op jit(solution)/shard_map/ppermute | solution.py:210
  87.1 9.7 %collective-permute-done.6.one = bf16[128,256]{1,0:T(8,128)(2,1)S(1)} collective-permute-done((bf16[128,256]{1,0:T(8,128)(2,1)S(1)}, bf16[128,256]{1,0:T(8,128)(2,1)S(1)}, u32[]{:S(2)}, u32[]{:S(2)}) %collective-permute-start.6) | collective-permute-done | bytes 65568 | tf_op jit(solution)/shard_map/ppermute | solution.py:210
  96.8 0.0 collective-permute-done.7.two
  96.8 0.0 all-to-all-done
  96.8 1.7 %shard_map.51 = bf16[128,512]{1,0:T(8,128)(2,1)} custom-call(f32[128,256]{1,0:T(8,128)S(1)} %get-tuple-element.24.near, bf16[128,256]{1,0:T(8,128)(2,1)S(1)} %collective-permute-done.6.one, bf16[128,256]{1,0:T(8,128)(2,1)S(1)} %collective-permute-done.7.two, bf16[768,256]{1,0:T(8,128)(2,1)} %bitcast.8.shares), custom_call_target="tpu_custom_call" | custom-call | tf_op jit(solution)/shard_map/pallas_call | solution.py:146
  (3 shorter events, 0.0 us)
Async XLA Ops:
  0.0 20.5 %copy-start.2 = (s32[1,1,2,6]{3,2,1,0:T(2,128)S(1)}, s32[1,1,2,6]{3,2,1,0:T(2,128)}, u32[]{:S(2)}) copy-start(s32[1,1,2,6]{3,2,1,0:T(2,128)} %param.5) | copy-start | bytes 148
  0.0 20.5 %copy-start.1 = (bf16[1,1,2,6,256,256]{5,4,3,2,1,0:T(8,128)(2,1)S(1)}, bf16[1,1,2,6,256,256]{5,4,3,2,1,0:T(8,128)(2,1)}, u32[]{:S(2)}) copy-start(bf16[1,1,2,6,256,256]{5,4,3,2,1,0:T(8,128)(2,1)} %param.4) | copy-start | bytes 4718596
  2.6 28.0 %collective-permute-start.3 = (bf16[528,256]{1,0:T(8,128)(2,1)}, bf16[528,256]{1,0:T(8,128)(2,1)}, u32[]{:S(2)}, u32[]{:S(2)}) collective-permute-start(bf16[528,256]{1,0:T(8,128)(2,1)} %fusion.2.right_zero.own), channel_id=1, source_target_pairs={{48,0},{96,48},{144,96},{192,144},{240,192},{288,240},{336,288},{3... | collective-permute-start | bytes 811016 | tf_op jit(solution)/shard_map/ppermute | solution.py:24
  18.6 34.2 %collective-permute-start.2 = (bf16[528,256]{1,0:T(8,128)(2,1)S(1)}, bf16[528,256]{1,0:T(8,128)(2,1)}, u32[]{:S(2)}, u32[]{:S(2)}) collective-permute-start(bf16[528,256]{1,0:T(8,128)(2,1)S(1)} %fusion.3.right_one.own), channel_id=1, source_target_pairs={{48,0},{96,48},{144,96},{192,144},{240,192},{288,240},{336,288},{3... | collective-permute-start | bytes 811016 | tf_op jit(solution)/shard_map/ppermute | solution.py:24
  22.6 33.4 %collective-permute-start.1 = (bf16[3104,256]{1,0:T(8,128)(2,1)S(1)}, bf16[3104,256]{1,0:T(8,128)(2,1)S(1)}, u32[]{:S(2)}, u32[]{:S(2)}) collective-permute-start(bf16[3104,256]{1,0:T(8,128)(2,1)S(1)} %get-tuple-element.18.lefts), channel_id=1, source_target_pairs={{6,0},{12,6},{18,12},{24,18},{30,24},{36,30},{42,36},{0,42},{7,1},... | collective-permute-start | bytes 4767752 | tf_op jit(solution)/shard_map/ppermute | solution.py:24
  24.6 31.4 %collective-permute-start = (bf16[1056,256]{1,0:T(8,128)(2,1)}, bf16[1056,256]{1,0:T(8,128)(2,1)}, u32[]{:S(2)}, u32[]{:S(2)}) collective-permute-start(bf16[1056,256]{1,0:T(8,128)(2,1)} %get-tuple-element.17), channel_id=1, source_target_pairs={{96,0},{144,48},{192,96},{240,144},{288,192},{336,240},{384,288},{... | collective-permute-start | bytes 1622024 | tf_op jit(solution)/shard_map/ppermute | solution.py:24
  27.8 36.8 %collective-permute-start.9 = (bf16[1552,256]{1,0:T(8,128)(2,1)}, bf16[1552,256]{1,0:T(8,128)(2,1)}, u32[]{:S(2)}, u32[]{:S(2)}) collective-permute-start(bf16[1552,256]{1,0:T(8,128)(2,1)} %get-tuple-element.28), channel_id=1, source_target_pairs={{12,0},{18,6},{24,12},{30,18},{36,24},{42,30},{0,36},{6,42},{13,1}... | collective-permute-start | bytes 2383880 | tf_op jit(solution)/shard_map/ppermute | solution.py:24
  30.6 25.4 %collective-permute-start.4 = (bf16[528,256]{1,0:T(8,128)(2,1)}, bf16[528,256]{1,0:T(8,128)(2,1)S(1)}, u32[]{:S(2)}, u32[]{:S(2)}) collective-permute-start(bf16[528,256]{1,0:T(8,128)(2,1)} %collective-permute-done.3.one), channel_id=1, source_target_pairs={{96,0},{144,48},{192,96},{240,144},{288,192},{336,240},{384,288},{... | collective-permute-start | bytes 811016 | tf_op jit(solution)/shard_map/ppermute | solution.py:24
  52.7 11.8 %collective-permute-start.8 = (bf16[528,256]{1,0:T(8,128)(2,1)}, bf16[528,256]{1,0:T(8,128)(2,1)S(1)}, u32[]{:S(2)}, u32[]{:S(2)}) collective-permute-start(bf16[528,256]{1,0:T(8,128)(2,1)} %collective-permute-done.2.right_one.one), channel_id=1, source_target_pairs={{96,0},{144,48},{192,96},{240,144},{288,192},{336,240},{384,288},{... | collective-permute-start | bytes 811016 | tf_op jit(solution)/shard_map/ppermute | solution.py:24
  59.0 0.7 copy-start.3
  59.7 15.7 %collective-permute-start.5 = (bf16[384,256]{1,0:T(8,128)(2,1)}, bf16[384,256]{1,0:T(8,128)(2,1)}, u32[]{:S(2)}, u32[]{:S(2)}) collective-permute-start(bf16[384,256]{1,0:T(8,128)(2,1)} %get-tuple-element.23), channel_id=1, source_target_pairs={{0,1},{1,0},{2,3},{3,2},{4,5},{5,4},{6,7},{7,6},{8,9},{9,8},{10,11... | collective-permute-start | bytes 589832 | tf_op jit(solution)/shard_map/ppermute | solution.py:192
  66.9 0.7 copy-start
  67.6 29.2 %all-to-all-start = ((bf16[6,128,256]{2,1,0:T(8,128)(2,1)}), bf16[6,128,256]{2,1,0:T(8,128)(2,1)}, u32[]{:S(2)}, u32[]{:S(2)}) async-start(bf16[6,128,256]{2,1,0:T(8,128)(2,1)} %bitcast.11), calls=%async_computation | async-start | bytes 786432 | tf_op jit(solution)/shard_map/all_to_all | solution.py:201
  75.4 0.9 copy-start.4
  77.3 19.5 %collective-permute-start.6 = (bf16[128,256]{1,0:T(8,128)(2,1)S(1)}, bf16[128,256]{1,0:T(8,128)(2,1)S(1)}, u32[]{:S(2)}, u32[]{:S(2)}) collective-permute-start(bf16[128,256]{1,0:T(8,128)(2,1)S(1)} %get-tuple-element.25), channel_id=1, source_target_pairs={{0,2},{1,3},{2,4},{3,5},{4,0},{5,1},{6,8},{7,9},{8,10},{9,11},{10,... | collective-permute-start | bytes 196616 | tf_op jit(solution)/shard_map/ppermute | solution.py:210
  82.1 14.6 %collective-permute-start.7 = (bf16[128,256]{1,0:T(8,128)(2,1)S(1)}, bf16[128,256]{1,0:T(8,128)(2,1)S(1)}, u32[]{:S(2)}, u32[]{:S(2)}) collective-permute-start(bf16[128,256]{1,0:T(8,128)(2,1)S(1)} %get-tuple-element.26), channel_id=1, source_target_pairs={{0,4},{1,5},{2,0},{3,1},{4,2},{5,3},{6,10},{7,11},{8,6},{9,7},{10,... | collective-permute-start | bytes 196616 | tf_op jit(solution)/shard_map/ppermute | solution.py:210

commit v8 on v6

--- a/solution.py
+++ b/solution.py
@@ -26,30 +26,30 @@
     return lax.ppermute(block, axis, [((i - distance) % size, i) for i in range(size)])
 
 
-def add_term(total, place_ref, left_ref, right_ref):
+def add_term(total, hit_ref, left_ref, right_ref):
     first, second = noted(right_ref, SB)
-    for q, place in enumerate(noted(left_ref, SA)):
-        place_ref[q] = place
-
-    def slot(q, carry):
-        place = place_ref[q]
+    left_places = noted(left_ref, SA)
+    count = jnp.int32(0)
+    for q in range(SA):
+        place = left_places[q]
         inner = lax.rem(place, KT)
-        used = place >= 0
-        hits_first = used & (first == inner)
-        hits_second = used & (second == inner)
-
-        @pl.when(hits_first | hits_second)
+        hits_first = first == inner
+        hit = (place >= 0) & (hits_first | (second == inner))
+
+        @pl.when(hit)
         def _():
-            left_rows = pl.ds(pl.multiple_of(q * TS, TS), TS)
-            right_rows = pl.ds(pl.multiple_of(jnp.where(hits_first, 0, TS), TS), TS)
-            rows = pl.ds(pl.multiple_of((place // KT) * TS, TS), TS)
-            total[rows, :] += jnp.dot(
-                left_ref[left_rows, :], right_ref[right_rows, :], preferred_element_type=jnp.float32
-            )
-
+            hit_ref[0, count] = q * TS
+            hit_ref[1, count] = jnp.where(hits_first, 0, TS)
+            hit_ref[2, count] = (place // KT) * TS
+
+        count = count + hit.astype(jnp.int32)
+
+    def product(n, carry):
+        left_rows, right_rows, rows = (pl.ds(pl.multiple_of(hit_ref[k, n], TS), TS) for k in range(3))
+        total[rows, :] += jnp.dot(left_ref[left_rows, :], right_ref[right_rows, :], preferred_element_type=jnp.float32)
         return carry
 
-    lax.fori_loop(0, SA, slot, 0)
+    lax.fori_loop(0, count, product, 0)
 
 
 def noted(packed_ref, slots):
@@ -66,11 +66,10 @@
     packed_ref[slots * TS :, :] = note.astype(jnp.float32).astype(jnp.bfloat16)
 
 
-def pack_right_kernel(place_ref, right_ref, *pieces):
-    for column, piece in enumerate(pieces):
-        for p in range(SB):
-            piece[p * TS : (p + 1) * TS, :] = right_ref[column, p]
-        write_note(piece, place_ref, column, SB)
+def packed(tiles, places):
+    count = places.shape[0]
+    note = jnp.pad(places.astype(jnp.bfloat16)[None], ((0, NOTE - 1), (0, TS - count)))
+    return jnp.concatenate([tiles.reshape(count * TS, TS), note])
 
 
 def pack_left_kernel(place_ref, left_ref, right_zero, right_one, lefts, left_zero, rights):
@@ -159,7 +158,8 @@
 
 def body(left_tiles, left_place, right_tiles, right_place):
     layer = lax.axis_index("layer").astype(jnp.int32).reshape(1)
-    pieces = call(pack_right_kernel, [array(PIECE, TS)] * HELD, [SMEM, VMEM], (right_place[0, 0], right_tiles[0, 0]))
+    right, right_at = right_tiles[0, 0], right_place[0, 0]
+    pieces = [packed(right[j], right_at[j]) for j in range(HELD)]
     right_one = [shifted(piece, "row", -1) for piece in pieces]
     lefts, left_zero, rights = call(
         pack_left_kernel,
@@ -188,7 +188,7 @@
                 (layer, mark, lefts, left_next, *arriving),
                 [
                     pltpu.VMEM((RT * TS, TS), jnp.float32),
-                    pltpu.SMEM((SA,), jnp.int32),
+                    pltpu.SMEM((3, SA), jnp.int32),
                     pltpu.VMEM((STEPS, PIECE, TS), jnp.bfloat16),
                     pltpu.VMEM((BLOCK, TS), jnp.bfloat16),
                     pltpu.SemaphoreType.DMA((STEPS + 1,)),

time: 97.9 us -> 97.4 us (level)
  local copies, waits for them, and re-layouts: 3.8 us -> 1.2 us
  Pallas kernels: 12.9 us -> 10.7 us
  waiting for transfers between devices: 19.6 us -> 21.4 us
  other arithmetic: 0 us -> 1.42 us
    unnamed x8 -> x4, local copies, waits for them, and re-layouts: 3.8 us -> 0.01 us
    pallas_call x9 -> x8, Pallas kernels: 12.9 us -> 10.7 us  [call(): pl.pallas_call(kernel, out_shape=out_shape, in_specs=in_specs, out_specs=...]
    ppermute x7, waiting for transfers between devices: 16.8 us -> 18.9 us  [shifted(): lax.ppermute(block, axis, [((i - distance) % size, i) for i in range(size)])]
    slice x0 -> x1, local copies, waits for them, and re-layouts: none -> 1.18 us  [body(): pieces = [packed(right[j], right_at[j]) for j in range(HELD)]]
where the time goes in v8:
time: 97.4 us; the launch traced here: 95.6 us
  starting transfers between devices  60.6 us (62%)
  waiting for transfers between devices  21.4 us (22%)
  Pallas kernels  10.7 us (11%)
  other arithmetic  1.42 us (1%)
  local copies, waits for them, and re-layouts  1.2 us (1%)
    ppermute x7, starting transfers between devices, shifted(): lax.ppermute(block, axis, [((i - distance) % size, i) for i in range(size)])  32.3 us
    ppermute x7, waiting for transfers between devices, shifted(): lax.ppermute(block, axis, [((i - distance) % size, i) for i in range(size)])  18.9 us
    ppermute x2, starting transfers between devices, body(): shares[j] = lax.ppermute(far, 'layer', across)  15.4 us
    ppermute x4, starting transfers between devices, body(): lax.ppermute(share, 'layer', trio[turn])  13 us
    pallas_call x8, Pallas kernels, call(): pl.pallas_call(kernel, out_shape=out_shape, in_specs=in_specs, out_specs=...  10.7 us
    ppermute x2, waiting for transfers between devices, body(): shares[j] = lax.ppermute(far, 'layer', across)  2.51 us
  transfers between devices with their start and end apart: 13, of which 2 were waited for; matrix products, arithmetic and copies ran while one was open for 0% of the time, Pallas kernels for 10%

profile of v8, /device:TPU:56, one launch (start us, length us, event | category | flops | bytes accessed | tf_op | source)
XLA Modules:
  0.0 95.6 jit_solution(14091238839530921222)
XLA Ops:
  0.0 0.0 copy-start.1
  0.0 0.0 copy-start
  0.0 1.2 %fusion.4 = (bf16[1,1,1,2,256,256]{5,4,3,2,1,0:T(8,128)(2,1)S(1)}, bf16[1,1,1,2,256,256]{5,4,3,2,1,0:T(8,128)(2,1)S(1)}) fusion(bf16[1,1,2,2,256,256]{5,4,3,2,1,0:T(8,128)(2,1)} %param.6), kind=kLoop, calls=%fused_computation.7 | loop fusion | bytes 1048576 | tf_op jit(solution)/shard_map/slice | solution.py:162
  1.2 0.7 convert.4
  1.9 0.7 fusion.2.right_zero.refs_0_
  2.6 15.9 %collective-permute-start.3 = (bf16[528,256]{1,0:T(8,128)(2,1)}, bf16[528,256]{1,0:T(8,128)(2,1)}, u32[]{:S(2)}, u32[]{:S(2)}) collective-permute-start(bf16[528,256]{1,0:T(8,128)(2,1)} %fusion.2.right_zero.refs_0_), channel_id=1, source_target_pairs={{48,0},{96,48},{144,96},{192,144},{240,192},{288,240},{336,288},{3... | collective-permute-start | bytes 811016 | tf_op jit(solution)/shard_map/ppermute | solution.py:26
  18.6 1.9 %collective-permute-start.2 = (bf16[528,256]{1,0:T(8,128)(2,1)S(1)}, bf16[528,256]{1,0:T(8,128)(2,1)}, u32[]{:S(2)}, u32[]{:S(2)}) collective-permute-start(bf16[528,256]{1,0:T(8,128)(2,1)S(1)} %fusion.3.right_one.refs_0_), channel_id=1, source_target_pairs={{48,0},{96,48},{144,96},{192,144},{240,192},{288,240},{336,288},{3... | collective-permute-start | bytes 811016 | tf_op jit(solution)/shard_map/ppermute | solution.py:26
  20.5 0.0 copy-done.1
  20.5 0.0 copy-done
  20.5 2.1 %shard_map.46 = (bf16[3104,256]{1,0:T(8,128)(2,1)S(1)}, bf16[1552,256]{1,0:T(8,128)(2,1)}, bf16[1056,256]{1,0:T(8,128)(2,1)}) custom-call(s32[2,6]{1,0:T(2,128)S(1)} %bitcast.10, bf16[2,6,256,256]{3,2,1,0:T(8,128)(2,1)S(1)} %bitcast.9, bf16[528,256]{1,0:T(8,128)(2,1)} %fusion.2.right_zero.refs_0_, bf16[528,256]{1,0:T(8,128)(2,1)S(1)} %fusion.3.right_one.refs_0_), custom_call_target="tpu_custom_call" | custom-call | tf_op jit(solution)/shard_map/pallas_call | solution.py:144
  22.6 1.9 %collective-permute-start.1 = (bf16[3104,256]{1,0:T(8,128)(2,1)S(1)}, bf16[3104,256]{1,0:T(8,128)(2,1)S(1)}, u32[]{:S(2)}, u32[]{:S(2)}) collective-permute-start(bf16[3104,256]{1,0:T(8,128)(2,1)S(1)} %get-tuple-element.29.lefts), channel_id=1, source_target_pairs={{6,0},{12,6},{18,12},{24,18},{30,24},{36,30},{42,36},{0,42},{7,1},... | collective-permute-start | bytes 4767752 | tf_op jit(solution)/shard_map/ppermute | solution.py:26
  24.6 3.2 %collective-permute-start = (bf16[1056,256]{1,0:T(8,128)(2,1)}, bf16[1056,256]{1,0:T(8,128)(2,1)}, u32[]{:S(2)}, u32[]{:S(2)}) collective-permute-start(bf16[1056,256]{1,0:T(8,128)(2,1)} %get-tuple-element.28), channel_id=1, source_target_pairs={{96,0},{144,48},{192,96},{240,144},{288,192},{336,240},{384,288},{... | collective-permute-start | bytes 1622024 | tf_op jit(solution)/shard_map/ppermute | solution.py:26
  27.8 2.8 %collective-permute-start.6 = (bf16[1552,256]{1,0:T(8,128)(2,1)}, bf16[1552,256]{1,0:T(8,128)(2,1)}, u32[]{:S(2)}, u32[]{:S(2)}) collective-permute-start(bf16[1552,256]{1,0:T(8,128)(2,1)} %get-tuple-element.37), channel_id=1, source_target_pairs={{12,0},{18,6},{24,12},{30,18},{36,24},{42,30},{0,36},{6,42},{13,1}... | collective-permute-start | bytes 2383880 | tf_op jit(solution)/shard_map/ppermute | solution.py:26
  30.6 0.0 collective-permute-done.3.refs_1_
  30.6 3.3 %collective-permute-start.4 = (bf16[528,256]{1,0:T(8,128)(2,1)}, bf16[528,256]{1,0:T(8,128)(2,1)S(1)}, u32[]{:S(2)}, u32[]{:S(2)}) collective-permute-start(bf16[528,256]{1,0:T(8,128)(2,1)} %collective-permute-done.3.refs_1_), channel_id=1, source_target_pairs={{96,0},{144,48},{192,96},{240,144},{288,192},{336,240},{384,288},{... | collective-permute-start | bytes 811016 | tf_op jit(solution)/shard_map/ppermute | solution.py:26
  33.9 18.9 %collective-permute-done.2.right_one.refs_1_ = bf16[528,256]{1,0:T(8,128)(2,1)} collective-permute-done((bf16[528,256]{1,0:T(8,128)(2,1)S(1)}, bf16[528,256]{1,0:T(8,128)(2,1)}, u32[]{:S(2)}, u32[]{:S(2)}) %collective-permute-start.2) | collective-permute-done | bytes 270368 | tf_op jit(solution)/shard_map/ppermute | solution.py:26
  52.7 3.2 %collective-permute-start.5 = (bf16[528,256]{1,0:T(8,128)(2,1)}, bf16[528,256]{1,0:T(8,128)(2,1)S(1)}, u32[]{:S(2)}, u32[]{:S(2)}) collective-permute-start(bf16[528,256]{1,0:T(8,128)(2,1)} %collective-permute-done.2.right_one.refs_1_), channel_id=1, source_target_pairs={{96,0},{144,48},{192,96},{240,144},{288,192},{336,240},{384,288},{... | collective-permute-start | bytes 811016 | tf_op jit(solution)/shard_map/ppermute | solution.py:26
  56.0 0.0 collective-permute-done.refs_2_
  56.0 0.0 collective-permute-done.1.left_next
  56.0 0.0 collective-permute-done.4.refs_3_
  56.0 2.3 %shard_map.48 = (bf16[256,256]{1,0:T(8,128)(2,1)S(1)}, bf16[256,256]{1,0:T(8,128)(2,1)S(1)}, bf16[256,256]{1,0:T(8,128)(2,1)S(1)}) custom-call(s32[1]{0:T(128)} %bitcast.layer, f32[8,128]{1,0:T(8,128)S(1)} %shard_map.47.mark, bf16[3104,256]{1,0:T(8,128)(2,1)S(1)} %get-tuple-element.29.lefts, bf16[3104,256]{1,0:T(8,128)(2,1)S(1)} %collective-permute-done.1.left_next, ...), custom_call_target="tpu_custom_call" | custom-call | tf_op jit(solution)/shard_map/pallas_call | solution.py:144
  58.3 1.9 %collective-permute-start.10 = (bf16[256,256]{1,0:T(8,128)(2,1)S(1)}, bf16[256,256]{1,0:T(8,128)(2,1)S(1)}, u32[]{:S(2)}, u32[]{:S(2)}) collective-permute-start(bf16[256,256]{1,0:T(8,128)(2,1)S(1)} %get-tuple-element.42), channel_id=1, source_target_pairs={{0,2},{1,0},{2,1},{3,5},{4,3},{5,4},{6,8},{7,6},{8,7},{9,11},{10,9... | collective-permute-start | bytes 393224 | tf_op jit(solution)/shard_map/ppermute | solution.py:200
  60.3 4.3 %collective-permute-start.9 = (bf16[256,256]{1,0:T(8,128)(2,1)S(1)}, bf16[256,256]{1,0:T(8,128)(2,1)S(1)}, u32[]{:S(2)}, u32[]{:S(2)}) collective-permute-start(bf16[256,256]{1,0:T(8,128)(2,1)S(1)} %get-tuple-element.41), channel_id=1, source_target_pairs={{0,1},{1,2},{2,0},{3,4},{4,5},{5,3},{6,7},{7,8},{8,6},{9,10},{10,1... | collective-permute-start | bytes 393224 | tf_op jit(solution)/shard_map/ppermute | solution.py:200
  64.6 0.0 collective-permute-done.5.refs_3_
  64.6 0.0 collective-permute-done.6.refs_4_
  64.6 3.1 %shard_map.49 = (bf16[256,256]{1,0:T(8,128)(2,1)S(1)}, bf16[256,256]{1,0:T(8,128)(2,1)}, bf16[256,256]{1,0:T(8,128)(2,1)}) custom-call(s32[1]{0:T(128)} %bitcast.layer, f32[8,128]{1,0:T(8,128)S(1)} %shard_map.47.mark, bf16[3104,256]{1,0:T(8,128)(2,1)S(1)} %get-tuple-element.29.lefts, bf16[3104,256]{1,0:T(8,128)(2,1)S(1)} %collective-permute-done.1.left_next, ...), custom_call_target="tpu_custom_call" | custom-call | tf_op jit(solution)/shard_map/pallas_call | solution.py:144
  67.7 3.4 %collective-permute-start.7 = (bf16[256,256]{1,0:T(8,128)(2,1)}, bf16[256,256]{1,0:T(8,128)(2,1)}, u32[]{:S(2)}, u32[]{:S(2)}) collective-permute-start(bf16[256,256]{1,0:T(8,128)(2,1)} %get-tuple-element.38), channel_id=1, source_target_pairs={{0,1},{1,2},{2,0},{3,4},{4,5},{5,3},{6,7},{7,8},{8,6},{9,10},{10,1... | collective-permute-start | bytes 393224 | tf_op jit(solution)/shard_map/ppermute | solution.py:200
  71.0 3.4 %collective-permute-start.8 = (bf16[256,256]{1,0:T(8,128)(2,1)}, bf16[256,256]{1,0:T(8,128)(2,1)}, u32[]{:S(2)}, u32[]{:S(2)}) collective-permute-start(bf16[256,256]{1,0:T(8,128)(2,1)} %get-tuple-element.39), channel_id=1, source_target_pairs={{0,2},{1,0},{2,1},{3,5},{4,3},{5,4},{6,8},{7,6},{8,7},{9,11},{10,9... | collective-permute-start | bytes 393224 | tf_op jit(solution)/shard_map/ppermute | solution.py:200
  74.4 0.0 collective-permute-done.10.two
  74.4 0.0 collective-permute-done.9.one
  74.5 0.1 shard_map.50
  74.5 9.3 %collective-permute-start.11 = (bf16[128,256]{1,0:T(8,128)(2,1)S(1)}, bf16[128,256]{1,0:T(8,128)(2,1)S(1)}, u32[]{:S(2)}, u32[]{:S(2)}) collective-permute-start(bf16[128,256]{1,0:T(8,128)(2,1)S(1)} %get-tuple-element.45), channel_id=1, source_target_pairs={{0,3},{1,4},{2,5},{3,0},{4,1},{5,2},{6,9},{7,10},{8,11},{9,6},{10,... | collective-permute-start | bytes 196616 | tf_op jit(solution)/shard_map/ppermute | solution.py:211
  83.8 0.0 collective-permute-done.7.one
  83.9 0.0 collective-permute-done.8.two
  83.9 1.6 %shard_map.52 = (f32[128,256]{1,0:T(8,128)S(1)}, bf16[128,256]{1,0:T(8,128)(2,1)}) custom-call(bf16[256,256]{1,0:T(8,128)(2,1)S(1)} %get-tuple-element.46.own, bf16[256,256]{1,0:T(8,128)(2,1)} %collective-permute-done.7.one, bf16[256,256]{1,0:T(8,128)(2,1)} %collective-permute-done.8.two), custom_call_target="tpu_custom_call" | custom-call | tf_op jit(solution)/shard_map/pallas_call | solution.py:144
  85.5 6.0 %collective-permute-start.12 = (bf16[128,256]{1,0:T(8,128)(2,1)}, bf16[128,256]{1,0:T(8,128)(2,1)}, u32[]{:S(2)}, u32[]{:S(2)}) collective-permute-start(bf16[128,256]{1,0:T(8,128)(2,1)} %get-tuple-element.50), channel_id=1, source_target_pairs={{0,3},{1,4},{2,5},{3,0},{4,1},{5,2},{6,9},{7,10},{8,11},{9,6},{10,... | collective-permute-start | bytes 196616 | tf_op jit(solution)/shard_map/ppermute | solution.py:211
  91.5 0.0 collective-permute-done.11.far
  91.6 2.5 %collective-permute-done.12.far = bf16[128,256]{1,0:T(8,128)(2,1)} collective-permute-done((bf16[128,256]{1,0:T(8,128)(2,1)}, bf16[128,256]{1,0:T(8,128)(2,1)}, u32[]{:S(2)}, u32[]{:S(2)}) %collective-permute-start.12) | collective-permute-done | bytes 65568 | tf_op jit(solution)/shard_map/ppermute | solution.py:211
  94.1 1.5 %shard_map.53 = bf16[128,512]{1,0:T(8,128)(2,1)} custom-call(bf16[128,256]{1,0:T(8,128)(2,1)S(1)} %shard_map.51.first, f32[128,256]{1,0:T(8,128)S(1)} %get-tuple-element.49.near, bf16[128,256]{1,0:T(8,128)(2,1)} %collective-permute-done.12.far), custom_call_target="tpu_custom_call" | custom-call | tf_op jit(solution)/shard_map/pallas_call | solution.py:144
  (4 shorter events, 0.0 us)
Async XLA Ops:
  0.0 20.5 %copy-start.1 = (s32[1,1,2,6]{3,2,1,0:T(2,128)S(1)}, s32[1,1,2,6]{3,2,1,0:T(2,128)}, u32[]{:S(2)}) copy-start(s32[1,1,2,6]{3,2,1,0:T(2,128)} %param.5) | copy-start | bytes 148
  0.0 20.5 %copy-start = (bf16[1,1,2,6,256,256]{5,4,3,2,1,0:T(8,128)(2,1)S(1)}, bf16[1,1,2,6,256,256]{5,4,3,2,1,0:T(8,128)(2,1)}, u32[]{:S(2)}) copy-start(bf16[1,1,2,6,256,256]{5,4,3,2,1,0:T(8,128)(2,1)} %param.4) | copy-start | bytes 4718596
  2.6 28.0 %collective-permute-start.3 = (bf16[528,256]{1,0:T(8,128)(2,1)}, bf16[528,256]{1,0:T(8,128)(2,1)}, u32[]{:S(2)}, u32[]{:S(2)}) collective-permute-start(bf16[528,256]{1,0:T(8,128)(2,1)} %fusion.2.right_zero.refs_0_), channel_id=1, source_target_pairs={{48,0},{96,48},{144,96},{192,144},{240,192},{288,240},{336,288},{3... | collective-permute-start | bytes 811016 | tf_op jit(solution)/shard_map/ppermute | solution.py:26
  18.6 34.2 %collective-permute-start.2 = (bf16[528,256]{1,0:T(8,128)(2,1)S(1)}, bf16[528,256]{1,0:T(8,128)(2,1)}, u32[]{:S(2)}, u32[]{:S(2)}) collective-permute-start(bf16[528,256]{1,0:T(8,128)(2,1)S(1)} %fusion.3.right_one.refs_0_), channel_id=1, source_target_pairs={{48,0},{96,48},{144,96},{192,144},{240,192},{288,240},{336,288},{3... | collective-permute-start | bytes 811016 | tf_op jit(solution)/shard_map/ppermute | solution.py:26
  22.6 33.4 %collective-permute-start.1 = (bf16[3104,256]{1,0:T(8,128)(2,1)S(1)}, bf16[3104,256]{1,0:T(8,128)(2,1)S(1)}, u32[]{:S(2)}, u32[]{:S(2)}) collective-permute-start(bf16[3104,256]{1,0:T(8,128)(2,1)S(1)} %get-tuple-element.29.lefts), channel_id=1, source_target_pairs={{6,0},{12,6},{18,12},{24,18},{30,24},{36,30},{42,36},{0,42},{7,1},... | collective-permute-start | bytes 4767752 | tf_op jit(solution)/shard_map/ppermute | solution.py:26
  24.6 31.4 %collective-permute-start = (bf16[1056,256]{1,0:T(8,128)(2,1)}, bf16[1056,256]{1,0:T(8,128)(2,1)}, u32[]{:S(2)}, u32[]{:S(2)}) collective-permute-start(bf16[1056,256]{1,0:T(8,128)(2,1)} %get-tuple-element.28), channel_id=1, source_target_pairs={{96,0},{144,48},{192,96},{240,144},{288,192},{336,240},{384,288},{... | collective-permute-start | bytes 1622024 | tf_op jit(solution)/shard_map/ppermute | solution.py:26
  27.8 36.8 %collective-permute-start.6 = (bf16[1552,256]{1,0:T(8,128)(2,1)}, bf16[1552,256]{1,0:T(8,128)(2,1)}, u32[]{:S(2)}, u32[]{:S(2)}) collective-permute-start(bf16[1552,256]{1,0:T(8,128)(2,1)} %get-tuple-element.37), channel_id=1, source_target_pairs={{12,0},{18,6},{24,12},{30,18},{36,24},{42,30},{0,36},{6,42},{13,1}... | collective-permute-start | bytes 2383880 | tf_op jit(solution)/shard_map/ppermute | solution.py:26
  30.6 25.4 %collective-permute-start.4 = (bf16[528,256]{1,0:T(8,128)(2,1)}, bf16[528,256]{1,0:T(8,128)(2,1)S(1)}, u32[]{:S(2)}, u32[]{:S(2)}) collective-permute-start(bf16[528,256]{1,0:T(8,128)(2,1)} %collective-permute-done.3.refs_1_), channel_id=1, source_target_pairs={{96,0},{144,48},{192,96},{240,144},{288,192},{336,240},{384,288},{... | collective-permute-start | bytes 811016 | tf_op jit(solution)/shard_map/ppermute | solution.py:26
  52.7 11.9 %collective-permute-start.5 = (bf16[528,256]{1,0:T(8,128)(2,1)}, bf16[528,256]{1,0:T(8,128)(2,1)S(1)}, u32[]{:S(2)}, u32[]{:S(2)}) collective-permute-start(bf16[528,256]{1,0:T(8,128)(2,1)} %collective-permute-done.2.right_one.refs_1_), channel_id=1, source_target_pairs={{96,0},{144,48},{192,96},{240,144},{288,192},{336,240},{384,288},{... | collective-permute-start | bytes 811016 | tf_op jit(solution)/shard_map/ppermute | solution.py:26
  58.3 16.1 %collective-permute-start.10 = (bf16[256,256]{1,0:T(8,128)(2,1)S(1)}, bf16[256,256]{1,0:T(8,128)(2,1)S(1)}, u32[]{:S(2)}, u32[]{:S(2)}) collective-permute-start(bf16[256,256]{1,0:T(8,128)(2,1)S(1)} %get-tuple-element.42), channel_id=1, source_target_pairs={{0,2},{1,0},{2,1},{3,5},{4,3},{5,4},{6,8},{7,6},{8,7},{9,11},{10,9... | collective-permute-start | bytes 393224 | tf_op jit(solution)/shard_map/ppermute | solution.py:200
  60.3 14.2 %collective-permute-start.9 = (bf16[256,256]{1,0:T(8,128)(2,1)S(1)}, bf16[256,256]{1,0:T(8,128)(2,1)S(1)}, u32[]{:S(2)}, u32[]{:S(2)}) collective-permute-start(bf16[256,256]{1,0:T(8,128)(2,1)S(1)} %get-tuple-element.41), channel_id=1, source_target_pairs={{0,1},{1,2},{2,0},{3,4},{4,5},{5,3},{6,7},{7,8},{8,6},{9,10},{10,1... | collective-permute-start | bytes 393224 | tf_op jit(solution)/shard_map/ppermute | solution.py:200
  67.7 16.2 %collective-permute-start.7 = (bf16[256,256]{1,0:T(8,128)(2,1)}, bf16[256,256]{1,0:T(8,128)(2,1)}, u32[]{:S(2)}, u32[]{:S(2)}) collective-permute-start(bf16[256,256]{1,0:T(8,128)(2,1)} %get-tuple-element.38), channel_id=1, source_target_pairs={{0,1},{1,2},{2,0},{3,4},{4,5},{5,3},{6,7},{7,8},{8,6},{9,10},{10,1... | collective-permute-start | bytes 393224 | tf_op jit(solution)/shard_map/ppermute | solution.py:200
  71.0 12.8 %collective-permute-start.8 = (bf16[256,256]{1,0:T(8,128)(2,1)}, bf16[256,256]{1,0:T(8,128)(2,1)}, u32[]{:S(2)}, u32[]{:S(2)}) collective-permute-start(bf16[256,256]{1,0:T(8,128)(2,1)} %get-tuple-element.39), channel_id=1, source_target_pairs={{0,2},{1,0},{2,1},{3,5},{4,3},{5,4},{6,8},{7,6},{8,7},{9,11},{10,9... | collective-permute-start | bytes 393224 | tf_op jit(solution)/shard_map/ppermute | solution.py:200
  74.5 17.0 %collective-permute-start.11 = (bf16[128,256]{1,0:T(8,128)(2,1)S(1)}, bf16[128,256]{1,0:T(8,128)(2,1)S(1)}, u32[]{:S(2)}, u32[]{:S(2)}) collective-permute-start(bf16[128,256]{1,0:T(8,128)(2,1)S(1)} %get-tuple-element.45), channel_id=1, source_target_pairs={{0,3},{1,4},{2,5},{3,0},{4,1},{5,2},{6,9},{7,10},{8,11},{9,6},{10,... | collective-permute-start | bytes 196616 | tf_op jit(solution)/shard_map/ppermute | solution.py:211
  85.5 8.6 %collective-permute-start.12 = (bf16[128,256]{1,0:T(8,128)(2,1)}, bf16[128,256]{1,0:T(8,128)(2,1)}, u32[]{:S(2)}, u32[]{:S(2)}) collective-permute-start(bf16[128,256]{1,0:T(8,128)(2,1)} %get-tuple-element.50), channel_id=1, source_target_pairs={{0,3},{1,4},{2,5},{3,0},{4,1},{5,2},{6,9},{7,10},{8,11},{9,6},{10,... | collective-permute-start | bytes 196616 | tf_op jit(solution)/shard_map/ppermute | solution.py:211

commit v9 on v8

--- a/solution.py
+++ b/solution.py
@@ -130,9 +130,9 @@
     total_kernel(near, far, out_ref.at[:, TS:])
 
 
-AHEAD = 4 * 10**10
-GATHER = 10**12
-FIRST = 10**12
+AHEAD = 2 * 10**10
+GATHER = 3 * 10**9
+FIRST = 3 * 10**9
 AFTER = 0
 SMEM = pl.BlockSpec(memory_space=pltpu.SMEM)
 VMEM = pl.BlockSpec(memory_space=pltpu.VMEM)

time: 97.4 us -> 93.5 us (0.960)
  the two profiles are of different devices: /device:TPU:56 before, /device:TPU:26 now
where the time goes in v9:
time: 93.5 us; the launch traced here: 92 us
  starting transfers between devices  66.9 us (72%)
  waiting for transfers between devices  15.2 us (16%)
  Pallas kernels  7.05 us (8%)
  other arithmetic  1.42 us (2%)
  local copies, waits for them, and re-layouts  1.2 us (1%)
    ppermute x7, starting transfers between devices, shifted(): lax.ppermute(block, axis, [((i - distance) % size, i) for i in range(size)])  30.5 us
    ppermute x4, starting transfers between devices, body(): lax.ppermute(share, 'layer', trio[turn])  19.6 us
    ppermute x2, starting transfers between devices, body(): shares[j] = lax.ppermute(far, 'layer', across)  16.8 us
    ppermute x7, waiting for transfers between devices, shifted(): lax.ppermute(block, axis, [((i - distance) % size, i) for i in range(size)])  13 us
    pallas_call x8, Pallas kernels, call(): pl.pallas_call(kernel, out_shape=out_shape, in_specs=in_specs, out_specs=...  7.05 us
    ppermute x2, waiting for transfers between devices, body(): shares[j] = lax.ppermute(far, 'layer', across)  2.2 us
  transfers between devices with their start and end apart: 13, of which 4 were waited for; matrix products, arithmetic and copies ran while one was open for 0% of the time, Pallas kernels for 7%

profile of v9, /device:TPU:26, one launch (start us, length us, event | category | flops | bytes accessed | tf_op | source)
XLA Modules:
  0.0 92.0 jit_solution(1827894556115668094)
XLA Ops:
  0.0 0.0 copy-start.1
  0.0 0.0 copy-start
  0.0 1.2 %fusion.4 = (bf16[1,1,1,2,256,256]{5,4,3,2,1,0:T(8,128)(2,1)S(1)}, bf16[1,1,1,2,256,256]{5,4,3,2,1,0:T(8,128)(2,1)S(1)}) fusion(bf16[1,1,2,2,256,256]{5,4,3,2,1,0:T(8,128)(2,1)} %param.6), kind=kLoop, calls=%fused_computation.7 | loop fusion | bytes 1048576 | tf_op jit(solution)/shard_map/slice | solution.py:162
  1.2 0.7 convert.4
  1.9 0.7 fusion.2.right_zero.refs_0_
  2.6 15.0 %collective-permute-start.3 = (bf16[528,256]{1,0:T(8,128)(2,1)}, bf16[528,256]{1,0:T(8,128)(2,1)}, u32[]{:S(2)}, u32[]{:S(2)}) collective-permute-start(bf16[528,256]{1,0:T(8,128)(2,1)} %fusion.2.right_zero.refs_0_), channel_id=1, source_target_pairs={{48,0},{96,48},{144,96},{192,144},{240,192},{288,240},{336,288},{3... | collective-permute-start | bytes 811016 | tf_op jit(solution)/shard_map/ppermute | solution.py:26
  17.7 1.9 %collective-permute-start.2 = (bf16[528,256]{1,0:T(8,128)(2,1)S(1)}, bf16[528,256]{1,0:T(8,128)(2,1)}, u32[]{:S(2)}, u32[]{:S(2)}) collective-permute-start(bf16[528,256]{1,0:T(8,128)(2,1)S(1)} %fusion.3.right_one.refs_0_), channel_id=1, source_target_pairs={{48,0},{96,48},{144,96},{192,144},{240,192},{288,240},{336,288},{3... | collective-permute-start | bytes 811016 | tf_op jit(solution)/shard_map/ppermute | solution.py:26
  19.6 0.0 copy-done.1
  19.6 0.0 copy-done
  19.6 2.1 %shard_map.46 = (bf16[3104,256]{1,0:T(8,128)(2,1)S(1)}, bf16[1552,256]{1,0:T(8,128)(2,1)}, bf16[1056,256]{1,0:T(8,128)(2,1)}) custom-call(s32[2,6]{1,0:T(2,128)S(1)} %bitcast.10, bf16[2,6,256,256]{3,2,1,0:T(8,128)(2,1)S(1)} %bitcast.9, bf16[528,256]{1,0:T(8,128)(2,1)} %fusion.2.right_zero.refs_0_, bf16[528,256]{1,0:T(8,128)(2,1)S(1)} %fusion.3.right_one.refs_0_), custom_call_target="tpu_custom_call" | custom-call | tf_op jit(solution)/shard_map/pallas_call | solution.py:144
  21.7 0.0 collective-permute-start.1
  21.7 2.3 %collective-permute-start = (bf16[1056,256]{1,0:T(8,128)(2,1)}, bf16[1056,256]{1,0:T(8,128)(2,1)}, u32[]{:S(2)}, u32[]{:S(2)}) collective-permute-start(bf16[1056,256]{1,0:T(8,128)(2,1)} %get-tuple-element.28), channel_id=1, source_target_pairs={{96,0},{144,48},{192,96},{240,144},{288,192},{336,240},{384,288},{... | collective-permute-start | bytes 1622024 | tf_op jit(solution)/shard_map/ppermute | solution.py:26
  24.1 4.4 %collective-permute-start.6 = (bf16[1552,256]{1,0:T(8,128)(2,1)}, bf16[1552,256]{1,0:T(8,128)(2,1)}, u32[]{:S(2)}, u32[]{:S(2)}) collective-permute-start(bf16[1552,256]{1,0:T(8,128)(2,1)} %get-tuple-element.37), channel_id=1, source_target_pairs={{12,0},{18,6},{24,12},{30,18},{36,24},{42,30},{0,36},{6,42},{13,1}... | collective-permute-start | bytes 2383880 | tf_op jit(solution)/shard_map/ppermute | solution.py:26
  28.5 0.0 collective-permute-done.3.refs_1_
  28.5 4.5 %collective-permute-start.4 = (bf16[528,256]{1,0:T(8,128)(2,1)}, bf16[528,256]{1,0:T(8,128)(2,1)S(1)}, u32[]{:S(2)}, u32[]{:S(2)}) collective-permute-start(bf16[528,256]{1,0:T(8,128)(2,1)} %collective-permute-done.3.refs_1_), channel_id=1, source_target_pairs={{96,0},{144,48},{192,96},{240,144},{288,192},{336,240},{384,288},{... | collective-permute-start | bytes 811016 | tf_op jit(solution)/shard_map/ppermute | solution.py:26
  33.0 4.7 %collective-permute-done.2.right_one.refs_1_ = bf16[528,256]{1,0:T(8,128)(2,1)} collective-permute-done((bf16[528,256]{1,0:T(8,128)(2,1)S(1)}, bf16[528,256]{1,0:T(8,128)(2,1)}, u32[]{:S(2)}, u32[]{:S(2)}) %collective-permute-start.2) | collective-permute-done | bytes 270368 | tf_op jit(solution)/shard_map/ppermute | solution.py:26
  37.8 2.3 %collective-permute-start.5 = (bf16[528,256]{1,0:T(8,128)(2,1)}, bf16[528,256]{1,0:T(8,128)(2,1)S(1)}, u32[]{:S(2)}, u32[]{:S(2)}) collective-permute-start(bf16[528,256]{1,0:T(8,128)(2,1)} %collective-permute-done.2.right_one.refs_1_), channel_id=1, source_target_pairs={{96,0},{144,48},{192,96},{240,144},{288,192},{336,240},{384,288},{... | collective-permute-start | bytes 811016 | tf_op jit(solution)/shard_map/ppermute | solution.py:26
  40.1 0.1 collective-permute-done.refs_2_
  40.2 8.1 %collective-permute-done.1.left_next = bf16[3104,256]{1,0:T(8,128)(2,1)S(1)} collective-permute-done((bf16[3104,256]{1,0:T(8,128)(2,1)S(1)}, bf16[3104,256]{1,0:T(8,128)(2,1)S(1)}, u32[]{:S(2)}, u32[]{:S(2)}) %collective-permute-start.1) | collective-permute-done | bytes 1589280 | tf_op jit(solution)/shard_map/ppermute | solution.py:26
  48.4 0.0 collective-permute-done.4.refs_3_
  48.4 2.5 %shard_map.48 = (bf16[256,256]{1,0:T(8,128)(2,1)S(1)}, bf16[256,256]{1,0:T(8,128)(2,1)S(1)}, bf16[256,256]{1,0:T(8,128)(2,1)S(1)}) custom-call(s32[1]{0:T(128)} %bitcast.layer, f32[8,128]{1,0:T(8,128)S(1)} %shard_map.47.mark, bf16[3104,256]{1,0:T(8,128)(2,1)S(1)} %get-tuple-element.29.lefts, bf16[3104,256]{1,0:T(8,128)(2,1)S(1)} %collective-permute-done.1.left_next, ...), custom_call_target="tpu_custom_call" | custom-call | tf_op jit(solution)/shard_map/pallas_call | solution.py:144
  50.9 3.3 %collective-permute-start.10 = (bf16[256,256]{1,0:T(8,128)(2,1)S(1)}, bf16[256,256]{1,0:T(8,128)(2,1)S(1)}, u32[]{:S(2)}, u32[]{:S(2)}) collective-permute-start(bf16[256,256]{1,0:T(8,128)(2,1)S(1)} %get-tuple-element.42), channel_id=1, source_target_pairs={{0,2},{1,0},{2,1},{3,5},{4,3},{5,4},{6,8},{7,6},{8,7},{9,11},{10,9... | collective-permute-start | bytes 393224 | tf_op jit(solution)/shard_map/ppermute | solution.py:200
  54.2 9.6 %collective-permute-start.9 = (bf16[256,256]{1,0:T(8,128)(2,1)S(1)}, bf16[256,256]{1,0:T(8,128)(2,1)S(1)}, u32[]{:S(2)}, u32[]{:S(2)}) collective-permute-start(bf16[256,256]{1,0:T(8,128)(2,1)S(1)} %get-tuple-element.41), channel_id=1, source_target_pairs={{0,1},{1,2},{2,0},{3,4},{4,5},{5,3},{6,7},{7,8},{8,6},{9,10},{10,1... | collective-permute-start | bytes 393224 | tf_op jit(solution)/shard_map/ppermute | solution.py:200
  63.8 0.0 collective-permute-done.5.refs_3_
  63.8 0.0 collective-permute-done.6.refs_4_
  63.8 1.6 %shard_map.49 = (bf16[256,256]{1,0:T(8,128)(2,1)S(1)}, bf16[256,256]{1,0:T(8,128)(2,1)S(1)}, bf16[256,256]{1,0:T(8,128)(2,1)S(1)}) custom-call(s32[1]{0:T(128)} %bitcast.layer, f32[8,128]{1,0:T(8,128)S(1)} %shard_map.47.mark, bf16[3104,256]{1,0:T(8,128)(2,1)S(1)} %get-tuple-element.29.lefts, bf16[3104,256]{1,0:T(8,128)(2,1)S(1)} %collective-permute-done.1.left_next, ...), custom_call_target="tpu_custom_call" | custom-call | tf_op jit(solution)/shard_map/pallas_call | solution.py:144
  65.4 4.3 %collective-permute-start.7 = (bf16[256,256]{1,0:T(8,128)(2,1)S(1)}, bf16[256,256]{1,0:T(8,128)(2,1)S(1)}, u32[]{:S(2)}, u32[]{:S(2)}) collective-permute-start(bf16[256,256]{1,0:T(8,128)(2,1)S(1)} %get-tuple-element.38), channel_id=1, source_target_pairs={{0,1},{1,2},{2,0},{3,4},{4,5},{5,3},{6,7},{7,8},{8,6},{9,10},{10,1... | collective-permute-start | bytes 393224 | tf_op jit(solution)/shard_map/ppermute | solution.py:200
  69.8 2.4 %collective-permute-start.8 = (bf16[256,256]{1,0:T(8,128)(2,1)S(1)}, bf16[256,256]{1,0:T(8,128)(2,1)S(1)}, u32[]{:S(2)}, u32[]{:S(2)}) collective-permute-start(bf16[256,256]{1,0:T(8,128)(2,1)S(1)} %get-tuple-element.39), channel_id=1, source_target_pairs={{0,2},{1,0},{2,1},{3,5},{4,3},{5,4},{6,8},{7,6},{8,7},{9,11},{10,9... | collective-permute-start | bytes 393224 | tf_op jit(solution)/shard_map/ppermute | solution.py:200
  72.2 0.0 collective-permute-done.10.two
  72.2 0.0 collective-permute-done.9.one
  72.2 0.1 shard_map.50
  72.2 10.7 %collective-permute-start.11 = (bf16[128,256]{1,0:T(8,128)(2,1)S(1)}, bf16[128,256]{1,0:T(8,128)(2,1)S(1)}, u32[]{:S(2)}, u32[]{:S(2)}) collective-permute-start(bf16[128,256]{1,0:T(8,128)(2,1)S(1)} %get-tuple-element.45), channel_id=1, source_target_pairs={{0,3},{1,4},{2,5},{3,0},{4,1},{5,2},{6,9},{7,10},{8,11},{9,6},{10,... | collective-permute-start | bytes 196616 | tf_op jit(solution)/shard_map/ppermute | solution.py:211
  83.0 0.0 collective-permute-done.7.one
  83.0 0.0 collective-permute-done.8.two
  83.0 0.1 shard_map.52
  83.0 6.0 %collective-permute-start.12 = (bf16[128,256]{1,0:T(8,128)(2,1)S(1)}, bf16[128,256]{1,0:T(8,128)(2,1)S(1)}, u32[]{:S(2)}, u32[]{:S(2)}) collective-permute-start(bf16[128,256]{1,0:T(8,128)(2,1)S(1)} %get-tuple-element.50), channel_id=1, source_target_pairs={{0,3},{1,4},{2,5},{3,0},{4,1},{5,2},{6,9},{7,10},{8,11},{9,6},{10,... | collective-permute-start | bytes 196616 | tf_op jit(solution)/shard_map/ppermute | solution.py:211
  89.1 0.0 collective-permute-done.11.far
  89.1 2.2 %collective-permute-done.12.far = bf16[128,256]{1,0:T(8,128)(2,1)S(1)} collective-permute-done((bf16[128,256]{1,0:T(8,128)(2,1)S(1)}, bf16[128,256]{1,0:T(8,128)(2,1)S(1)}, u32[]{:S(2)}, u32[]{:S(2)}) %collective-permute-start.12) | collective-permute-done | bytes 65568 | tf_op jit(solution)/shard_map/ppermute | solution.py:211
  91.3 0.7 shard_map.53
  (4 shorter events, 0.0 us)
Async XLA Ops:
  0.0 19.6 %copy-start.1 = (s32[1,1,2,6]{3,2,1,0:T(2,128)S(1)}, s32[1,1,2,6]{3,2,1,0:T(2,128)}, u32[]{:S(2)}) copy-start(s32[1,1,2,6]{3,2,1,0:T(2,128)} %param.5) | copy-start | bytes 148
  0.0 19.6 %copy-start = (bf16[1,1,2,6,256,256]{5,4,3,2,1,0:T(8,128)(2,1)S(1)}, bf16[1,1,2,6,256,256]{5,4,3,2,1,0:T(8,128)(2,1)}, u32[]{:S(2)}) copy-start(bf16[1,1,2,6,256,256]{5,4,3,2,1,0:T(8,128)(2,1)} %param.4) | copy-start | bytes 4718596
  2.6 25.9 %collective-permute-start.3 = (bf16[528,256]{1,0:T(8,128)(2,1)}, bf16[528,256]{1,0:T(8,128)(2,1)}, u32[]{:S(2)}, u32[]{:S(2)}) collective-permute-start(bf16[528,256]{1,0:T(8,128)(2,1)} %fusion.2.right_zero.refs_0_), channel_id=1, source_target_pairs={{48,0},{96,48},{144,96},{192,144},{240,192},{288,240},{336,288},{3... | collective-permute-start | bytes 811016 | tf_op jit(solution)/shard_map/ppermute | solution.py:26
  17.7 20.1 %collective-permute-start.2 = (bf16[528,256]{1,0:T(8,128)(2,1)S(1)}, bf16[528,256]{1,0:T(8,128)(2,1)}, u32[]{:S(2)}, u32[]{:S(2)}) collective-permute-start(bf16[528,256]{1,0:T(8,128)(2,1)S(1)} %fusion.3.right_one.refs_0_), channel_id=1, source_target_pairs={{48,0},{96,48},{144,96},{192,144},{240,192},{288,240},{336,288},{3... | collective-permute-start | bytes 811016 | tf_op jit(solution)/shard_map/ppermute | solution.py:26
  21.7 26.6 %collective-permute-start.1 = (bf16[3104,256]{1,0:T(8,128)(2,1)S(1)}, bf16[3104,256]{1,0:T(8,128)(2,1)S(1)}, u32[]{:S(2)}, u32[]{:S(2)}) collective-permute-start(bf16[3104,256]{1,0:T(8,128)(2,1)S(1)} %get-tuple-element.29.lefts), channel_id=1, source_target_pairs={{6,0},{12,6},{18,12},{24,18},{30,24},{36,30},{42,36},{0,42},{7,1},... | collective-permute-start | bytes 4767752 | tf_op jit(solution)/shard_map/ppermute | solution.py:26
  21.7 18.5 %collective-permute-start = (bf16[1056,256]{1,0:T(8,128)(2,1)}, bf16[1056,256]{1,0:T(8,128)(2,1)}, u32[]{:S(2)}, u32[]{:S(2)}) collective-permute-start(bf16[1056,256]{1,0:T(8,128)(2,1)} %get-tuple-element.28), channel_id=1, source_target_pairs={{96,0},{144,48},{192,96},{240,144},{288,192},{336,240},{384,288},{... | collective-permute-start | bytes 1622024 | tf_op jit(solution)/shard_map/ppermute | solution.py:26
  24.1 39.7 %collective-permute-start.6 = (bf16[1552,256]{1,0:T(8,128)(2,1)}, bf16[1552,256]{1,0:T(8,128)(2,1)}, u32[]{:S(2)}, u32[]{:S(2)}) collective-permute-start(bf16[1552,256]{1,0:T(8,128)(2,1)} %get-tuple-element.37), channel_id=1, source_target_pairs={{12,0},{18,6},{24,12},{30,18},{36,24},{42,30},{0,36},{6,42},{13,1}... | collective-permute-start | bytes 2383880 | tf_op jit(solution)/shard_map/ppermute | solution.py:26
  28.5 19.9 %collective-permute-start.4 = (bf16[528,256]{1,0:T(8,128)(2,1)}, bf16[528,256]{1,0:T(8,128)(2,1)S(1)}, u32[]{:S(2)}, u32[]{:S(2)}) collective-permute-start(bf16[528,256]{1,0:T(8,128)(2,1)} %collective-permute-done.3.refs_1_), channel_id=1, source_target_pairs={{96,0},{144,48},{192,96},{240,144},{288,192},{336,240},{384,288},{... | collective-permute-start | bytes 811016 | tf_op jit(solution)/shard_map/ppermute | solution.py:26
  37.8 26.0 %collective-permute-start.5 = (bf16[528,256]{1,0:T(8,128)(2,1)}, bf16[528,256]{1,0:T(8,128)(2,1)S(1)}, u32[]{:S(2)}, u32[]{:S(2)}) collective-permute-start(bf16[528,256]{1,0:T(8,128)(2,1)} %collective-permute-done.2.right_one.refs_1_), channel_id=1, source_target_pairs={{96,0},{144,48},{192,96},{240,144},{288,192},{336,240},{384,288},{... | collective-permute-start | bytes 811016 | tf_op jit(solution)/shard_map/ppermute | solution.py:26
  50.9 21.3 %collective-permute-start.10 = (bf16[256,256]{1,0:T(8,128)(2,1)S(1)}, bf16[256,256]{1,0:T(8,128)(2,1)S(1)}, u32[]{:S(2)}, u32[]{:S(2)}) collective-permute-start(bf16[256,256]{1,0:T(8,128)(2,1)S(1)} %get-tuple-element.42), channel_id=1, source_target_pairs={{0,2},{1,0},{2,1},{3,5},{4,3},{5,4},{6,8},{7,6},{8,7},{9,11},{10,9... | collective-permute-start | bytes 393224 | tf_op jit(solution)/shard_map/ppermute | solution.py:200
  54.2 18.0 %collective-permute-start.9 = (bf16[256,256]{1,0:T(8,128)(2,1)S(1)}, bf16[256,256]{1,0:T(8,128)(2,1)S(1)}, u32[]{:S(2)}, u32[]{:S(2)}) collective-permute-start(bf16[256,256]{1,0:T(8,128)(2,1)S(1)} %get-tuple-element.41), channel_id=1, source_target_pairs={{0,1},{1,2},{2,0},{3,4},{4,5},{5,3},{6,7},{7,8},{8,6},{9,10},{10,1... | collective-permute-start | bytes 393224 | tf_op jit(solution)/shard_map/ppermute | solution.py:200
  65.4 17.6 %collective-permute-start.7 = (bf16[256,256]{1,0:T(8,128)(2,1)S(1)}, bf16[256,256]{1,0:T(8,128)(2,1)S(1)}, u32[]{:S(2)}, u32[]{:S(2)}) collective-permute-start(bf16[256,256]{1,0:T(8,128)(2,1)S(1)} %get-tuple-element.38), channel_id=1, source_target_pairs={{0,1},{1,2},{2,0},{3,4},{4,5},{5,3},{6,7},{7,8},{8,6},{9,10},{10,1... | collective-permute-start | bytes 393224 | tf_op jit(solution)/shard_map/ppermute | solution.py:200
  69.8 13.2 %collective-permute-start.8 = (bf16[256,256]{1,0:T(8,128)(2,1)S(1)}, bf16[256,256]{1,0:T(8,128)(2,1)S(1)}, u32[]{:S(2)}, u32[]{:S(2)}) collective-permute-start(bf16[256,256]{1,0:T(8,128)(2,1)S(1)} %get-tuple-element.39), channel_id=1, source_target_pairs={{0,2},{1,0},{2,1},{3,5},{4,3},{5,4},{6,8},{7,6},{8,7},{9,11},{10,9... | collective-permute-start | bytes 393224 | tf_op jit(solution)/shard_map/ppermute | solution.py:200
  72.2 16.9 %collective-permute-start.11 = (bf16[128,256]{1,0:T(8,128)(2,1)S(1)}, bf16[128,256]{1,0:T(8,128)(2,1)S(1)}, u32[]{:S(2)}, u32[]{:S(2)}) collective-permute-start(bf16[128,256]{1,0:T(8,128)(2,1)S(1)} %get-tuple-element.45), channel_id=1, source_target_pairs={{0,3},{1,4},{2,5},{3,0},{4,1},{5,2},{6,9},{7,10},{8,11},{9,6},{10,... | collective-permute-start | bytes 196616 | tf_op jit(solution)/shard_map/ppermute | solution.py:211
  83.0 8.3 %collective-permute-start.12 = (bf16[128,256]{1,0:T(8,128)(2,1)S(1)}, bf16[128,256]{1,0:T(8,128)(2,1)S(1)}, u32[]{:S(2)}, u32[]{:S(2)}) collective-permute-start(bf16[128,256]{1,0:T(8,128)(2,1)S(1)} %get-tuple-element.50), channel_id=1, source_target_pairs={{0,3},{1,4},{2,5},{3,0},{4,1},{5,2},{6,9},{7,10},{8,11},{9,6},{10,... | collective-permute-start | bytes 196616 | tf_op jit(solution)/shard_map/ppermute | solution.py:211

commit v10 on v9

--- a/solution.py
+++ b/solution.py
@@ -98,8 +98,8 @@
     total, place_ref, pieces, last, sem = refs[count + TRIO :]
     targets = [pieces.at[step] for step in range(STEPS)] + [last] * column
     copies = [pltpu.make_async_copy(source, target, sem.at[n]) for n, (source, target) in enumerate(zip(arriving, targets))]
-    for copy in copies:
-        copy.start()
+    for n in (0, 1, 3, 2, *range(STEPS, count)):
+        copies[n].start()
     blocks = [part(lefts, 0, BLOCK), part(lefts, 1, BLOCK), part(left_next, 0, BLOCK), part(left_next, 1, BLOCK), last]
     total[...] = jnp.zeros_like(total)
     for step in range(STEPS):

time: 93.5 us -> 93 us (level)
  the two profiles are of different devices: /device:TPU:26 before, /device:TPU:56 now
where the time goes in v10:
time: 93 us; the launch traced here: 91.6 us
  starting transfers between devices  59.7 us (64%)
  waiting for transfers between devices  21.4 us (23%)
  Pallas kernels  7.62 us (8%)
  other arithmetic  1.42 us (2%)
  local copies, waits for them, and re-layouts  1.2 us (1%)
    ppermute x7, starting transfers between devices, shifted(): lax.ppermute(block, axis, [((i - distance) % size, i) for i in range(size)])  32.3 us
    ppermute x7, waiting for transfers between devices, shifted(): lax.ppermute(block, axis, [((i - distance) % size, i) for i in range(size)])  18.9 us
    ppermute x2, starting transfers between devices, body(): shares[j] = lax.ppermute(far, 'layer', across)  14.5 us
    ppermute x4, starting transfers between devices, body(): lax.ppermute(share, 'layer', trio[turn])  13 us
    pallas_call x8, Pallas kernels, call(): pl.pallas_call(kernel, out_shape=out_shape, in_specs=in_specs, out_specs=...  7.62 us
    ppermute x2, waiting for transfers between devices, body(): shares[j] = lax.ppermute(far, 'layer', across)  2.55 us
  transfers between devices with their start and end apart: 13, of which 2 were waited for; matrix products, arithmetic and copies ran while one was open for 0% of the time, Pallas kernels for 8%

profile of v10, /device:TPU:56, one launch (start us, length us, event | category | flops | bytes accessed | tf_op | source)
XLA Modules:
  0.0 91.6 jit_solution(605866256968560703)
XLA Ops:
  0.0 0.0 copy-start.1
  0.0 0.0 copy-start
  0.0 1.2 %fusion.4 = (bf16[1,1,1,2,256,256]{5,4,3,2,1,0:T(8,128)(2,1)S(1)}, bf16[1,1,1,2,256,256]{5,4,3,2,1,0:T(8,128)(2,1)S(1)}) fusion(bf16[1,1,2,2,256,256]{5,4,3,2,1,0:T(8,128)(2,1)} %param.6), kind=kLoop, calls=%fused_computation.7 | loop fusion | bytes 1048576 | tf_op jit(solution)/shard_map/slice | solution.py:162
  1.2 0.7 convert.4
  1.9 0.7 fusion.2.right_zero.refs_0_
  2.6 15.9 %collective-permute-start.3 = (bf16[528,256]{1,0:T(8,128)(2,1)}, bf16[528,256]{1,0:T(8,128)(2,1)}, u32[]{:S(2)}, u32[]{:S(2)}) collective-permute-start(bf16[528,256]{1,0:T(8,128)(2,1)} %fusion.2.right_zero.refs_0_), channel_id=1, source_target_pairs={{48,0},{96,48},{144,96},{192,144},{240,192},{288,240},{336,288},{3... | collective-permute-start | bytes 811016 | tf_op jit(solution)/shard_map/ppermute | solution.py:26
  18.6 1.9 %collective-permute-start.2 = (bf16[528,256]{1,0:T(8,128)(2,1)S(1)}, bf16[528,256]{1,0:T(8,128)(2,1)}, u32[]{:S(2)}, u32[]{:S(2)}) collective-permute-start(bf16[528,256]{1,0:T(8,128)(2,1)S(1)} %fusion.3.right_one.refs_0_), channel_id=1, source_target_pairs={{48,0},{96,48},{144,96},{192,144},{240,192},{288,240},{336,288},{3... | collective-permute-start | bytes 811016 | tf_op jit(solution)/shard_map/ppermute | solution.py:26
  20.5 0.0 copy-done.1
  20.5 0.0 copy-done
  20.5 2.1 %shard_map.46 = (bf16[3104,256]{1,0:T(8,128)(2,1)S(1)}, bf16[1552,256]{1,0:T(8,128)(2,1)}, bf16[1056,256]{1,0:T(8,128)(2,1)}) custom-call(s32[2,6]{1,0:T(2,128)S(1)} %bitcast.10, bf16[2,6,256,256]{3,2,1,0:T(8,128)(2,1)S(1)} %bitcast.9, bf16[528,256]{1,0:T(8,128)(2,1)} %fusion.2.right_zero.refs_0_, bf16[528,256]{1,0:T(8,128)(2,1)S(1)} %fusion.3.right_one.refs_0_), custom_call_target="tpu_custom_call" | custom-call | tf_op jit(solution)/shard_map/pallas_call | solution.py:144
  22.6 1.9 %collective-permute-start.1 = (bf16[3104,256]{1,0:T(8,128)(2,1)S(1)}, bf16[3104,256]{1,0:T(8,128)(2,1)S(1)}, u32[]{:S(2)}, u32[]{:S(2)}) collective-permute-start(bf16[3104,256]{1,0:T(8,128)(2,1)S(1)} %get-tuple-element.29.lefts), channel_id=1, source_target_pairs={{6,0},{12,6},{18,12},{24,18},{30,24},{36,30},{42,36},{0,42},{7,1},... | collective-permute-start | bytes 4767752 | tf_op jit(solution)/shard_map/ppermute | solution.py:26
  24.6 3.2 %collective-permute-start = (bf16[1056,256]{1,0:T(8,128)(2,1)}, bf16[1056,256]{1,0:T(8,128)(2,1)}, u32[]{:S(2)}, u32[]{:S(2)}) collective-permute-start(bf16[1056,256]{1,0:T(8,128)(2,1)} %get-tuple-element.28), channel_id=1, source_target_pairs={{96,0},{144,48},{192,96},{240,144},{288,192},{336,240},{384,288},{... | collective-permute-start | bytes 1622024 | tf_op jit(solution)/shard_map/ppermute | solution.py:26
  27.8 2.8 %collective-permute-start.6 = (bf16[1552,256]{1,0:T(8,128)(2,1)}, bf16[1552,256]{1,0:T(8,128)(2,1)}, u32[]{:S(2)}, u32[]{:S(2)}) collective-permute-start(bf16[1552,256]{1,0:T(8,128)(2,1)} %get-tuple-element.37), channel_id=1, source_target_pairs={{12,0},{18,6},{24,12},{30,18},{36,24},{42,30},{0,36},{6,42},{13,1}... | collective-permute-start | bytes 2383880 | tf_op jit(solution)/shard_map/ppermute | solution.py:26
  30.6 0.0 collective-permute-done.3.refs_1_
  30.6 3.3 %collective-permute-start.4 = (bf16[528,256]{1,0:T(8,128)(2,1)}, bf16[528,256]{1,0:T(8,128)(2,1)S(1)}, u32[]{:S(2)}, u32[]{:S(2)}) collective-permute-start(bf16[528,256]{1,0:T(8,128)(2,1)} %collective-permute-done.3.refs_1_), channel_id=1, source_target_pairs={{96,0},{144,48},{192,96},{240,144},{288,192},{336,240},{384,288},{... | collective-permute-start | bytes 811016 | tf_op jit(solution)/shard_map/ppermute | solution.py:26
  33.9 18.9 %collective-permute-done.2.right_one.refs_1_ = bf16[528,256]{1,0:T(8,128)(2,1)} collective-permute-done((bf16[528,256]{1,0:T(8,128)(2,1)S(1)}, bf16[528,256]{1,0:T(8,128)(2,1)}, u32[]{:S(2)}, u32[]{:S(2)}) %collective-permute-start.2) | collective-permute-done | bytes 270368 | tf_op jit(solution)/shard_map/ppermute | solution.py:26
  52.7 3.2 %collective-permute-start.5 = (bf16[528,256]{1,0:T(8,128)(2,1)}, bf16[528,256]{1,0:T(8,128)(2,1)S(1)}, u32[]{:S(2)}, u32[]{:S(2)}) collective-permute-start(bf16[528,256]{1,0:T(8,128)(2,1)} %collective-permute-done.2.right_one.refs_1_), channel_id=1, source_target_pairs={{96,0},{144,48},{192,96},{240,144},{288,192},{336,240},{384,288},{... | collective-permute-start | bytes 811016 | tf_op jit(solution)/shard_map/ppermute | solution.py:26
  56.0 0.0 collective-permute-done.refs_2_
  56.0 0.0 collective-permute-done.1.left_next
  56.0 0.0 collective-permute-done.4.refs_3_
  56.0 2.3 %shard_map.48 = (bf16[256,256]{1,0:T(8,128)(2,1)S(1)}, bf16[256,256]{1,0:T(8,128)(2,1)S(1)}, bf16[256,256]{1,0:T(8,128)(2,1)S(1)}) custom-call(s32[1]{0:T(128)} %bitcast.layer, f32[8,128]{1,0:T(8,128)S(1)} %shard_map.47.mark, bf16[3104,256]{1,0:T(8,128)(2,1)S(1)} %get-tuple-element.29.lefts, bf16[3104,256]{1,0:T(8,128)(2,1)S(1)} %collective-permute-done.1.left_next, ...), custom_call_target="tpu_custom_call" | custom-call | tf_op jit(solution)/shard_map/pallas_call | solution.py:144
  58.3 1.9 %collective-permute-start.10 = (bf16[256,256]{1,0:T(8,128)(2,1)S(1)}, bf16[256,256]{1,0:T(8,128)(2,1)S(1)}, u32[]{:S(2)}, u32[]{:S(2)}) collective-permute-start(bf16[256,256]{1,0:T(8,128)(2,1)S(1)} %get-tuple-element.42), channel_id=1, source_target_pairs={{0,2},{1,0},{2,1},{3,5},{4,3},{5,4},{6,8},{7,6},{8,7},{9,11},{10,9... | collective-permute-start | bytes 393224 | tf_op jit(solution)/shard_map/ppermute | solution.py:200
  60.3 4.3 %collective-permute-start.9 = (bf16[256,256]{1,0:T(8,128)(2,1)S(1)}, bf16[256,256]{1,0:T(8,128)(2,1)S(1)}, u32[]{:S(2)}, u32[]{:S(2)}) collective-permute-start(bf16[256,256]{1,0:T(8,128)(2,1)S(1)} %get-tuple-element.41), channel_id=1, source_target_pairs={{0,1},{1,2},{2,0},{3,4},{4,5},{5,3},{6,7},{7,8},{8,6},{9,10},{10,1... | collective-permute-start | bytes 393224 | tf_op jit(solution)/shard_map/ppermute | solution.py:200
  64.6 0.0 collective-permute-done.5.refs_3_
  64.6 0.0 collective-permute-done.6.refs_4_
  64.6 2.4 %shard_map.49 = (bf16[256,256]{1,0:T(8,128)(2,1)S(1)}, bf16[256,256]{1,0:T(8,128)(2,1)S(1)}, bf16[256,256]{1,0:T(8,128)(2,1)S(1)}) custom-call(s32[1]{0:T(128)} %bitcast.layer, f32[8,128]{1,0:T(8,128)S(1)} %shard_map.47.mark, bf16[3104,256]{1,0:T(8,128)(2,1)S(1)} %get-tuple-element.29.lefts, bf16[3104,256]{1,0:T(8,128)(2,1)S(1)} %collective-permute-done.1.left_next, ...), custom_call_target="tpu_custom_call" | custom-call | tf_op jit(solution)/shard_map/pallas_call | solution.py:144
  67.0 3.5 %collective-permute-start.7 = (bf16[256,256]{1,0:T(8,128)(2,1)S(1)}, bf16[256,256]{1,0:T(8,128)(2,1)S(1)}, u32[]{:S(2)}, u32[]{:S(2)}) collective-permute-start(bf16[256,256]{1,0:T(8,128)(2,1)S(1)} %get-tuple-element.38), channel_id=1, source_target_pairs={{0,1},{1,2},{2,0},{3,4},{4,5},{5,3},{6,7},{7,8},{8,6},{9,10},{10,1... | collective-permute-start | bytes 393224 | tf_op jit(solution)/shard_map/ppermute | solution.py:200
  70.5 3.2 %collective-permute-start.8 = (bf16[256,256]{1,0:T(8,128)(2,1)S(1)}, bf16[256,256]{1,0:T(8,128)(2,1)S(1)}, u32[]{:S(2)}, u32[]{:S(2)}) collective-permute-start(bf16[256,256]{1,0:T(8,128)(2,1)S(1)} %get-tuple-element.39), channel_id=1, source_target_pairs={{0,2},{1,0},{2,1},{3,5},{4,3},{5,4},{6,8},{7,6},{8,7},{9,11},{10,9... | collective-permute-start | bytes 393224 | tf_op jit(solution)/shard_map/ppermute | solution.py:200
  73.7 0.0 collective-permute-done.10.two
  73.7 0.0 collective-permute-done.9.one
  73.7 0.1 shard_map.50
  73.8 9.1 %collective-permute-start.11 = (bf16[128,256]{1,0:T(8,128)(2,1)S(1)}, bf16[128,256]{1,0:T(8,128)(2,1)S(1)}, u32[]{:S(2)}, u32[]{:S(2)}) collective-permute-start(bf16[128,256]{1,0:T(8,128)(2,1)S(1)} %get-tuple-element.45), channel_id=1, source_target_pairs={{0,3},{1,4},{2,5},{3,0},{4,1},{5,2},{6,9},{7,10},{8,11},{9,6},{10,... | collective-permute-start | bytes 196616 | tf_op jit(solution)/shard_map/ppermute | solution.py:211
  82.9 0.0 collective-permute-done.7.one
  82.9 0.0 collective-permute-done.8.two
  83.0 0.1 shard_map.52
  83.0 5.4 %collective-permute-start.12 = (bf16[128,256]{1,0:T(8,128)(2,1)S(1)}, bf16[128,256]{1,0:T(8,128)(2,1)S(1)}, u32[]{:S(2)}, u32[]{:S(2)}) collective-permute-start(bf16[128,256]{1,0:T(8,128)(2,1)S(1)} %get-tuple-element.50), channel_id=1, source_target_pairs={{0,3},{1,4},{2,5},{3,0},{4,1},{5,2},{6,9},{7,10},{8,11},{9,6},{10,... | collective-permute-start | bytes 196616 | tf_op jit(solution)/shard_map/ppermute | solution.py:211
  88.4 0.0 collective-permute-done.11.far
  88.4 2.6 %collective-permute-done.12.far = bf16[128,256]{1,0:T(8,128)(2,1)S(1)} collective-permute-done((bf16[128,256]{1,0:T(8,128)(2,1)S(1)}, bf16[128,256]{1,0:T(8,128)(2,1)S(1)}, u32[]{:S(2)}, u32[]{:S(2)}) %collective-permute-start.12) | collective-permute-done | bytes 65568 | tf_op jit(solution)/shard_map/ppermute | solution.py:211
  91.0 0.7 shard_map.53
  (4 shorter events, 0.0 us)
Async XLA Ops:
  0.0 20.5 %copy-start.1 = (s32[1,1,2,6]{3,2,1,0:T(2,128)S(1)}, s32[1,1,2,6]{3,2,1,0:T(2,128)}, u32[]{:S(2)}) copy-start(s32[1,1,2,6]{3,2,1,0:T(2,128)} %param.5) | copy-start | bytes 148
  0.0 20.5 %copy-start = (bf16[1,1,2,6,256,256]{5,4,3,2,1,0:T(8,128)(2,1)S(1)}, bf16[1,1,2,6,256,256]{5,4,3,2,1,0:T(8,128)(2,1)}, u32[]{:S(2)}) copy-start(bf16[1,1,2,6,256,256]{5,4,3,2,1,0:T(8,128)(2,1)} %param.4) | copy-start | bytes 4718596
  2.6 28.0 %collective-permute-start.3 = (bf16[528,256]{1,0:T(8,128)(2,1)}, bf16[528,256]{1,0:T(8,128)(2,1)}, u32[]{:S(2)}, u32[]{:S(2)}) collective-permute-start(bf16[528,256]{1,0:T(8,128)(2,1)} %fusion.2.right_zero.refs_0_), channel_id=1, source_target_pairs={{48,0},{96,48},{144,96},{192,144},{240,192},{288,240},{336,288},{3... | collective-permute-start | bytes 811016 | tf_op jit(solution)/shard_map/ppermute | solution.py:26
  18.6 34.2 %collective-permute-start.2 = (bf16[528,256]{1,0:T(8,128)(2,1)S(1)}, bf16[528,256]{1,0:T(8,128)(2,1)}, u32[]{:S(2)}, u32[]{:S(2)}) collective-permute-start(bf16[528,256]{1,0:T(8,128)(2,1)S(1)} %fusion.3.right_one.refs_0_), channel_id=1, source_target_pairs={{48,0},{96,48},{144,96},{192,144},{240,192},{288,240},{336,288},{3... | collective-permute-start | bytes 811016 | tf_op jit(solution)/shard_map/ppermute | solution.py:26
  22.6 33.4 %collective-permute-start.1 = (bf16[3104,256]{1,0:T(8,128)(2,1)S(1)}, bf16[3104,256]{1,0:T(8,128)(2,1)S(1)}, u32[]{:S(2)}, u32[]{:S(2)}) collective-permute-start(bf16[3104,256]{1,0:T(8,128)(2,1)S(1)} %get-tuple-element.29.lefts), channel_id=1, source_target_pairs={{6,0},{12,6},{18,12},{24,18},{30,24},{36,30},{42,36},{0,42},{7,1},... | collective-permute-start | bytes 4767752 | tf_op jit(solution)/shard_map/ppermute | solution.py:26
  24.6 31.4 %collective-permute-start = (bf16[1056,256]{1,0:T(8,128)(2,1)}, bf16[1056,256]{1,0:T(8,128)(2,1)}, u32[]{:S(2)}, u32[]{:S(2)}) collective-permute-start(bf16[1056,256]{1,0:T(8,128)(2,1)} %get-tuple-element.28), channel_id=1, source_target_pairs={{96,0},{144,48},{192,96},{240,144},{288,192},{336,240},{384,288},{... | collective-permute-start | bytes 1622024 | tf_op jit(solution)/shard_map/ppermute | solution.py:26
  27.8 36.8 %collective-permute-start.6 = (bf16[1552,256]{1,0:T(8,128)(2,1)}, bf16[1552,256]{1,0:T(8,128)(2,1)}, u32[]{:S(2)}, u32[]{:S(2)}) collective-permute-start(bf16[1552,256]{1,0:T(8,128)(2,1)} %get-tuple-element.37), channel_id=1, source_target_pairs={{12,0},{18,6},{24,12},{30,18},{36,24},{42,30},{0,36},{6,42},{13,1}... | collective-permute-start | bytes 2383880 | tf_op jit(solution)/shard_map/ppermute | solution.py:26
  30.6 25.4 %collective-permute-start.4 = (bf16[528,256]{1,0:T(8,128)(2,1)}, bf16[528,256]{1,0:T(8,128)(2,1)S(1)}, u32[]{:S(2)}, u32[]{:S(2)}) collective-permute-start(bf16[528,256]{1,0:T(8,128)(2,1)} %collective-permute-done.3.refs_1_), channel_id=1, source_target_pairs={{96,0},{144,48},{192,96},{240,144},{288,192},{336,240},{384,288},{... | collective-permute-start | bytes 811016 | tf_op jit(solution)/shard_map/ppermute | solution.py:26
  52.7 11.9 %collective-permute-start.5 = (bf16[528,256]{1,0:T(8,128)(2,1)}, bf16[528,256]{1,0:T(8,128)(2,1)S(1)}, u32[]{:S(2)}, u32[]{:S(2)}) collective-permute-start(bf16[528,256]{1,0:T(8,128)(2,1)} %collective-permute-done.2.right_one.refs_1_), channel_id=1, source_target_pairs={{96,0},{144,48},{192,96},{240,144},{288,192},{336,240},{384,288},{... | collective-permute-start | bytes 811016 | tf_op jit(solution)/shard_map/ppermute | solution.py:26
  58.3 15.4 %collective-permute-start.10 = (bf16[256,256]{1,0:T(8,128)(2,1)S(1)}, bf16[256,256]{1,0:T(8,128)(2,1)S(1)}, u32[]{:S(2)}, u32[]{:S(2)}) collective-permute-start(bf16[256,256]{1,0:T(8,128)(2,1)S(1)} %get-tuple-element.42), channel_id=1, source_target_pairs={{0,2},{1,0},{2,1},{3,5},{4,3},{5,4},{6,8},{7,6},{8,7},{9,11},{10,9... | collective-permute-start | bytes 393224 | tf_op jit(solution)/shard_map/ppermute | solution.py:200
  60.3 13.5 %collective-permute-start.9 = (bf16[256,256]{1,0:T(8,128)(2,1)S(1)}, bf16[256,256]{1,0:T(8,128)(2,1)S(1)}, u32[]{:S(2)}, u32[]{:S(2)}) collective-permute-start(bf16[256,256]{1,0:T(8,128)(2,1)S(1)} %get-tuple-element.41), channel_id=1, source_target_pairs={{0,1},{1,2},{2,0},{3,4},{4,5},{5,3},{6,7},{7,8},{8,6},{9,10},{10,1... | collective-permute-start | bytes 393224 | tf_op jit(solution)/shard_map/ppermute | solution.py:200
  67.0 16.0 %collective-permute-start.7 = (bf16[256,256]{1,0:T(8,128)(2,1)S(1)}, bf16[256,256]{1,0:T(8,128)(2,1)S(1)}, u32[]{:S(2)}, u32[]{:S(2)}) collective-permute-start(bf16[256,256]{1,0:T(8,128)(2,1)S(1)} %get-tuple-element.38), channel_id=1, source_target_pairs={{0,1},{1,2},{2,0},{3,4},{4,5},{5,3},{6,7},{7,8},{8,6},{9,10},{10,1... | collective-permute-start | bytes 393224 | tf_op jit(solution)/shard_map/ppermute | solution.py:200
  70.5 12.4 %collective-permute-start.8 = (bf16[256,256]{1,0:T(8,128)(2,1)S(1)}, bf16[256,256]{1,0:T(8,128)(2,1)S(1)}, u32[]{:S(2)}, u32[]{:S(2)}) collective-permute-start(bf16[256,256]{1,0:T(8,128)(2,1)S(1)} %get-tuple-element.39), channel_id=1, source_target_pairs={{0,2},{1,0},{2,1},{3,5},{4,3},{5,4},{6,8},{7,6},{8,7},{9,11},{10,9... | collective-permute-start | bytes 393224 | tf_op jit(solution)/shard_map/ppermute | solution.py:200
  73.8 14.6 %collective-permute-start.11 = (bf16[128,256]{1,0:T(8,128)(2,1)S(1)}, bf16[128,256]{1,0:T(8,128)(2,1)S(1)}, u32[]{:S(2)}, u32[]{:S(2)}) collective-permute-start(bf16[128,256]{1,0:T(8,128)(2,1)S(1)} %get-tuple-element.45), channel_id=1, source_target_pairs={{0,3},{1,4},{2,5},{3,0},{4,1},{5,2},{6,9},{7,10},{8,11},{9,6},{10,... | collective-permute-start | bytes 196616 | tf_op jit(solution)/shard_map/ppermute | solution.py:211
  83.0 8.0 %collective-permute-start.12 = (bf16[128,256]{1,0:T(8,128)(2,1)S(1)}, bf16[128,256]{1,0:T(8,128)(2,1)S(1)}, u32[]{:S(2)}, u32[]{:S(2)}) collective-permute-start(bf16[128,256]{1,0:T(8,128)(2,1)S(1)} %get-tuple-element.50), channel_id=1, source_target_pairs={{0,3},{1,4},{2,5},{3,0},{4,1},{5,2},{6,9},{7,10},{8,11},{9,6},{10,... | collective-permute-start | bytes 196616 | tf_op jit(solution)/shard_map/ppermute | solution.py:211
